TPU v7x, 256 devices: a whole 4x4x8 slice. The times are simulated.
256 devices in a mesh: dom: 32 (over x, y, core), col: 8 (over z).
Axes of the slice: x: 4, y: 4, z: 8, core: 2. Of those that a mesh axis runs over, the one named last changes fastest.
Arguments:
- node_states: bfloat16 [32768, 512], P(('dom', 'col')), may hold values from -6 to 6
- norm_gain: float32 [512], replicated, may hold values from 0.5 to 1.5
- qkv_weight: bfloat16 [1536, 512], P('col'), may hold values from -0.375 to 0.375
- out_weight: bfloat16 [512, 512], P('col'), may hold values from -0.25 to 0.25
- local_slots: int32 [256, 8], P('dom'), may hold values from 0 to 7
- local_live: int32 [256, 8], P('dom'), may hold values 0 or 1
- far_owner: int32 [256, 4], replicated, may hold values from 0 to 31, all different within a row; in each aligned block of 8 rows (0 to 7, 8 to 15, ...) at most 2 rows name the same one
- far_slot: int32 [256, 4], replicated, may hold values from 0 to 7
- out_grad: bfloat16 [32768, 512], P(('dom', 'col')), may hold values from -6 to 6
Outputs:
- layer_out: bfloat16 [32768, 512], P(('dom', 'col'))
- state_grad: bfloat16 [32768, 512], P(('dom', 'col'))
- qkv_grad: float32 [1536, 512], P('col')
- out_weight_grad: float32 [512, 512], P('col')
Inputs may be any that keep to these rules, and one draw needn't show every extreme that they name: `far_owner`: each row names 4 different partitions; among the rows of one partition's 8 node blocks no partition is named by more than 2 rows, and in every draw some partition is named by exactly 2 of them.
All inputs are finite; a program needn't handle non-finite values. No bound on the sum of `local_live` on one device may be relied on, other than what follows from the above.
Results may differ from a plain program's by a relative error of at most 0.02.
Values may be sent and summed in bfloat16 or wider, within the bound.
No kernel may reach another device: no remote copies, remote signals or barrier semaphores. Data moves between devices by JAX's collectives and lax.ppermute only.
A program may use at most 64 MiB of HBM per device.

v0:
```python
import math

import jax
import jax.numpy as jnp
from jax import lax
from jax.sharding import PartitionSpec as P

D = 512
HD = 64
BLK = 128
NB_DEV = 8
LOC = 8
DEG = 4


query_group = 4
norm_eps = 1e-06


def slot_tables(far_owner, far_slot, dom_count, slot_cap, own_index):
    entries = far_owner.shape[1] * NB_DEV
    owners = far_owner.reshape(dom_count, entries)
    slot_table = far_slot.reshape(dom_count, entries)
    positions = jnp.arange(entries, dtype=jnp.int32)
    before = positions[None, :] < positions[:, None]
    rank_table = jnp.sum((owners[:, :, None] == owners[:, None, :]) & before[None], axis=2)
    to_owner = owners == own_index
    pick_rank = (
        (rank_table[:, :, None] == jnp.arange(slot_cap, dtype=jnp.int32)[None, None, :])
        & to_owner[:, :, None]
    ).astype(jnp.bfloat16)
    pick_block = (
        slot_table[:, :, None] == jnp.arange(NB_DEV, dtype=jnp.int32)[None, None, :]
    ).astype(jnp.bfloat16)
    select = jnp.einsum(
        "rec,reb->rcb", pick_rank, pick_block, preferred_element_type=jnp.float32
    ).astype(jnp.bfloat16)
    own_owner = lax.dynamic_index_in_dim(owners, own_index, 0, keepdims=False)
    own_rank = lax.dynamic_index_in_dim(rank_table, own_index, 0, keepdims=False)
    places = own_owner * slot_cap + own_rank
    return (select, places)


def shards(
    node_states,
    norm_gain,
    qkv_weight,
    out_weight,
    local_slots,
    local_live,
    far_owner,
    far_slot,
    out_grad,
):
    dom_count = lax.axis_size("dom")
    own_index = lax.axis_index("dom")
    col_index = lax.axis_index("col")
    rows_own = node_states.shape[0]
    node_total = far_owner.shape[0] * BLK
    slot_cap = max(2, 6 * NB_DEV // dom_count)
    heads_here = out_weight.shape[0] // HD
    score_scale = 1.0 / math.sqrt(HD)
    state_whole, grad_whole = (
        lax.all_gather(node_states, "col", axis=0, tiled=True),
        lax.all_gather(out_grad, "col", axis=0, tiled=True),
    )
    row_count = state_whole.shape[0]
    state_float = state_whole.astype(jnp.float32)
    inv_rms = lax.rsqrt(jnp.mean(state_float * state_float, axis=1, keepdims=True) + norm_eps)
    hidden = (state_float * inv_rms * norm_gain).astype(jnp.bfloat16)
    projected = lax.dot_general(
        hidden, qkv_weight, (((1,), (1,)), ((), ())), preferred_element_type=jnp.float32
    ).astype(jnp.bfloat16)
    projected = projected.reshape(NB_DEV, BLK, heads_here, 3, HD)
    queries = projected[:, :, :, 0]
    key_value = projected[:, :, :, 1:]
    pair_flat = key_value.reshape(NB_DEV, -1)
    select, places = slot_tables(far_owner, far_slot, dom_count, slot_cap, own_index)
    fetched = lax.all_to_all(
        jnp.einsum("rcb,bf->rcf", select, pair_flat, preferred_element_type=jnp.float32).astype(
            jnp.bfloat16
        ),
        "dom",
        split_axis=0,
        concat_axis=0,
        tiled=True,
    ).reshape(dom_count * slot_cap, -1)
    self_slot = jnp.arange(NB_DEV, dtype=jnp.int32)[:, None]
    near_table = jnp.concatenate([self_slot, local_slots], axis=1)
    entry_live = jnp.concatenate(
        [
            jnp.ones((NB_DEV, 1), jnp.float32),
            local_live.astype(jnp.float32),
            jnp.ones((NB_DEV, DEG), jnp.float32),
        ],
        axis=1,
    )
    place_table = places.reshape(NB_DEV, DEG)
    near_hits = (
        near_table[:, :, None] == jnp.arange(NB_DEV, dtype=jnp.int32)[None, None, :]
    ).astype(jnp.float32)
    starts = jnp.arange(NB_DEV // query_group, dtype=jnp.int32) * query_group

    def gather_keys(source, offset):
        near_index = lax.dynamic_slice_in_dim(near_table, offset, query_group, 0)
        far_index = lax.dynamic_slice_in_dim(place_table, offset, query_group, 0)
        near_keys = key_value[near_index]
        far_keys = source[far_index].reshape(query_group, DEG, BLK, heads_here, 2, HD)
        return jnp.concatenate([near_keys, far_keys], axis=1)

    def probabilities_of(query_grp, keys_grp, offset):
        live_grp = lax.dynamic_slice_in_dim(entry_live, offset, query_group, 0)
        scores = (
            jnp.einsum(
                "gqhc,gmkhc->ghqmk",
                query_grp,
                keys_grp[:, :, :, :, 0],
                preferred_element_type=jnp.float32,
            )
            * score_scale
        )
        return jnp.exp(scores) * live_grp[:, None, None, :, None]

    def forward_step(carried, offset):
        keys_grp = gather_keys(fetched, offset)
        query_grp = lax.dynamic_slice_in_dim(queries, offset, query_group, 0)
        probabilities = probabilities_of(query_grp, keys_grp, offset)
        numerator = jnp.einsum(
            "ghqmk,gmkhc->gqhc",
            probabilities.astype(jnp.bfloat16),
            keys_grp[:, :, :, :, 1],
            preferred_element_type=jnp.float32,
        )
        denominator = jnp.transpose(jnp.sum(probabilities, axis=(3, 4)), (0, 2, 1))
        return (carried, (numerator, denominator))

    _, (numerator, denominator) = lax.scan(forward_step, jnp.int32(0), starts)
    numerator = numerator.reshape(NB_DEV, BLK, heads_here, HD)
    denominator = denominator.reshape(NB_DEV, BLK, heads_here)
    attn_float = numerator / denominator[..., None]
    attn_rounded = attn_float.astype(jnp.bfloat16).reshape(row_count, heads_here * HD)
    state_own = node_states.astype(jnp.float32)
    out_terms = jnp.dot(attn_rounded, out_weight, preferred_element_type=jnp.float32)
    mixed_own = lax.psum_scatter(
        out_terms.astype(jnp.bfloat16), "col", scatter_dimension=0, tiled=True
    ).astype(jnp.float32)
    layer_out = (state_own + mixed_own).astype(jnp.bfloat16)
    attn_grad = lax.dot_general(
        grad_whole, out_weight, (((1,), (1,)), ((), ())), preferred_element_type=jnp.float32
    )
    attn_grad = attn_grad.reshape(NB_DEV, BLK, heads_here, HD)
    scaled = (attn_grad / denominator[..., None]).astype(jnp.bfloat16)
    correction = jnp.sum(attn_grad * attn_float, axis=3) / denominator

    def backward_step(accumulated, offset):
        keys_grp = gather_keys(fetched, offset)
        query_grp = lax.dynamic_slice_in_dim(queries, offset, query_group, 0)
        scaled_grp = lax.dynamic_slice_in_dim(scaled, offset, query_group, 0)
        correction_grp = lax.dynamic_slice_in_dim(correction, offset, query_group, 0)
        probabilities = probabilities_of(query_grp, keys_grp, offset)
        prob_grad = (
            jnp.einsum(
                "gqhc,gmkhc->ghqmk",
                scaled_grp,
                keys_grp[:, :, :, :, 1],
                preferred_element_type=jnp.float32,
            )
            - jnp.transpose(correction_grp, (0, 2, 1))[:, :, :, None, None]
        )
        score_grad = (probabilities * prob_grad).astype(jnp.bfloat16)
        query_grad = (
            jnp.einsum(
                "ghqmk,gmkhc->gqhc",
                score_grad,
                keys_grp[:, :, :, :, 0],
                preferred_element_type=jnp.float32,
            )
            * score_scale
        )
        key_grad = (
            jnp.einsum(
                "ghqmk,gqhc->gmkhc", score_grad, query_grp, preferred_element_type=jnp.float32
            )
            * score_scale
        )
        value_grad = jnp.einsum(
            "ghqmk,gqhc->gmkhc",
            probabilities.astype(jnp.bfloat16),
            scaled_grp,
            preferred_element_type=jnp.float32,
        )
        pair_grad = jnp.stack([key_grad, value_grad], axis=4)
        near_grads = pair_grad[:, : 1 + LOC].reshape(query_group, 1 + LOC, -1)
        hits_grp = lax.dynamic_slice_in_dim(near_hits, offset, query_group, 0)
        accumulated = accumulated + jnp.einsum(
            "gmb,gmf->bf", hits_grp, near_grads, precision=lax.Precision.HIGHEST
        )
        far_grads = pair_grad[:, 1 + LOC :].reshape(query_group * DEG, -1).astype(jnp.bfloat16)
        return (accumulated, (query_grad, far_grads))

    start_acc = jnp.zeros(pair_flat.shape, jnp.float32)
    accumulated, (query_grad, far_grads) = lax.scan(backward_step, start_acc, starts)
    far_grads = far_grads.reshape(NB_DEV * DEG, -1)
    buffer = (
        jnp.zeros((dom_count * slot_cap, far_grads.shape[1]), jnp.bfloat16)
        .at[places]
        .set(far_grads)
    )
    returned = lax.all_to_all(
        buffer.reshape(dom_count, slot_cap, -1), "dom", split_axis=0, concat_axis=0, tiled=True
    )
    accumulated = accumulated + jnp.einsum(
        "rcb,rcf->bf", select, returned, preferred_element_type=jnp.float32
    )
    query_grad = query_grad.reshape(NB_DEV, BLK, heads_here, 1, HD)
    pair_acc = accumulated.reshape(NB_DEV, BLK, heads_here, 2, HD)
    proj_grad = (
        jnp.concatenate([query_grad, pair_acc], axis=3)
        .astype(jnp.bfloat16)
        .reshape(row_count, heads_here * 3 * HD)
    )
    inv_own = lax.dynamic_slice_in_dim(inv_rms, col_index * rows_own, rows_own, 0)
    back_terms = jnp.dot(proj_grad, qkv_weight, preferred_element_type=jnp.float32)
    back_own = lax.psum_scatter(
        back_terms.astype(jnp.bfloat16), "col", scatter_dimension=0, tiled=True
    ).astype(jnp.float32)
    norm_stat = jnp.sum(norm_gain * back_own * state_own, axis=1, keepdims=True)
    state_grad = (
        out_grad.astype(jnp.float32)
        + inv_own * norm_gain * back_own
        - state_own * inv_own * inv_own * inv_own * norm_stat / D
    ).astype(jnp.bfloat16)
    qkv_terms = lax.dot_general(
        proj_grad, hidden, (((0,), (0,)), ((), ())), preferred_element_type=jnp.float32
    )
    out_terms_grad = lax.dot_general(
        attn_rounded, grad_whole, (((0,), (0,)), ((), ())), preferred_element_type=jnp.float32
    )
    qkv_total, out_total = (
        lax.psum(qkv_terms.astype(jnp.bfloat16), "dom").astype(jnp.float32),
        lax.psum(out_terms_grad.astype(jnp.bfloat16), "dom").astype(jnp.float32),
    )
    inv_root = 1.0 / math.sqrt(node_total)
    return (layer_out, state_grad, qkv_total * inv_root, out_total * inv_root)


def solution(mesh):
    placed = (
        P(("dom", "col"), None),
        P(),
        P("col", None),
        P("col", None),
        P("dom", None),
        P("dom", None),
        P(),
        P(),
        P(("dom", "col"), None),
    )
    return jax.shard_map(
        shards,
        mesh=mesh,
        in_specs=placed,
        out_specs=(
            P(("dom", "col"), None),
            P(("dom", "col"), None),
            P("col", None),
            P("col", None),
        ),
        check_vma=False,
    )
```

profile of v0, /device:TPU:2, one launch (start us, length us, event | category | flops | bytes accessed | tf_op | source)
XLA Modules:
  0.0 506.9 jit_solution(2446908319697251182)
XLA Ops:
  10.9 40.6 %all-gather.3.cloned.1.call-done = bf16[1024,512]{1,0:T(8,128)(2,1)} async-done(((bf16[128,512]{1,0:T(8,128)(2,1)}), bf16[1024,512]{1,0:T(8,128)(2,1)}) %all-gather.3.cloned.1.call-update) | async-done | bytes 1048592 | tf_op jit(solution)/shard_map/all_gather | solution.py:64
  56.5 3.5 copy.118
  60.0 7.6 %all-to-all-start = ((bf16[32,2,16384]{2,1,0:T(2,128)(2,1)}), bf16[32,2,16384]{2,1,0:T(2,128)(2,1)}, u32[]{:S(2)}, u32[]{:S(2)}) async-start(bf16[32,2,16384]{2,1,0:T(2,128)(2,1)} %copy.118), calls=%async_computation | async-start | bytes 4194304 | tf_op jit(solution)/shard_map/all_to_all | solution.py:79
  70.0 23.7 %all-to-all-done = bf16[32,2,16384]{2,1,0:T(2,128)(2,1)} async-done(((bf16[32,2,16384]{2,1,0:T(2,128)(2,1)}), bf16[32,2,16384]{2,1,0:T(2,128)(2,1)}, u32[]{:S(2)}, u32[]{:S(2)}) %all-to-all-start) | async-done | bytes 2097184 | tf_op jit(solution)/shard_map/all_to_all | solution.py:79
  93.6 2.7 reshape.285
  96.4 52.1 %while.27 = (s32[]{:T(128)}, f32[2,4,128,1,64]{2,1,0,4,3:T(4,128)}, f32[2,4,128,1]{2,3,1,0:T(1,128)S(1)}, s32[2]{0:T(128)S(1)}, s32[8,9]{1,0:T(8,128)S(1)}, /*in...) while((s32[]{:T(128)}, f32[2,4,128,1,64]{2,1,0,4,3:T(4,128)}, ...), condition=%wide.region_4.5_spmd, body=%wide.region_2.4_spmd.sunk | while | flops 225347232 | bytes 25380976 | solution.py:137
  101.9 2.4 copy.168
  104.4 8.1 %gather_fusion.1 = bf16[36,128,2,64]{3,2,1,0:T(2,128)(2,1)} fusion(bf16[8,128,2,64]{3,2,1,0:T(2,128)(2,1)S(1)} %bitcast.206, s32[1024]{0:T(1024)S(1)} %pad_clamp_fusion.9), kind=kCustom, calls=%fused_computation.clone.1 | custom fusion | bytes 2359440 | tf_op jit(solution)/shard_map/while/body/eval_jaxpr/gather | solution.py:107
  112.5 6.0 %copy.169 = bf16[36,128,2,64]{1,3,0,2:T(8,128)(2,1)} copy(bf16[36,128,2,64]{3,2,1,0:T(2,128)(2,1)} %gather_fusion.1) | data formatting | bytes 2359296 | tf_op jit(solution)/shard_map/while/body/eval_jaxpr/gather | solution.py:107
  128.0 2.4 copy.168
  130.4 8.1 %gather_fusion.1 = bf16[36,128,2,64]{3,2,1,0:T(2,128)(2,1)} fusion(bf16[8,128,2,64]{3,2,1,0:T(2,128)(2,1)S(1)} %bitcast.206, s32[1024]{0:T(1024)S(1)} %pad_clamp_fusion.9), kind=kCustom, calls=%fused_computation.clone.1 | custom fusion | bytes 2359440 | tf_op jit(solution)/shard_map/while/body/eval_jaxpr/gather | solution.py:107
  138.5 6.0 %copy.169 = bf16[36,128,2,64]{1,3,0,2:T(8,128)(2,1)} copy(bf16[36,128,2,64]{3,2,1,0:T(2,128)(2,1)} %gather_fusion.1) | data formatting | bytes 2359296 | tf_op jit(solution)/shard_map/while/body/eval_jaxpr/gather | solution.py:107
  152.1 111.0 %while.28 = (s32[]{:T(128)}, f32[8,16384]{1,0:T(8,128)}, bf16[2,4,128,1,64]{2,4,1,3,0:T(8,128)(2,1)}, bf16[2,16,16384]{2,1,0:T(8,128)(2,1)}, s32[2]{0:T(128)S(1)...) while((s32[]{:T(128)}, f32[8,16384]{1,0:T(8,128)}, ...), condition=%wide.region_8.9_spmd.clone, body=%wide.region_7.8_spmd.clone.sunk | while | flops 614107264 | bytes 67276784 | solution.py:202
  157.9 2.4 copy.171
  160.3 8.1 %gather_fusion.2 = bf16[36,128,2,64]{3,2,1,0:T(2,128)(2,1)} fusion(bf16[8,128,2,64]{3,2,1,0:T(2,128)(2,1)S(1)} %bitcast.207, s32[1024]{0:T(1024)S(1)} %pad_clamp_fusion.10), kind=kCustom, calls=%fused_computation.2.clone.clone.1 | custom fusion | bytes 2359440 | tf_op jit(solution)/shard_map/while/body/eval_jaxpr/gather | solution.py:107
  168.4 6.0 %copy.170 = bf16[36,128,2,64]{1,3,0,2:T(8,128)(2,1)} copy(bf16[36,128,2,64]{3,2,1,0:T(2,128)(2,1)} %gather_fusion.2) | data formatting | bytes 2359296 | tf_op jit(solution)/shard_map/while/body/eval_jaxpr/gather | solution.py:107
  186.4 7.1 %copy.172 = f32[4,9,128,1,2,64]{5,4,2,1,0,3:T(2,128)} copy(f32[4,9,128,1,2,64]{2,5,1,0,4,3:T(8,128)} %fusion.152) | data formatting | bytes 4718592 | tf_op jit(solution)/shard_map/while/body/eval_jaxpr/reshape | solution.py:193
  193.5 7.3 %reshape.412 = f32[4,9,16384]{2,1,0:T(8,128)} reshape(f32[4,9,128,1,2,64]{5,4,2,1,0,3:T(2,128)} %copy.172) | data formatting | bytes 4718592 | tf_op jit(solution)/shard_map/while/body/eval_jaxpr/reshape | solution.py:193
  200.7 6.1 %fusion.153 = f32[8,16384]{1,0:T(8,128)S(1)} fusion(f32[4,9,16384]{2,1,0:T(8,128)} %reshape.412, f32[8,16384]{1,0:T(8,128)S(1)} %copy-done.3, pred[]{:T(512)S(6)} %compare.3, f32[8,9,8]{1,2,0:T(8,128)S(1)} %get-tuple-element.467, s32[]{:T(128)S(6)} %select_n.69), kind=kOutput, calls=%fused_computation.34.clone.1 | convolution fusion | flops 56885248 | bytes 3424261 | tf_op jit(solution)/shard_map/while/body/eval_jaxpr/gmb,gmf->bf/dot_general | solution.py:195
  213.4 2.4 copy.171
  215.8 8.1 %gather_fusion.2 = bf16[36,128,2,64]{3,2,1,0:T(2,128)(2,1)} fusion(bf16[8,128,2,64]{3,2,1,0:T(2,128)(2,1)S(1)} %bitcast.207, s32[1024]{0:T(1024)S(1)} %pad_clamp_fusion.10), kind=kCustom, calls=%fused_computation.2.clone.clone.1 | custom fusion | bytes 2359440 | tf_op jit(solution)/shard_map/while/body/eval_jaxpr/gather | solution.py:107
  223.9 6.0 %copy.170 = bf16[36,128,2,64]{1,3,0,2:T(8,128)(2,1)} copy(bf16[36,128,2,64]{3,2,1,0:T(2,128)(2,1)} %gather_fusion.2) | data formatting | bytes 2359296 | tf_op jit(solution)/shard_map/while/body/eval_jaxpr/gather | solution.py:107
  241.9 7.1 %copy.172 = f32[4,9,128,1,2,64]{5,4,2,1,0,3:T(2,128)} copy(f32[4,9,128,1,2,64]{2,5,1,0,4,3:T(8,128)} %fusion.152) | data formatting | bytes 4718592 | tf_op jit(solution)/shard_map/while/body/eval_jaxpr/reshape | solution.py:193
  249.0 7.3 %reshape.412 = f32[4,9,16384]{2,1,0:T(8,128)} reshape(f32[4,9,128,1,2,64]{5,4,2,1,0,3:T(2,128)} %copy.172) | data formatting | bytes 4718592 | tf_op jit(solution)/shard_map/while/body/eval_jaxpr/reshape | solution.py:193
  256.2 6.1 %fusion.153 = f32[8,16384]{1,0:T(8,128)S(1)} fusion(f32[4,9,16384]{2,1,0:T(8,128)} %reshape.412, f32[8,16384]{1,0:T(8,128)S(1)} %copy-done.3, pred[]{:T(512)S(6)} %compare.3, f32[8,9,8]{1,2,0:T(8,128)S(1)} %get-tuple-element.467, s32[]{:T(128)S(6)} %select_n.69), kind=kOutput, calls=%fused_computation.34.clone.1 | convolution fusion | flops 56885248 | bytes 3424261 | tf_op jit(solution)/shard_map/while/body/eval_jaxpr/gmb,gmf->bf/dot_general | solution.py:195
  263.1 3.6 scatter_custom_fusion
  266.7 2.7 reshape.290
  269.4 6.9 %all-to-all-start.1 = ((bf16[32,2,16384]{2,1,0:T(2,128)(2,1)}), bf16[32,2,16384]{2,1,0:T(2,128)(2,1)S(1)}, u32[]{:S(2)}, u32[]{:S(2)}) async-start(bf16[32,2,16384]{2,1,0:T(2,128)(2,1)} %reshape.290), calls=%async_computation.2 | async-start | bytes 4194304 | tf_op jit(solution)/shard_map/all_to_all | solution.py:209
  279.9 22.4 %all-to-all-done.1 = bf16[32,2,16384]{2,1,0:T(2,128)(2,1)S(1)} async-done(((bf16[32,2,16384]{2,1,0:T(2,128)(2,1)}), bf16[32,2,16384]{2,1,0:T(2,128)(2,1)S(1)}, u32[]{:S(2)}, u32[]{:S(2)}) %all-to-all-start.1) | async-done | bytes 2097184 | tf_op jit(solution)/shard_map/all_to_all | solution.py:209
  312.1 105.2 %all-reduce.3.cloned.1.call-done = (bf16[192,512]{1,0:T(8,128)(2,1)}, bf16[64,512]{1,0:T(8,128)(2,1)}) async-done(((bf16[192,512]{1,0:T(8,128)(2,1)}, bf16[64,512]{1,0:T(8,128)(2,1)}), (bf16[192,512]{1,0:T(8,128)(2,1)}, bf16[64,512]{1,0:T(8,128)(2,1)})) %all-reduce.3.cloned.1.call-update) | async-done | bytes 262160 | tf_op jit(solution)/shard_map/psum | solution.py:240
  420.6 38.1 %reduce-scatter.5.cloned.1.call-done = bf16[128,512]{1,0:T(8,128)(2,1)} async-done(((bf16[1024,512]{1,0:T(8,128)(2,1)}), bf16[128,512]{1,0:T(8,128)(2,1)}) %reduce-scatter.5.cloned.1.call-update) | async-done | bytes 131088 | tf_op jit(solution)/shard_map/reduce_scatter | solution.py:224
  459.7 38.9 %reduce-scatter.3.cloned.1.call-done = bf16[128,512]{1,0:T(8,128)(2,1)} async-done(((bf16[1024,512]{1,0:T(8,128)(2,1)}), bf16[128,512]{1,0:T(8,128)(2,1)}) %reduce-scatter.3.cloned.1.call-update) | async-done | bytes 131088 | tf_op jit(solution)/shard_map/reduce_scatter | solution.py:144
  (195 shorter events, 82.4 us)
Async XLA Ops:
  7.2 45.9 %copy-start = (bf16[192,512]{1,0:T(8,128)(2,1)S(1)}, bf16[192,512]{1,0:T(8,128)(2,1)}, u32[]{:S(2)}) copy-start(bf16[192,512]{1,0:T(8,128)(2,1)} %param.15) | copy-start | bytes 589828
  7.2 44.3 %all-gather.3.cloned.1.call-start = ((), (), s32[]{:S(2)}) async-start(), calls=%async_computation.4 | async-start | bytes 1179648 | tf_op jit(solution)/shard_map/all_gather | solution.py:64
  10.9 44.9 %copy-start.15 = (bf16[32,2,8]{0,2,1:T(8,128)(2,1)}, bf16[32,2,8]{0,2,1:T(8,128)(2,1)S(1)}, u32[]{:S(2)}) copy-start(bf16[32,2,8]{0,2,1:T(8,128)(2,1)S(1)} %copy.117) | copy-start | bytes 3076
  53.0 1.9 copy-start.20
  60.0 8.5 %copy-start.19 = (s32[8,8]{1,0:T(8,128)S(1)}, s32[8,8]{1,0:T(8,128)}, u32[]{:S(2)}) copy-start(s32[8,8]{1,0:T(8,128)} %param.18) | copy-start | bytes 772
  60.0 9.7 %copy-start.18 = (s32[8,8]{1,0:T(8,128)S(1)}, s32[8,8]{1,0:T(8,128)}, u32[]{:S(2)}) copy-start(s32[8,8]{1,0:T(8,128)} %param.17) | copy-start | bytes 772
  60.0 33.6 %all-to-all-start = ((bf16[32,2,16384]{2,1,0:T(2,128)(2,1)}), bf16[32,2,16384]{2,1,0:T(2,128)(2,1)}, u32[]{:S(2)}, u32[]{:S(2)}) async-start(bf16[32,2,16384]{2,1,0:T(2,128)(2,1)} %copy.118), calls=%async_computation | async-start | bytes 4194304 | tf_op jit(solution)/shard_map/all_to_all | solution.py:79
  67.6 81.9 %all-gather.5.cloned.1.call-start = ((), (), s32[]{:S(2)}) async-start(), calls=%async_computation.6 | async-start | bytes 1179648 | tf_op jit(solution)/shard_map/all_gather | solution.py:65
  118.5 2.2 copy-start.2
  120.7 1.0 copy-start.12
  144.5 2.2 copy-start.2
  146.7 1.0 copy-start.12
  149.5 1.8 copy-start.9
  174.4 1.8 copy-start.1
  174.4 1.8 copy-start.6
  193.5 7.3 %copy-start.3 = (f32[8,16384]{1,0:T(8,128)S(1)}, f32[8,16384]{1,0:T(8,128)}, u32[]{:S(2)}) copy-start(f32[8,16384]{1,0:T(8,128)} %get-tuple-element.446) | copy-start | bytes 1572868 | tf_op jit(solution)/shard_map/while
  229.9 1.8 copy-start.1
  229.9 1.8 copy-start.6
  249.0 7.3 %copy-start.3 = (f32[8,16384]{1,0:T(8,128)S(1)}, f32[8,16384]{1,0:T(8,128)}, u32[]{:S(2)}) copy-start(f32[8,16384]{1,0:T(8,128)} %get-tuple-element.446) | copy-start | bytes 1572868 | tf_op jit(solution)/shard_map/while
  269.4 32.9 %all-to-all-start.1 = ((bf16[32,2,16384]{2,1,0:T(2,128)(2,1)}), bf16[32,2,16384]{2,1,0:T(2,128)(2,1)S(1)}, u32[]{:S(2)}, u32[]{:S(2)}) async-start(bf16[32,2,16384]{2,1,0:T(2,128)(2,1)} %reshape.290), calls=%async_computation.2 | async-start | bytes 4194304 | tf_op jit(solution)/shard_map/all_to_all | solution.py:209
  276.3 25.9 %copy-start.5 = (f32[8,16384]{1,0:T(8,128)S(1)}, f32[8,16384]{1,0:T(8,128)}, u32[]{:S(2)}) copy-start(f32[8,16384]{1,0:T(8,128)} %get-tuple-element.134) | copy-start | bytes 1572868
  276.3 25.9 %copy-start.16 = (bf16[32,2,8]{0,2,1:T(8,128)(2,1)S(1)}, bf16[32,2,8]{0,2,1:T(8,128)(2,1)}, u32[]{:S(2)}) copy-start(bf16[32,2,8]{0,2,1:T(8,128)(2,1)} %copy-done.15) | copy-start | bytes 3076
  276.3 141.0 %all-reduce.3.cloned.1.call-start = ((), (), s32[]{:S(2)}) async-start(), calls=%async_computation.8 | async-start | bytes 524288 | tf_op jit(solution)/shard_map/psum | solution.py:240
  304.2 3.5 copy-start.8
  304.2 3.5 copy-start.17
  304.2 3.5 copy-start.21
  308.9 1.6 copy-start.10
  308.9 1.6 copy-start.14
  308.9 149.7 %reduce-scatter.5.cloned.1.call-start = ((), (), s32[]{:S(2)}) async-start(), calls=%async_computation.7 | async-start | bytes 1179648 | tf_op jit(solution)/shard_map/reduce_scatter | solution.py:224
  310.5 148.2 %copy-start.7 = (bf16[128,512]{1,0:T(8,128)(2,1)S(1)}, bf16[128,512]{1,0:T(8,128)(2,1)}, u32[]{:S(2)}) copy-start(bf16[128,512]{1,0:T(8,128)(2,1)} %param.13) | copy-start | bytes 393220
  310.5 188.1 %copy-start.11 = (bf16[128,512]{1,0:T(8,128)(2,1)S(1)}, bf16[128,512]{1,0:T(8,128)(2,1)}, u32[]{:S(2)}) copy-start(bf16[128,512]{1,0:T(8,128)(2,1)} %param.21) | copy-start | bytes 393220
  310.5 188.1 %reduce-scatter.3.cloned.1.call-start = ((), (), s32[]{:S(2)}) async-start(), calls=%async_computation.5 | async-start | bytes 1179648 | tf_op jit(solution)/shard_map/reduce_scatter | solution.py:144
  (4 other events, 3.0 us)
Sparse Core Ops, SparseCore 0:
  9.8 41.6 all-gather.2
  70.3 37.0 all-gather.4
  309.1 108.2 all-reduce.2
  419.9 38.6 reduce-scatter.4
  461.2 37.3 reduce-scatter.2
where the time goes:
time: 509 us; the launch traced here: 507 us
  waiting for transfers between devices  270 us (53%)
  local copies, waits for them, and re-layouts  144 us (28%)
  matrix products  41.7 us (8%)
  starting transfers between devices  14.9 us (3%)
  other arithmetic  14.7 us (3%)
  between operations  14.2 us (3%)
  loops' own time  7.75 us (2%)
    psum x1, waiting for transfers between devices, shards(): lax.psum(qkv_terms.astype(jnp.bfloat16), 'dom').astype(jnp.float32)  105 us
    gather x8, local copies, waits for them, and re-layouts, gather_keys(): near_keys = key_value[near_index]  56.4 us
    all_gather x1, waiting for transfers between devices, shards(): lax.all_gather(node_states, 'col', axis=0, tiled=True)  40.6 us
    reduce_scatter x1, waiting for transfers between devices, shards(): lax.psum_scatter(out_terms.astype(jnp.bfloat16), 'col', scatter_dimension...  38.9 us
    reduce_scatter x1, waiting for transfers between devices, shards(): lax.psum_scatter(back_terms.astype(jnp.bfloat16), 'col', scatter_dimensio...  38.1 us
    reshape x4, local copies, waits for them, and re-layouts, backward_step(): near_grads = pair_grad[:, :1 + LOC].reshape(query_group, 1 + LOC, -1)  28.6 us
    all_to_all x1, waiting for transfers between devices, shards(): lax.all_to_all(jnp.einsum('rcb,bf->rcf', select, pair_flat, preferred_ele...  23.7 us
    all_to_all x1, waiting for transfers between devices, shards(): lax.all_to_all(buffer.reshape(dom_count, slot_cap, -1), 'dom', split_axis...  22.4 us
  transfers between devices with their start and end apart: 7, of which 6 were waited for; matrix products, arithmetic and copies ran while one was open for 13% of the time, Pallas kernels for 0%

commit v1 on v0

v1 whole, which is shorter than its diff:
```python
import math

import jax
import jax.numpy as jnp
from jax import lax
from jax.experimental import pallas as pl
from jax.experimental.pallas import tpu as pltpu
from jax.sharding import PartitionSpec as P

D = 512
HD = 64
BLK = 128
NB = 8
DEG = 4
CAP = 2
ROWS = NB * BLK
EPS = 1e-06
SCALE = 1.0 / math.sqrt(HD)

F32 = jnp.float32
BF16 = jnp.bfloat16
VMEM_LIMIT = 40 * 1024 * 1024

NT = (((1,), (1,)), ((), ()))
TN = (((0,), (0,)), ((), ()))


def dot(a, b):
    return jnp.dot(a, b, preferred_element_type=F32)


def dot_nt(a, b):
    return lax.dot_general(a, b, NT, preferred_element_type=F32)


def whole(shape=None):
    return pl.BlockSpec(memory_space=pltpu.VMEM)


def scalars():
    return pl.BlockSpec(memory_space=pltpu.SMEM)


def call(body, outs, ins, scratch=(), flops=0, name=None):
    return pl.pallas_call(
        body,
        out_shape=outs,
        in_specs=ins,
        out_specs=jax.tree.map(lambda _: whole(), outs),
        scratch_shapes=list(scratch),
        compiler_params=pltpu.CompilerParams(vmem_limit_bytes=VMEM_LIMIT),
        cost_estimate=pl.CostEstimate(flops=flops, bytes_accessed=4 << 20, transcendentals=0),
        name=name,
    )


def lanes_low(shape):
    return lax.broadcasted_iota(jnp.int32, shape, len(shape) - 1) < HD


def rows_of(b):
    return pl.ds(pl.multiple_of(b * BLK, BLK), BLK)


def project_body(send_ref, state_ref, gain_ref, weight_ref, hidden_ref, query_ref, kv_ref, out_ref):
    gain = gain_ref[...]
    weight = weight_ref[...]
    wide = jnp.concatenate(
        [weight[:HD], jnp.zeros((HD, D), BF16), weight[HD:]], axis=0
    )

    def step(b, _):
        x = state_ref[b].astype(F32)
        inv = lax.rsqrt(jnp.mean(x * x, axis=1, keepdims=True) + EPS)
        hidden = (x * inv * gain).astype(BF16)
        hidden_ref[rows_of(b), :] = hidden
        proj = dot_nt(hidden, wide).astype(BF16)
        query_ref[rows_of(b), :] = proj[:, :BLK] * jnp.asarray(SCALE, BF16)
        kv_ref[b] = proj[:, BLK:]
        return 0

    lax.fori_loop(0, NB, step, 0, unroll=True)

    def fill(s, _):
        out_ref[s] = kv_ref[send_ref[s]]
        return 0

    lax.fori_loop(0, out_ref.shape[0], fill, 0, unroll=8)


def near_forward_body(query_ref, kv_ref, count_ref, num_ref, ones_ref):
    kv = kv_ref[...].reshape(ROWS, BLK)
    ones_ref[...] = jnp.where(lanes_low(kv.shape), jnp.asarray(1, BF16), kv)

    def step(b, _):
        score = dot_nt(query_ref[rows_of(b), :], kv_ref[...].reshape(ROWS, BLK))
        prob = jnp.exp(score) * count_ref[pl.ds(b, 1), :]
        num_ref[rows_of(b), :] = dot(prob.astype(BF16), ones_ref[...])
        return 0

    lax.fori_loop(0, NB, step, 0, unroll=2)


def far_body(
    place_ref,
    query_ref,
    far_ref,
    num_ref,
    grad_ref,
    weight_ref,
    attn_ref,
    scaled_ref,
    extra_ref,
    back_ref,
    kv_ref,
    ag_ref,
):
    wide = jnp.concatenate([jnp.zeros((HD, D), BF16), weight_ref[...]], axis=0)
    ag_ref[...] = dot_nt(grad_ref[...].reshape(ROWS, D), wide)

    def step(b, _):
        rows = rows_of(b)
        for j in range(DEG):
            kv_ref[pl.ds(j * BLK, BLK), :] = far_ref[place_ref[b * DEG + j]]
        kv = kv_ref[...]
        query = query_ref[rows, :]
        prob = jnp.exp(dot_nt(query, kv))
        prob_low = prob.astype(BF16)
        values = jnp.where(lanes_low(kv.shape), jnp.asarray(1, BF16), kv)
        num = num_ref[rows, :] + dot(prob_low, values)
        low = lanes_low(num.shape)
        den = jnp.where(low, num, pltpu.roll(num, HD, 1))
        attn = num / den
        grad = ag_ref[rows, :]
        scaled = (grad / den).astype(BF16)
        scaled_ref[rows, :] = scaled
        corr = jnp.sum(grad * attn, axis=1, keepdims=True) / den
        attn_ref[:, rows] = attn.T[HD:].astype(BF16)
        diff = dot_nt(scaled, kv) - corr[:, :1]
        score_grad = (prob * diff).astype(BF16)
        extra_ref[rows, :] = jnp.where(low, dot(score_grad, kv), corr)
        both = (query + scaled).astype(F32).T.astype(BF16)
        key_grad = dot(both[:HD], score_grad).astype(BF16)
        value_grad = dot(both[HD:], prob_low).astype(BF16)
        for j in range(DEG):
            place = place_ref[b * DEG + j]
            back_ref[place, :HD, :] = key_grad[:, j * BLK : (j + 1) * BLK]
            back_ref[place, HD:, :] = value_grad[:, j * BLK : (j + 1) * BLK]
        return 0

    lax.fori_loop(0, NB, step, 0)


def near_backward_body(
    query_ref, kv_ref, count_ref, scaled_ref, extra_ref, query_grad_ref, acc_ref
):
    acc_ref[...] = jnp.zeros_like(acc_ref)

    def step(b, _):
        rows = rows_of(b)
        query, scaled, extra = query_ref[rows, :], scaled_ref[rows, :], extra_ref[rows, :]
        kv = kv_ref[...].reshape(ROWS, BLK)
        prob = jnp.exp(dot_nt(query, kv)) * count_ref[pl.ds(b, 1), :]
        diff = dot_nt(scaled, kv) - extra[:, HD : HD + 1]
        score_grad = (prob * diff).astype(BF16)
        query_grad = dot(score_grad, kv) + extra
        query_grad_ref[:, rows] = (query_grad.T[:HD] * SCALE).astype(BF16)
        both = (query + scaled).astype(F32).T.astype(BF16)
        acc_ref[:HD, :] += dot(both[:HD], score_grad)
        acc_ref[HD:, :] += dot(both[HD:], prob.astype(BF16))
        return 0

    lax.fori_loop(0, NB, step, 0)


def gather_grads_body(
    home_ref,
    returned_ref,
    near_ref,
    query_grad_ref,
    attn_ref,
    hidden_ref,
    grad_ref,
    node_ref,
    part_ref,
    acc_ref,
):
    for n in range(NB):
        acc_ref[n] = near_ref[:, n * BLK : (n + 1) * BLK]

    def add(s, _):
        home = home_ref[s]

        @pl.when(home >= 0)
        def _():
            acc_ref[home] += returned_ref[s].astype(F32)

        return 0

    lax.fori_loop(0, returned_ref.shape[0], add, 0)
    for n in range(NB):
        cols = slice(n * BLK, (n + 1) * BLK)
        node_ref[n, :HD, :] = query_grad_ref[:, cols]
        node_ref[n, HD : 3 * HD, :] = acc_ref[n].astype(BF16)
        node_ref[n, 3 * HD :, :] = attn_ref[:, cols]
    proj = jnp.concatenate([node_ref[n, : 3 * HD, :] for n in range(NB)], axis=1)
    part_ref[: 3 * HD, :] = dot(proj, hidden_ref[...]).astype(BF16)
    part_ref[3 * HD :, :] = dot(attn_ref[...], grad_ref[...].reshape(ROWS, D)).astype(BF16)


def sum_body(share_ref, total_ref):
    total = jnp.sum(share_ref[...].astype(F32), axis=0).astype(BF16)
    total_ref[...] = jnp.broadcast_to(total[None], total_ref.shape)


def finish_body(node_ref, weight_ref, out_weight_ref, state_ref, grad_ref, gain_ref, layer_ref, back_ref):
    heads = node_ref.shape[0]
    out = jnp.zeros((BLK, D), F32)
    back = jnp.zeros((BLK, D), F32)
    for h in range(heads):
        terms = node_ref[h].astype(F32).T.astype(BF16)
        back += dot(terms[:, : 3 * HD], weight_ref[h])
        out += dot(terms[:, 3 * HD :], out_weight_ref[h])
    state = state_ref[...].astype(F32)
    gain = gain_ref[...]
    layer_ref[...] = (state + out).astype(BF16)
    inv = lax.rsqrt(jnp.mean(state * state, axis=1, keepdims=True) + EPS)
    stat = jnp.sum(gain * back * state, axis=1, keepdims=True)
    back_ref[...] = (
        grad_ref[...].astype(F32) + inv * gain * back - state * (inv * inv * inv * stat / D)
    ).astype(BF16)


def shards(
    node_states,
    norm_gain,
    qkv_weight,
    out_weight,
    local_slots,
    local_live,
    far_owner,
    far_slot,
    out_grad,
):
    doms = lax.axis_size("dom")
    cols = lax.axis_size("col")
    me = lax.axis_index("dom")
    slots = doms * CAP
    gain = norm_gain[None]

    state_whole = lax.all_to_all(
        jnp.broadcast_to(node_states[None], (cols, BLK, D)), "col", 0, 0, tiled=True
    )
    grad_whole = lax.all_gather(out_grad, "col", axis=0)
    weight_whole = lax.all_gather(qkv_weight, "col", axis=0)
    out_weight_whole = lax.all_gather(out_weight, "col", axis=0)

    entries = NB * DEG
    owners = far_owner.reshape(doms, entries)
    wanted = far_slot.reshape(doms, entries)
    place = jnp.arange(entries, dtype=jnp.int32)
    before = place[None, :] < place[:, None]
    rank = jnp.sum((owners[:, :, None] == owners[:, None, :]) & before[None], axis=2, dtype=jnp.int32)
    mine = (owners == me)[:, None, :] & (
        rank[:, None, :] == jnp.arange(CAP, dtype=jnp.int32)[None, :, None]
    )
    home = jnp.max(jnp.where(mine, wanted[:, None, :], -1), axis=2).reshape(slots)
    send = jnp.maximum(home, 0)
    places = (
        lax.dynamic_index_in_dim(owners, me, 0, keepdims=False) * CAP
        + lax.dynamic_index_in_dim(rank, me, 0, keepdims=False)
    )
    block = jnp.arange(NB, dtype=jnp.int32)
    hits = (local_slots[:, :, None] == block[None, None, :]) & (local_live[:, :, None] != 0)
    count = jnp.sum(hits, axis=1, dtype=jnp.int32) + (block[:, None] == block[None, :])
    count = jnp.repeat(count.astype(F32), BLK, axis=1)

    unit = 2 * ROWS * ROWS * BLK
    hidden, query, kv, outgoing = call(
        project_body,
        (
            jax.ShapeDtypeStruct((ROWS, D), BF16),
            jax.ShapeDtypeStruct((ROWS, BLK), BF16),
            jax.ShapeDtypeStruct((NB, BLK, BLK), BF16),
            jax.ShapeDtypeStruct((slots, BLK, BLK), BF16),
        ),
        [scalars(), whole(), whole(), whole()],
        flops=2 * ROWS * D * 256,
        name="project",
    )(send, state_whole, gain, qkv_weight)

    fetched = lax.all_to_all(outgoing, "dom", 0, 0, tiled=True)

    near = call(
        near_forward_body,
        jax.ShapeDtypeStruct((ROWS, BLK), F32),
        [whole()] * 3,
        scratch=[pltpu.VMEM((ROWS, BLK), BF16)],
        flops=2 * unit,
        name="near_forward",
    )(query, kv, count)

    attn, scaled, extra, outgoing_back = call(
        far_body,
        (
            jax.ShapeDtypeStruct((HD, ROWS), BF16),
            jax.ShapeDtypeStruct((ROWS, BLK), BF16),
            jax.ShapeDtypeStruct((ROWS, BLK), F32),
            jax.ShapeDtypeStruct((slots, BLK, BLK), BF16),
        ),
        [scalars()] + [whole()] * 5,
        scratch=[pltpu.VMEM((DEG * BLK, BLK), BF16), pltpu.VMEM((ROWS, BLK), F32)],
        flops=2 * unit,
        name="far_both",
    )(places, query, fetched, near, grad_whole, out_weight)

    returned = lax.all_to_all(outgoing_back, "dom", 0, 0, tiled=True)

    query_grad, near_grad = call(
        near_backward_body,
        (
            jax.ShapeDtypeStruct((HD, ROWS), BF16),
            jax.ShapeDtypeStruct((BLK, ROWS), F32),
        ),
        [whole()] * 5,
        flops=5 * unit,
        name="near_backward",
    )(query, kv, count, scaled, extra)

    node_terms, part = call(
        gather_grads_body,
        (
            jax.ShapeDtypeStruct((NB, 4 * HD, BLK), BF16),
            jax.ShapeDtypeStruct((4 * HD, D), BF16),
        ),
        [scalars()] + [whole()] * 6,
        scratch=[pltpu.VMEM((NB, BLK, BLK), F32)],
        flops=2 * ROWS * D * 256,
        name="gather_grads",
    )(home, returned, near_grad, query_grad, attn, hidden, grad_whole)

    share_rows = 4 * HD // doms
    shares = lax.all_to_all(part.reshape(doms, share_rows, D), "dom", 0, 0, tiled=True)
    node_whole = lax.all_to_all(node_terms, "col", 0, 0, tiled=True)

    totals = call(
        sum_body,
        jax.ShapeDtypeStruct((doms, share_rows, D), BF16),
        [whole()],
        name="sum_shares",
    )(shares)
    total = lax.all_to_all(totals, "dom", 0, 0, tiled=True).reshape(4 * HD, D)

    layer_out, state_grad = call(
        finish_body,
        (
            jax.ShapeDtypeStruct((BLK, D), BF16),
            jax.ShapeDtypeStruct((BLK, D), BF16),
        ),
        [whole()] * 6,
        flops=2 * BLK * D * 2048,
        name="finish",
    )(node_whole, weight_whole, out_weight_whole, node_states, out_grad, gain)

    inv_root = 1.0 / math.sqrt(far_owner.shape[0] * BLK)
    grads = total.astype(F32) * inv_root
    return (layer_out, state_grad, grads[: 3 * HD], grads[3 * HD :])


def solution(mesh):
    placed = (
        P(("dom", "col"), None),
        P(),
        P("col", None),
        P("col", None),
        P("dom", None),
        P("dom", None),
        P(),
        P(),
        P(("dom", "col"), None),
    )
    return jax.shard_map(
        shards,
        mesh=mesh,
        in_specs=placed,
        out_specs=(
            P(("dom", "col"), None),
            P(("dom", "col"), None),
            P("col", None),
            P("col", None),
        ),
        check_vma=False,
    )
```

time: 509 us -> 226 us (0.44)
  waiting for transfers between devices: 270 us -> 78.7 us
  local copies, waits for them, and re-layouts: 144 us -> 21.3 us
  blocking collectives: 0 us -> 60.9 us
  matrix products: 41.7 us -> 0 us
  Pallas kernels: 0 us -> 19.6 us
  other arithmetic: 14.7 us -> 1.09 us
  starting transfers between devices: 14.9 us -> 28.1 us
  loops' own time: 7.75 us -> 0 us
    psum x1 -> x0, waiting for transfers between devices: 105 us -> none  [shards(): lax.psum(qkv_terms.astype(jnp.bfloat16), 'dom').astype(jnp.float32)]
    reduce_scatter x2 -> x0, waiting for transfers between devices: 76.9 us -> none  [the longest x1 38.9 us: shards(): lax.psum_scatter(out_terms.astype(jnp.bfloat16), 'col', scatter_dimension...]
    gather x12 -> x0, local copies, waits for them, and re-layouts: 59.9 us -> none  [the longest x8 56.4 us: gather_keys(): near_keys = key_value[near_index]]
    reshape x17 -> x3, local copies, waits for them, and re-layouts: 53.7 us -> 0.28 us  [the longest x1 0.11 us: shards(): jnp.max(jnp.where(mine, wanted[:, None, :], -1), axis=2).reshape(slots)]
    dot_general x25 -> x0, matrix products: 41.7 us -> none  [the longest x2 12.1 us: backward_step(): jnp.einsum('gmb,gmf->bf', hits_grp, near_grads, precision=lax.Precision.H...]
    all_gather x0 -> x1, blocking collectives: none -> 34.7 us  [shards(): out_weight_whole = lax.all_gather(out_weight, 'col', axis=0)]
    all_to_all x0 -> x2, blocking collectives: none -> 26.2 us  [the longest x1 13.6 us: shards(): lax.all_to_all(part.reshape(doms, share_rows, D), 'dom', 0, 0, tiled=True)]
    pallas_call x0 -> x7, Pallas kernels: none -> 19.6 us  [the longest x1 7.1 us: shards(): call(far_body, (jax.ShapeDtypeStruct((HD, ROWS), BF16), jax.ShapeDtypeStr...]
  transfers between devices with their start and end apart: 7 -> 6, of which waited for: 6 -> 3; matrix products, arithmetic and copies ran while one was open for 13% -> 1% of each run, Pallas kernels for 0% -> 4%
where the time goes in v1:
time: 226 us; the launch traced here: 224 us
  waiting for transfers between devices  78.7 us (35%)
  blocking collectives  60.9 us (27%)
  starting transfers between devices  28.1 us (12%)
  local copies, waits for them, and re-layouts  21.3 us (9%)
  Pallas kernels  19.6 us (9%)
  between operations  14.3 us (6%)
    all_gather x1, blocking collectives, shards(): out_weight_whole = lax.all_gather(out_weight, 'col', axis=0)  34.7 us
    all_gather x1, waiting for transfers between devices, shards(): grad_whole = lax.all_gather(out_grad, 'col', axis=0)  33.8 us
    all_to_all x1, waiting for transfers between devices, shards(): lax.all_to_all(jnp.broadcast_to(node_states[None], (cols, BLK, D)), 'col'...  27.1 us
    unnamed x60, local copies, waits for them, and re-layouts  17.3 us
    all_to_all x1, waiting for transfers between devices, shards(): returned = lax.all_to_all(outgoing_back, 'dom', 0, 0, tiled=True)  16.5 us
    all_to_all x1, blocking collectives, shards(): lax.all_to_all(part.reshape(doms, share_rows, D), 'dom', 0, 0, tiled=True)  13.6 us
    all_to_all x1, blocking collectives, shards(): total = lax.all_to_all(totals, 'dom', 0, 0, tiled=True).reshape(4 * HD, D)  12.6 us
    all_to_all x1, starting transfers between devices, shards(): lax.all_to_all(jnp.broadcast_to(node_states[None], (cols, BLK, D)), 'col'...  8.47 us
  transfers between devices with their start and end apart: 6, of which 3 were waited for; matrix products, arithmetic and copies ran while one was open for 1% of the time, Pallas kernels for 4%

profile of v1, /device:TPU:2, one launch (start us, length us, event | category | flops | bytes accessed | tf_op | source)
XLA Modules:
  0.0 224.0 jit_solution(12686511082616221443)
XLA Ops:
  7.2 2.0 broadcast_in_dim.23
  9.2 8.5 %all-to-all-start = ((bf16[8,128,512]{2,1,0:T(8,128)(2,1)}), bf16[8,128,512]{2,1,0:T(8,128)(2,1)S(1)}, u32[]{:S(2)}, u32[]{:S(2)}) async-start(bf16[8,128,512]{2,1,0:T(8,128)(2,1)} %broadcast_in_dim.23), calls=%async_computation | async-start | bytes 2097152 | tf_op jit(solution)/shard_map/all_to_all | solution.py:251
  18.2 0.8 convert_reduce_fusion
  19.4 27.1 %all-to-all-done.state_ref = bf16[8,128,512]{2,1,0:T(8,128)(2,1)S(1)} async-done(((bf16[8,128,512]{2,1,0:T(8,128)(2,1)}), bf16[8,128,512]{2,1,0:T(8,128)(2,1)S(1)}, u32[]{:S(2)}, u32[]{:S(2)}) %all-to-all-start) | async-done | bytes 1048608 | tf_op jit(solution)/shard_map/all_to_all | solution.py:251
  46.4 1.6 project.1
  48.0 1.4 copy-done.2
  49.4 1.0 copy-done.5
  50.4 7.8 %all-to-all-start.1 = ((bf16[64,128,128]{2,1,0:T(8,128)(2,1)}), bf16[64,128,128]{2,1,0:T(8,128)(2,1)S(1)}, u32[]{:S(2)}, u32[]{:S(2)}) async-start(bf16[64,128,128]{2,1,0:T(8,128)(2,1)} %copy-done.2), calls=%async_computation.1 | async-start | bytes 4194304 | tf_op jit(solution)/shard_map/all_to_all | solution.py:292
  59.2 2.5 %near_forward.1.num_ref = f32[1024,128]{1,0:T(8,128)S(1)} custom-call(bf16[1024,128]{1,0:T(8,128)(2,1)S(1)} %get-tuple-element.18.query_ref, bf16[8,128,128]{2,1,0:T(8,128)(2,1)S(1)} %get-tuple-element.20.kv_ref, f32[8,1024]{1,0:T(8,128)S(1)} %broadcast_bitcast_fusion.count_ref), custom_call_target="tpu_custom_call" | custom-call | flops 536870912 | bytes 4194304 | tf_op jit(solution)/shard_map/near_forward/pallas_call | solution.py:294
  61.6 33.8 %all-gather.6.cloned.1.call-done = bf16[1024,512]{1,0:T(8,128)(2,1)} async-done(((bf16[128,512]{1,0:T(8,128)(2,1)}), bf16[1024,512]{1,0:T(8,128)(2,1)}) %all-gather.6.cloned.1.call-update) | async-done | bytes 1048592 | tf_op jit(solution)/shard_map/all_gather | solution.py:254
  95.4 1.2 copy-done
  96.7 7.1 %far_both.1 = (bf16[64,1024]{1,0:T(8,128)(2,1)S(1)}, bf16[1024,128]{1,0:T(8,128)(2,1)S(1)}, f32[1024,128]{1,0:T(8,128)S(1)}, bf16[64,128,128]{2,1,0:T(8,128)(2,1)S(1)}) custom-call(s32[32]{0:T(128)S(1)} %add_bitcast_fusion.place_ref, bf16[1024,128]{1,0:T(8,128)(2,1)S(1)} %get-tuple-element.18.query_ref, bf16[64,128,128]{2,1,0:T(8,128)(2,1)S(1)} %all-to-all-done.1.far_ref, ...), custom_call_target="tpu_custom_call" | custom-call | flops 536870912 | bytes 4194304 | tf_op jit(solution)/shard_map/far_both/pallas_call | solution.py:303
  103.8 1.4 copy-done.3
  105.8 0.8 copy-done.19
  107.3 7.4 %all-to-all-start.2 = ((bf16[64,128,128]{2,1,0:T(8,128)(2,1)}), bf16[64,128,128]{2,1,0:T(8,128)(2,1)S(1)}, u32[]{:S(2)}, u32[]{:S(2)}) async-start(bf16[64,128,128]{2,1,0:T(8,128)(2,1)} %copy-done.3), calls=%async_computation.2 | async-start | bytes 4194304 | tf_op jit(solution)/shard_map/all_to_all | solution.py:317
  115.5 1.0 copy-done.20
  116.5 0.9 copy-done.22
  117.5 0.9 copy-done.24
  118.4 4.3 %near_backward.1 = (bf16[64,1024]{1,0:T(8,128)(2,1)S(1)}, f32[128,1024]{1,0:T(8,128)S(1)}) custom-call(bf16[1024,128]{1,0:T(8,128)(2,1)S(1)} %get-tuple-element.18.query_ref, bf16[8,128,128]{2,1,0:T(8,128)(2,1)S(1)} %copy-done.22, f32[8,1024]{1,0:T(8,128)S(1)} %broadcast_bitcast_fusion.count_ref, bf16[1024,128]{1,0:T(8,128)(2,1)S(1)} %copy-done.24, ...), custom_call_target="tpu_custom_call" | custom-call | flops 1342177280 | bytes 4194304 | tf_op jit(solution)/shard_map/near_backward/pallas_call | solution.py:319
  122.8 0.8 copy-done.8
  124.2 16.5 %all-to-all-done.2.returned_ref = bf16[64,128,128]{2,1,0:T(8,128)(2,1)S(1)} async-done(((bf16[64,128,128]{2,1,0:T(8,128)(2,1)}), bf16[64,128,128]{2,1,0:T(8,128)(2,1)S(1)}, u32[]{:S(2)}, u32[]{:S(2)}) %all-to-all-start.2) | async-done | bytes 2097184 | tf_op jit(solution)/shard_map/all_to_all | solution.py:317
  140.7 1.2 copy-done.6
  141.9 1.0 copy-done.9
  143.0 0.9 copy-done.15
  143.9 0.9 copy-done.17
  144.8 2.3 %gather_grads.1 = (bf16[8,256,128]{2,1,0:T(8,128)(2,1)S(1)}, bf16[256,512]{1,0:T(8,128)(2,1)S(1)}) custom-call(s32[64]{0:T(128)S(1)} %reshape.55.home_ref, bf16[64,128,128]{2,1,0:T(8,128)(2,1)S(1)} %all-to-all-done.2.returned_ref, f32[128,1024]{1,0:T(8,128)S(1)} %copy-done.9, bf16[64,1024]{1,0:T(8,128)(2,1)S(1)} %copy-done.17, ...), custom_call_target="tpu_custom_call" | custom-call | flops 268435456 | bytes 4194304 | tf_op jit(solution)/shard_map/gather_grads/pallas_call | solution.py:330
  147.1 13.6 %all_to_all.30.share_ref = bf16[32,8,512]{2,1,0:T(8,128)(2,1)S(1)} all-to-all(bf16[32,8,512]{2,1,0:T(8,128)(2,1)S(1)} %bitcast.17), channel_id=1, replica_groups=mesh['dom'=32,'col'=8] {'dom'}, dimensions={0} | all-to-all | bytes 524288 | tf_op jit(solution)/shard_map/all_to_all | solution.py:343
  160.7 12.6 %all_to_all.31 = bf16[32,8,512]{2,1,0:T(8,128)(2,1)S(1)} all-to-all(bf16[32,8,512]{2,1,0:T(8,128)(2,1)S(1)} %sum_shares.1), channel_id=1, replica_groups=mesh['dom'=32,'col'=8] {'dom'}, dimensions={0} | all-to-all | bytes 524288 | tf_op jit(solution)/shard_map/all_to_all | solution.py:352
  173.3 4.4 %all-to-all-start.3 = ((bf16[8,256,128]{2,1,0:T(8,128)(2,1)}), bf16[8,256,128]{2,1,0:T(8,128)(2,1)S(1)}, u32[]{:S(2)}, u32[]{:S(2)}) async-start(bf16[8,256,128]{2,1,0:T(8,128)(2,1)} %copy-done.12), calls=%async_computation.3 | async-start | bytes 1048576 | tf_op jit(solution)/shard_map/all_to_all | solution.py:344
  177.7 34.7 %all-gather.2 = bf16[512,512]{1,0:T(8,128)(2,1)S(1)} all-gather(bf16[64,512]{1,0:T(8,128)(2,1)S(1)} %copy-done.13), channel_id=4, replica_groups=mesh['dom'=32,'col'=8] {'col'}, dimensions={0}, use_global_device_ids=true | all-gather | bytes 589824 | tf_op jit(solution)/shard_map/all_gather | solution.py:256
  213.9 1.4 copy-done.4
  215.3 1.9 finish.1
  (71 shorter events, 6.2 us)
Async XLA Ops:
  7.2 10.5 %copy-start.25 = (s32[256,4]{0,1:T(4,128)S(1)}, s32[256,4]{0,1:T(4,128)}, u32[]{:S(2)}) copy-start(s32[256,4]{0,1:T(4,128)} %param.15) | copy-start | bytes 12292
  7.2 10.8 %copy-start.26 = (s32[256,4]{0,1:T(4,128)S(1)}, s32[256,4]{0,1:T(4,128)}, u32[]{:S(2)}) copy-start(s32[256,4]{0,1:T(4,128)} %param.16) | copy-start | bytes 12292
  7.2 39.2 %copy-start.18 = (f32[512]{0:T(512)S(1)}, f32[512]{0:T(512)}, u32[]{:S(2)}) copy-start(f32[512]{0:T(512)} %param.10) | copy-start | bytes 6148
  7.2 39.2 %copy-start.7 = (bf16[192,512]{1,0:T(8,128)(2,1)S(1)}, bf16[192,512]{1,0:T(8,128)(2,1)}, u32[]{:S(2)}) copy-start(bf16[192,512]{1,0:T(8,128)(2,1)} %weight_ref.2) | copy-start | bytes 589828
  9.2 37.2 %all-to-all-start = ((bf16[8,128,512]{2,1,0:T(8,128)(2,1)}), bf16[8,128,512]{2,1,0:T(8,128)(2,1)S(1)}, u32[]{:S(2)}, u32[]{:S(2)}) async-start(bf16[8,128,512]{2,1,0:T(8,128)(2,1)} %broadcast_in_dim.23), calls=%async_computation | async-start | bytes 2097152 | tf_op jit(solution)/shard_map/all_to_all | solution.py:251
  48.0 1.4 copy-start.2
  49.4 1.0 copy-start.5
  50.3 8.8 %copy-start.21 = (bf16[8,128,128]{2,1,0:T(8,128)(2,1)}, bf16[8,128,128]{2,1,0:T(8,128)(2,1)S(1)}, u32[]{:S(2)}) copy-start(bf16[8,128,128]{2,1,0:T(8,128)(2,1)S(1)} %get-tuple-element.20.kv_ref) | copy-start | bytes 786436
  50.3 8.5 %copy-start.27 = (s32[8,8]{1,0:T(8,128)S(1)}, s32[8,8]{1,0:T(8,128)}, u32[]{:S(2)}) copy-start(s32[8,8]{1,0:T(8,128)} %param.14) | copy-start | bytes 772
  50.3 8.5 %copy-start.28 = (s32[8,8]{1,0:T(8,128)S(1)}, s32[8,8]{1,0:T(8,128)}, u32[]{:S(2)}) copy-start(s32[8,8]{1,0:T(8,128)} %param.13) | copy-start | bytes 772
  50.4 45.1 %all-to-all-start.1 = ((bf16[64,128,128]{2,1,0:T(8,128)(2,1)}), bf16[64,128,128]{2,1,0:T(8,128)(2,1)S(1)}, u32[]{:S(2)}, u32[]{:S(2)}) async-start(bf16[64,128,128]{2,1,0:T(8,128)(2,1)} %copy-done.2), calls=%async_computation.1 | async-start | bytes 4194304 | tf_op jit(solution)/shard_map/all_to_all | solution.py:292
  58.1 37.3 %copy-start.13 = (bf16[64,512]{1,0:T(8,128)(2,1)S(1)}, bf16[64,512]{1,0:T(8,128)(2,1)}, u32[]{:S(2)}) copy-start(bf16[64,512]{1,0:T(8,128)(2,1)} %weight_ref.3) | copy-start | bytes 196612
  58.1 37.3 %all-gather.6.cloned.1.call-start = ((), (), s32[]{:S(2)}) async-start(), calls=%async_computation.6 | async-start | bytes 1179648 | tf_op jit(solution)/shard_map/all_gather | solution.py:254
  95.4 1.2 copy-start
  103.8 1.4 copy-start.3
  105.8 0.8 copy-start.19
  107.3 33.4 %all-to-all-start.2 = ((bf16[64,128,128]{2,1,0:T(8,128)(2,1)}), bf16[64,128,128]{2,1,0:T(8,128)(2,1)S(1)}, u32[]{:S(2)}, u32[]{:S(2)}) async-start(bf16[64,128,128]{2,1,0:T(8,128)(2,1)} %copy-done.3), calls=%async_computation.2 | async-start | bytes 4194304 | tf_op jit(solution)/shard_map/all_to_all | solution.py:317
  114.7 99.2 %all-gather.8.cloned.1.call-start = ((), (), s32[]{:S(2)}) async-start(), calls=%async_computation.7 | async-start | bytes 1769472 | tf_op jit(solution)/shard_map/all_gather | solution.py:255
  115.5 1.0 copy-start.20
  116.5 0.9 copy-start.22
  117.5 0.9 copy-start.24
  118.4 22.3 %copy-start.1 = (bf16[1024,512]{1,0:T(8,128)(2,1)S(1)}, bf16[1024,512]{1,0:T(8,128)(2,1)}, u32[]{:S(2)}) copy-start(bf16[1024,512]{1,0:T(8,128)(2,1)} %all-gather.6.cloned.1.call-done) | copy-start | bytes 3145732
  122.7 0.8 copy-start.8
  140.7 1.2 copy-start.6
  141.9 1.0 copy-start.9
  143.0 0.9 copy-start.15
  143.9 0.9 copy-start.17
  147.1 26.2 %copy-start.12 = (bf16[8,256,128]{2,1,0:T(8,128)(2,1)}, bf16[8,256,128]{2,1,0:T(8,128)(2,1)S(1)}, u32[]{:S(2)}) copy-start(bf16[8,256,128]{2,1,0:T(8,128)(2,1)S(1)} %get-tuple-element.28) | copy-start | bytes 1572868
  160.7 53.2 %copy-start.10 = (bf16[128,512]{1,0:T(8,128)(2,1)S(1)}, bf16[128,512]{1,0:T(8,128)(2,1)}, u32[]{:S(2)}) copy-start(bf16[128,512]{1,0:T(8,128)(2,1)} %state_ref.1) | copy-start | bytes 393220
  160.7 53.2 %copy-start.11 = (bf16[128,512]{1,0:T(8,128)(2,1)S(1)}, bf16[128,512]{1,0:T(8,128)(2,1)}, u32[]{:S(2)}) copy-start(bf16[128,512]{1,0:T(8,128)(2,1)} %grad_ref.1) | copy-start | bytes 393220
  173.3 40.6 %all-to-all-start.3 = ((bf16[8,256,128]{2,1,0:T(8,128)(2,1)}), bf16[8,256,128]{2,1,0:T(8,128)(2,1)S(1)}, u32[]{:S(2)}, u32[]{:S(2)}) async-start(bf16[8,256,128]{2,1,0:T(8,128)(2,1)} %copy-done.12), calls=%async_computation.3 | async-start | bytes 1048576 | tf_op jit(solution)/shard_map/all_to_all | solution.py:344
  213.9 1.4 copy-start.4
  (3 other events, 2.0 us)
Sparse Core Ops, SparseCore 0:
  60.7 34.6 all-gather.5
  117.4 38.6 all-gather.7

commit v2 on v1

v2 whole, which is shorter than its diff:
```python
import functools
import math

import jax
import jax.numpy as jnp
from jax import lax
from jax.experimental import pallas as pl
from jax.experimental.pallas import tpu as pltpu
from jax.sharding import PartitionSpec as P

D = 512
HD = 64
BLK = 128
NB = 8
DEG = 4
CAP = 2
ROWS = NB * BLK
EPS = 1e-06
SCALE = 1.0 / math.sqrt(HD)

F32 = jnp.float32
BF16 = jnp.bfloat16
VMEM_LIMIT = 60 * 1024 * 1024

NT = (((1,), (1,)), ((), ()))
TN = (((0,), (0,)), ((), ()))


def dot(a, b):
    return jnp.dot(a, b, preferred_element_type=F32)


def dot_nt(a, b):
    return lax.dot_general(a, b, NT, preferred_element_type=F32)


def whole():
    return pl.BlockSpec(memory_space=pltpu.VMEM)


def scalars():
    return pl.BlockSpec(memory_space=pltpu.SMEM)


def left():
    return pl.BlockSpec(memory_space=pl.ANY)


def shaped(*dims, kind=BF16):
    return jax.ShapeDtypeStruct(dims, kind)


def call(body, outs, ins, scratch=(), flops=0, name=None, out_specs=None, limit=VMEM_LIMIT):
    return pl.pallas_call(
        body,
        out_shape=outs,
        in_specs=ins,
        out_specs=out_specs or [left() for _ in outs],
        scratch_shapes=list(scratch),
        compiler_params=pltpu.CompilerParams(vmem_limit_bytes=limit),
        cost_estimate=pl.CostEstimate(flops=flops, bytes_accessed=1 << 20, transcendentals=0),
        name=name,
    )


def held(shapes):
    return [pltpu.VMEM(s.shape, s.dtype) for s in shapes]


def copies(sources, targets, sems):
    return [
        pltpu.make_async_copy(a, b, sems.at[i]) for i, (a, b) in enumerate(zip(sources, targets, strict=True))
    ]


def start_all(jobs):
    for job in jobs:
        job.start()


def wait_all(jobs):
    for job in jobs:
        job.wait()


def staged(body, numbers, ins, outs, scratch=()):
    def run(*refs):
        scalar_refs, refs = refs[:numbers], refs[numbers:]
        in_refs, refs = refs[: len(ins)], refs[len(ins) :]
        out_refs, refs = refs[: len(outs)], refs[len(outs) :]
        in_held, refs = refs[: len(ins)], refs[len(ins) :]
        out_held, refs = refs[: len(outs)], refs[len(outs) :]
        own, (in_sems, out_sems) = refs[:-2], refs[-2:]
        loads = copies(in_refs, in_held, in_sems)
        start_all(loads)
        wait_all(loads)
        body(*scalar_refs, *in_held, *out_held, *own)
        stores = copies(out_held, out_refs, out_sems)
        start_all(stores)
        wait_all(stores)

    return {
        "body": run,
        "outs": tuple(outs),
        "ins": [scalars()] * numbers + [left()] * len(ins),
        "scratch": [
            *held(ins),
            *held(outs),
            *scratch,
            pltpu.SemaphoreType.DMA((len(ins),)),
            pltpu.SemaphoreType.DMA((len(outs),)),
        ],
    }


def lanes_low(shape):
    return lax.broadcasted_iota(jnp.int32, shape, len(shape) - 1) < HD


def rows_of(b):
    return pl.ds(pl.multiple_of(b * BLK, BLK), BLK)


def ring_gather(x, axis, n):
    up = [(i, (i + 1) % n) for i in range(n)]
    down = [(i, (i - 1) % n) for i in range(n)]
    chunks = [x] * n
    ahead = behind = x
    for k in range(1, n // 2 + 1):
        chunks[k] = ahead = lax.ppermute(ahead, axis, up)
        if k < n - k:
            chunks[n - k] = behind = lax.ppermute(behind, axis, down)
    return chunks


def ring_scatter(pieces, axis, n):
    return [pieces[0]] + [
        lax.ppermute(pieces[k], axis, [(i, (i + k) % n) for i in range(n)]) for k in range(1, n)
    ]


def block_before(col, k):
    return lax.rem(col + NB - k, NB)


def block_after(col, k):
    return lax.rem(col + k, NB)


def project_body(col_ref, send_ref, *refs):
    chunk_refs, refs = refs[:NB], refs[NB:]
    gain_in, weight_in, hidden_out, query_out, kv_out, sent_out, *refs = refs
    chunk_ref, gain_ref, weight_ref, hidden_ref, query_ref, kv_ref, sent_ref, in_sems, out_sems = refs
    loads = copies(
        [gain_in, weight_in, *chunk_refs],
        [gain_ref, weight_ref, *(chunk_ref.at[k] for k in range(NB))],
        in_sems,
    )
    start_all(loads)
    wait_all(loads[:2])
    col = col_ref[0]
    gain = gain_ref[...]
    weight = weight_ref[...]
    wide = jnp.concatenate([weight[:HD], jnp.zeros((HD, D), BF16), weight[HD:]], axis=0)
    for k in range(NB):
        loads[2 + k].wait()
        b = block_before(col, k)
        x = chunk_ref[k].astype(F32)
        inv = lax.rsqrt(jnp.mean(x * x, axis=1, keepdims=True) + EPS)
        hidden = (x * inv * gain).astype(BF16)
        hidden_ref[rows_of(b), :] = hidden
        proj = dot_nt(hidden, wide).astype(BF16)
        query_ref[rows_of(b), :] = proj[:, :BLK] * jnp.asarray(SCALE, BF16)
        kv_ref[b] = proj[:, BLK:]
    parts = out_sems.shape[0] - 3
    step = sent_ref.shape[0] // parts
    stores = copies(
        [hidden_ref, query_ref, kv_ref, *(sent_ref.at[pl.ds(i * step, step)] for i in range(parts))],
        [hidden_out, query_out, kv_out, *(sent_out.at[pl.ds(i * step, step)] for i in range(parts))],
        out_sems,
    )
    for i in range(parts):

        def fill(s, _):
            sent_ref[i * step + s] = kv_ref[send_ref[i * step + s]]
            return 0

        lax.fori_loop(0, step, fill, 0, unroll=True)
        stores[3 + i].start()
    start_all(stores[:3])
    wait_all(stores)


def near_forward_body(query_ref, kv_ref, count_ref, num_ref, ones_ref):
    kv = kv_ref[...].reshape(ROWS, BLK)
    ones_ref[...] = jnp.where(lanes_low(kv.shape), jnp.asarray(1, BF16), kv)

    def step(b, _):
        score = dot_nt(query_ref[rows_of(b), :], kv_ref[...].reshape(ROWS, BLK))
        prob = jnp.exp(score) * count_ref[pl.ds(b, 1), :]
        num_ref[rows_of(b), :] = dot(prob.astype(BF16), ones_ref[...])
        return 0

    lax.fori_loop(0, NB, step, 0, unroll=2)


def attn_grad_body(col_ref, *refs):
    chunk_refs = refs[:NB]
    weight_ref, ag_ref = refs[NB:]
    col = col_ref[0]
    wide = jnp.concatenate([jnp.zeros((HD, D), BF16), weight_ref[...]], axis=0)
    for k in range(NB):
        ag_ref[rows_of(block_before(col, k)), :] = dot_nt(chunk_refs[k][...], wide)


def far_body(
    place_ref,
    query_in,
    far_in,
    num_in,
    ag_in,
    attn_out,
    scaled_out,
    extra_out,
    back_out,
    far_ref,
    query_ref,
    num_ref,
    ag_ref,
    attn_ref,
    scaled_ref,
    extra_ref,
    prob_ref,
    prob_low_ref,
    both_ref,
    stage_ref,
    far_sems,
    in_sems,
    out_sems,
    back_sems,
):
    entries = NB * DEG
    loads = copies([query_in, num_in, ag_in], [query_ref, num_ref, ag_ref], in_sems)
    fetches = copies(
        [far_in.at[place_ref[e]] for e in range(entries)],
        [far_ref.at[pl.ds(e * BLK, BLK)] for e in range(entries)],
        far_sems,
    )
    loads[0].start()
    start_all(fetches)
    start_all(loads[1:])
    wait_all(loads)
    width = DEG * BLK

    for b in range(NB):
        rows = slice(b * BLK, (b + 1) * BLK)
        wait_all(fetches[b * DEG : (b + 1) * DEG])
        kv = far_ref[b * width : (b + 1) * width, :]
        prob = jnp.exp(dot_nt(query_ref[rows, :], kv))
        prob_ref[rows, :] = prob
        prob_low = prob.astype(BF16)
        prob_low_ref[rows, :] = prob_low
        values = jnp.where(lanes_low(kv.shape), jnp.asarray(1, BF16), kv)
        extra_ref[rows, :] = num_ref[rows, :] + dot(prob_low, values)
    for b in range(NB):
        rows = slice(b * BLK, (b + 1) * BLK)
        num = extra_ref[rows, :]
        den = jnp.where(lanes_low(num.shape), num, pltpu.roll(num, HD, 1))
        attn = num / den
        grad = ag_ref[rows, :]
        scaled = (grad / den).astype(BF16)
        scaled_ref[rows, :] = scaled
        extra_ref[rows, :] = jnp.sum(grad * attn, axis=1, keepdims=True) / den
        attn_ref[:, rows] = attn.T[HD:].astype(BF16)
        both_ref[:, rows] = (query_ref[rows, :] + scaled).astype(F32).T.astype(BF16)
    backs = []
    for b in range(NB):
        rows = slice(b * BLK, (b + 1) * BLK)
        kv = far_ref[b * width : (b + 1) * width, :]
        corr = extra_ref[rows, :]
        diff = dot_nt(scaled_ref[rows, :], kv) - corr[:, :1]
        score_grad = (prob_ref[rows, :] * diff).astype(BF16)
        extra_ref[rows, :] = jnp.where(lanes_low(corr.shape), dot(score_grad, kv), corr)
        key_grad = dot(both_ref[:HD, rows], score_grad).astype(BF16)
        value_grad = dot(both_ref[HD:, rows], prob_low_ref[rows, :]).astype(BF16)
        for j in range(DEG):
            e = b * DEG + j
            stage_ref[e, :HD, :] = key_grad[:, j * BLK : (j + 1) * BLK]
            stage_ref[e, HD:, :] = value_grad[:, j * BLK : (j + 1) * BLK]
            back = pltpu.make_async_copy(stage_ref.at[e], back_out.at[place_ref[e]], back_sems.at[e])
            back.start()
            backs.append(back)
    stores = copies([attn_ref, scaled_ref, extra_ref], [attn_out, scaled_out, extra_out], out_sems)
    start_all(stores)
    wait_all(backs)
    wait_all(stores)


def near_backward_body(col_ref, query_ref, kv_ref, count_ref, scaled_ref, extra_ref, attn_ref, hidden_ref, *refs):
    chunk_refs = refs[:NB]
    query_grad_ref, near_ref, part_ref, acc_ref = refs[NB:]
    col = col_ref[0]
    acc_ref[...] = jnp.zeros_like(acc_ref)

    def step(b, _):
        rows = rows_of(b)
        query, scaled, extra = query_ref[rows, :], scaled_ref[rows, :], extra_ref[rows, :]
        kv = kv_ref[...].reshape(ROWS, BLK)
        prob = jnp.exp(dot_nt(query, kv)) * count_ref[pl.ds(b, 1), :]
        diff = dot_nt(scaled, kv) - extra[:, HD : HD + 1]
        score_grad = (prob * diff).astype(BF16)
        query_grad = dot(score_grad, kv) + extra
        query_grad_ref[:, rows] = (query_grad.T[:HD] * SCALE).astype(BF16)
        both = (query + scaled).astype(F32).T.astype(BF16)
        acc_ref[:HD, :] += dot(both[:HD], score_grad)
        acc_ref[HD:, :] += dot(both[HD:], prob.astype(BF16))
        return 0

    lax.fori_loop(0, NB, step, 0)
    for n in range(NB):
        near_ref[n] = acc_ref[:, n * BLK : (n + 1) * BLK]
    part_ref[:HD, :] = dot(query_grad_ref[...], hidden_ref[...]).astype(BF16)
    out_part = jnp.zeros((HD, D), F32)
    for k in range(NB):
        out_part += dot(attn_ref[:, rows_of(block_before(col, k))], chunk_refs[k][...])
    part_ref[HD:, :] = out_part.astype(BF16)


def gather_grads_body(col_ref, home_ref, *refs):
    ins, outs, refs = refs[:6], refs[6 : 7 + NB], refs[7 + NB :]
    returned_in, near_in, query_grad_in, attn_in, hidden_in, early_in = ins
    *piece_refs, part_out = outs
    returned_ref, even_ref, odd_ref, proj_ref, hidden_ref, part_ref, in_sems, out_sems, far_sems = refs
    col = col_ref[0]
    parts = far_sems.shape[0]
    step = returned_in.shape[0] // parts
    fetches = copies(
        [returned_in.at[pl.ds(i * step, step)] for i in range(parts)],
        [returned_ref.at[pl.ds(i * step, step)] for i in range(parts)],
        far_sems,
    )
    loads = copies(
        [near_in, query_grad_in, attn_in, hidden_in, early_in.at[pl.ds(0, HD)], early_in.at[pl.ds(HD, HD)]],
        [
            even_ref.at[pl.ds(0, NB)],
            proj_ref.at[pl.ds(0, HD)],
            proj_ref.at[pl.ds(3 * HD, HD)],
            hidden_ref,
            part_ref.at[pl.ds(0, HD)],
            part_ref.at[pl.ds(3 * HD, HD)],
        ],
        in_sems,
    )
    start_all(loads[:1])
    start_all(fetches)
    start_all(loads[1:])
    odd_ref[...] = jnp.zeros_like(odd_ref)
    loads[0].wait()
    for i in range(parts):
        fetches[i].wait()

        def add(s, _):
            at = i * step + 2 * s
            even, odd = home_ref[at], home_ref[at + 1]
            even_ref[even] += returned_ref[at].astype(F32)
            odd_ref[odd] += returned_ref[at + 1].astype(F32)
            return 0

        lax.fori_loop(0, step // 2, add, 0, unroll=True)
    for n in range(NB):
        proj_ref[HD : 3 * HD, n * BLK : (n + 1) * BLK] = (even_ref[n] + odd_ref[n]).astype(BF16)
    wait_all(loads[1:])
    part_ref[HD : 3 * HD, :] = dot(proj_ref[HD : 3 * HD, :], hidden_ref[...]).astype(BF16)
    stores = copies(
        [part_ref, *(proj_ref.at[:, rows_of(block_after(col, k))] for k in range(NB))],
        [part_out, *piece_refs],
        out_sems,
    )
    start_all(stores)
    wait_all(stores)


def sum_body(share_ref, total_ref):
    total = jnp.sum(share_ref[...].astype(F32), axis=0).astype(BF16)
    total_ref[...] = jnp.broadcast_to(total[None], total_ref.shape)


def scale_body(inv_root, total_ref, qkv_ref, out_ref):
    total = total_ref[...].astype(F32) * inv_root
    qkv_ref[...] = total[: 3 * HD]
    out_ref[...] = total[3 * HD :]


def finish_body(*refs):
    piece_refs, weight_refs = refs[:NB], refs[NB : 2 * NB]
    state_ref, grad_ref, gain_ref, layer_ref, back_ref = refs[2 * NB :]
    out = jnp.zeros((BLK, D), F32)
    back = jnp.zeros((BLK, D), F32)
    for k in range(NB):
        terms = piece_refs[k][...].astype(F32).T.astype(BF16)
        back += dot(terms[:, : 3 * HD], weight_refs[k][: 3 * HD, :])
        out += dot(terms[:, 3 * HD :], weight_refs[k][3 * HD :, :])
    state = state_ref[...].astype(F32)
    gain = gain_ref[...]
    layer_ref[...] = (state + out).astype(BF16)
    inv = lax.rsqrt(jnp.mean(state * state, axis=1, keepdims=True) + EPS)
    stat = jnp.sum(gain * back * state, axis=1, keepdims=True)
    back_ref[...] = (
        grad_ref[...].astype(F32) + inv * gain * back - state * (inv * inv * inv * stat / D)
    ).astype(BF16)


def shards(
    node_states,
    norm_gain,
    qkv_weight,
    out_weight,
    local_slots,
    local_live,
    far_owner,
    far_slot,
    out_grad,
):
    doms = lax.axis_size("dom")
    me = lax.axis_index("dom")
    col = lax.axis_index("col").astype(jnp.int32).reshape(1)
    slots = doms * CAP
    gain = norm_gain[None]

    state_chunks = ring_gather(node_states, "col", NB)

    entries = NB * DEG
    owners = far_owner.reshape(doms, entries)
    wanted = far_slot.reshape(doms, entries)
    place = jnp.arange(entries, dtype=jnp.int32)
    before = place[None, :] < place[:, None]
    rank = jnp.sum((owners[:, :, None] == owners[:, None, :]) & before[None], axis=2, dtype=jnp.int32)
    mine = (owners == me)[:, None, :] & (
        rank[:, None, :] == jnp.arange(CAP, dtype=jnp.int32)[None, :, None]
    )
    home = jnp.min(jnp.where(mine, wanted[:, None, :], NB), axis=2).reshape(slots)
    send = jnp.minimum(home, NB - 1)
    places = (
        lax.dynamic_index_in_dim(owners, me, 0, keepdims=False) * CAP
        + lax.dynamic_index_in_dim(rank, me, 0, keepdims=False)
    )
    block = jnp.arange(NB, dtype=jnp.int32)
    hits = (local_slots[:, :, None] == block[None, None, :]) & (local_live[:, :, None] != 0)
    count = jnp.sum(hits, axis=1, dtype=jnp.int32) + (block[:, None] == block[None, :])
    count = jnp.repeat(count.astype(F32), BLK, axis=1)

    unit = 2 * ROWS * ROWS * BLK
    node = shaped(BLK, D)
    heads_node = shaped(ROWS, BLK)
    heads_float = shaped(ROWS, BLK, kind=F32)
    across = shaped(HD, ROWS)
    blocks = shaped(NB, BLK, BLK)
    exchanged = shaped(slots, BLK, BLK)
    row = shaped(1, D, kind=F32)
    counts = shaped(NB, ROWS, kind=F32)
    states = shaped(ROWS, D)
    piece = shaped(4 * HD, BLK)

    def gather_sems(n):
        return pltpu.SemaphoreType.DMA((n,))

    hidden, query, kv, outgoing = call(
        project_body,
        (states, heads_node, blocks, exchanged),
        [scalars()] * 2 + [left()] * (NB + 2),
        scratch=[
            *held([shaped(NB, BLK, D), row, shaped(3 * HD, D), states, heads_node, blocks, exchanged]),
            gather_sems(NB + 2),
            gather_sems(3 + 4),
        ],
        flops=2 * ROWS * D * 256,
        name="project",
    )(col, send, *state_chunks, gain, qkv_weight)

    outgoing, grad_own = lax.optimization_barrier((outgoing, out_grad))
    fetched = lax.all_to_all(outgoing, "dom", 0, 0, tiled=True)
    grad_chunks = ring_gather(grad_own, "col", NB)

    (near,) = call(
        **staged(near_forward_body, 0, [heads_node, blocks, counts], [heads_float], held([heads_node])),
        flops=2 * unit,
        name="near_forward",
    )(query, kv, count)

    (attn_grad,) = call(
        **staged(attn_grad_body, 1, [node] * NB + [shaped(HD, D)], [heads_float]),
        flops=2 * ROWS * D * BLK,
        name="attn_grad",
    )(col, *grad_chunks, out_weight)

    attn, scaled, extra, outgoing_back = call(
        far_body,
        (across, heads_node, heads_float, exchanged),
        [scalars()] + [left()] * 4,
        scratch=[
            *held([shaped(entries * BLK, BLK), heads_node, heads_float, heads_float]),
            *held([across, heads_node, heads_float]),
            *held([shaped(ROWS, DEG * BLK, kind=F32), shaped(ROWS, DEG * BLK), shaped(BLK, ROWS)]),
            *held([shaped(entries, BLK, BLK)]),
            gather_sems(entries),
            gather_sems(3),
            gather_sems(3),
            gather_sems(entries),
        ],
        flops=2 * unit,
        name="far_both",
    )(places, query, fetched, near, attn_grad)

    outgoing_back, weights_own = lax.optimization_barrier(
        (outgoing_back, jnp.concatenate([qkv_weight, out_weight], axis=0))
    )
    returned = lax.all_to_all(outgoing_back, "dom", 0, 0, tiled=True)
    weight_chunks = ring_gather(weights_own, "col", NB)

    query_grad, near_grad, early = call(
        **staged(
            near_backward_body,
            1,
            [heads_node, blocks, counts, heads_node, heads_float, across, states] + [node] * NB,
            [across, shaped(NB, BLK, BLK, kind=F32), shaped(2 * HD, D)],
            held([shaped(BLK, ROWS, kind=F32)]),
        ),
        flops=5 * unit,
        name="near_backward",
    )(col, query, kv, count, scaled, extra, attn, hidden, *grad_chunks)

    returned, near_grad, *weight_chunks = lax.optimization_barrier((returned, near_grad, *weight_chunks))

    *pieces, part = call(
        gather_grads_body,
        (piece,) * NB + (shaped(4 * HD, D),),
        [scalars()] * 2 + [left()] * 6,
        scratch=[
            *held([exchanged, shaped(NB + 1, BLK, BLK, kind=F32), shaped(NB + 1, BLK, BLK, kind=F32)]),
            *held([shaped(4 * HD, ROWS), states, shaped(4 * HD, D)]),
            gather_sems(6),
            gather_sems(1 + NB),
            gather_sems(4),
        ],
        flops=2 * ROWS * D * 128,
        name="gather_grads",
    )(col, home, returned, near_grad, query_grad, attn, hidden, early)

    share_rows = 4 * HD // doms
    shares = lax.all_to_all(part.reshape(doms, share_rows, D), "dom", 0, 0, tiled=True)
    arrived = ring_scatter(pieces, "col", NB)

    small = 4 * 1024 * 1024
    (totals,) = call(
        sum_body,
        (shaped(doms, share_rows, D),),
        [whole()],
        out_specs=[whole()],
        name="sum_shares",
        limit=small,
    )(shares)
    total = lax.all_to_all(totals, "dom", 0, 0, tiled=True).reshape(4 * HD, D)
    inv_root = 1.0 / math.sqrt(far_owner.shape[0] * BLK)
    qkv_grad, out_weight_grad = call(
        functools.partial(scale_body, inv_root),
        (shaped(3 * HD, D, kind=F32), shaped(HD, D, kind=F32)),
        [whole()],
        out_specs=[whole()] * 2,
        name="scale",
        limit=small,
    )(total)

    layer_out, state_grad = call(
        **staged(
            finish_body,
            0,
            [piece] * NB + [shaped(4 * HD, D)] * NB + [node, node, row],
            [node, node],
        ),
        flops=2 * BLK * D * 2048,
        name="finish",
    )(*arrived, *weight_chunks, node_states, out_grad, gain)

    return (layer_out, state_grad, qkv_grad, out_weight_grad)


def solution(mesh):
    placed = (
        P(("dom", "col"), None),
        P(),
        P("col", None),
        P("col", None),
        P("dom", None),
        P("dom", None),
        P(),
        P(),
        P(("dom", "col"), None),
    )
    return jax.shard_map(
        shards,
        mesh=mesh,
        in_specs=placed,
        out_specs=(
            P(("dom", "col"), None),
            P(("dom", "col"), None),
            P("col", None),
            P("col", None),
        ),
        check_vma=False,
    )
```

time: 226 us -> 181 us (0.80)
  blocking collectives: 60.9 us -> 15.1 us
  starting transfers between devices: 28.1 us -> 68.1 us
  waiting for transfers between devices: 78.7 us -> 45.3 us
  Pallas kernels: 19.6 us -> 39.1 us
  local copies, waits for them, and re-layouts: 21.3 us -> 8.09 us
  between operations: 14.3 us -> 1.21 us
    ppermute x0 -> x28, starting transfers between devices: none -> 47.9 us  [the longest x9 30.1 us: ring_gather(): chunks[n - k] = behind = lax.ppermute(behind, axis, down)]
    ppermute x0 -> x28, waiting for transfers between devices: none -> 45.3 us  [the longest x12 36.7 us: ring_gather(): chunks[k] = ahead = lax.ppermute(ahead, axis, up)]
    all_gather x1 -> x0, blocking collectives: 34.7 us -> none  [shards(): out_weight_whole = lax.all_gather(out_weight, 'col', axis=0)]
    all_gather x2 -> x0, waiting for transfers between devices: 33.8 us -> none  [the longest x1 33.8 us: shards(): grad_whole = lax.all_gather(out_grad, 'col', axis=0)]
    all_to_all x2 -> x1, waiting for transfers between devices: 27.1 us -> 0.01 us  [shards(): total = lax.all_to_all(totals, 'dom', 0, 0, tiled=True).reshape(4 * HD, D)]
    pallas_call x7 -> x9, Pallas kernels: 19.6 us -> 39.1 us  [the longest x1 8.62 us: shards(): call(far_body, (across, heads_node, heads_float, exchanged), [scalars()]...]
    all_to_all x1, waiting for transfers between devices: 16.5 us -> 0.01 us  [shards(): returned = lax.all_to_all(outgoing_back, 'dom', 0, 0, tiled=True)]
    all_to_all x1 -> x0, blocking collectives: 12.6 us -> none  [shards(): total = lax.all_to_all(totals, 'dom', 0, 0, tiled=True).reshape(4 * HD, D)]
  transfers between devices with their start and end apart: 6 -> 31, of which waited for: 3 -> 16; matrix products, arithmetic and copies ran while one was open for 1% -> 3% of each run, Pallas kernels for 4% -> 10%
where the time goes in v2:
time: 181 us; the launch traced here: 179 us
  starting transfers between devices  68.1 us (38%)
  waiting for transfers between devices  45.3 us (25%)
  Pallas kernels  39.1 us (22%)
  blocking collectives  15.1 us (8%)
  local copies, waits for them, and re-layouts  8.09 us (4%)
  other arithmetic  2.16 us (1%)
    ppermute x12, waiting for transfers between devices, ring_gather(): chunks[k] = ahead = lax.ppermute(ahead, axis, up)  36.7 us
    ppermute x9, starting transfers between devices, ring_gather(): chunks[n - k] = behind = lax.ppermute(behind, axis, down)  30.1 us
    ppermute x7, starting transfers between devices, ring_scatter(): lax.ppermute(pieces[k], axis, [(i, (i + k) % n) for i in range(n)])  15.6 us
    all_to_all x1, blocking collectives, shards(): lax.all_to_all(part.reshape(doms, share_rows, D), 'dom', 0, 0, tiled=True)  15.1 us
    pallas_call x1, Pallas kernels, shards(): call(far_body, (across, heads_node, heads_float, exchanged), [scalars()]...  8.62 us
    all_to_all x1, starting transfers between devices, shards(): fetched = lax.all_to_all(outgoing, 'dom', 0, 0, tiled=True)  7.77 us
    pallas_call x1, Pallas kernels, shards(): call(**staged(near_backward_body, 1, [heads_node, blocks, counts, heads_n...  7.67 us
    all_to_all x1, starting transfers between devices, shards(): returned = lax.all_to_all(outgoing_back, 'dom', 0, 0, tiled=True)  7.4 us
  transfers between devices with their start and end apart: 31, of which 16 were waited for; matrix products, arithmetic and copies ran while one was open for 3% of the time, Pallas kernels for 10%

profile of v2, /device:TPU:2, one launch (start us, length us, event | category | flops | bytes accessed | tf_op | source)
XLA Modules:
  0.0 179.1 jit_solution(5937500068250669800)
XLA Ops:
  2.6 4.0 %collective-permute-start.4 = (bf16[128,512]{1,0:T(8,128)(2,1)}, bf16[128,512]{1,0:T(8,128)(2,1)S(1)}, u32[]{:S(2)}, u32[]{:S(2)}) collective-permute-start(bf16[128,512]{1,0:T(8,128)(2,1)} %refs_16_.1), channel_id=1, source_target_pairs={{0,7},{1,0},{2,1},{3,2},{4,3},{5,4},{6,5},{7,6},{8,15},{9,8},{10,9... | collective-permute-start | bytes 393224 | tf_op jit(solution)/shard_map/ppermute | solution.py:132
  7.6 2.7 %collective-permute-done.refs_1_ = bf16[128,512]{1,0:T(8,128)(2,1)S(1)} collective-permute-done((bf16[128,512]{1,0:T(8,128)(2,1)}, bf16[128,512]{1,0:T(8,128)(2,1)S(1)}, u32[]{:S(2)}, u32[]{:S(2)}) %collective-permute-start) | collective-permute-done | bytes 131104 | tf_op jit(solution)/shard_map/ppermute | solution.py:130
  10.3 3.3 %collective-permute-start.5 = (bf16[128,512]{1,0:T(8,128)(2,1)S(1)}, bf16[128,512]{1,0:T(8,128)(2,1)S(1)}, u32[]{:S(2)}, u32[]{:S(2)}) collective-permute-start(bf16[128,512]{1,0:T(8,128)(2,1)S(1)} %collective-permute-done.4.refs_7_), channel_id=1, source_target_pairs={{0,7},{1,0},{2,1},{3,2},{4,3},{5,4},{6,5},{7,6},{8,15},{9,8},{10,9... | collective-permute-start | bytes 393224 | tf_op jit(solution)/shard_map/ppermute | solution.py:132
  13.6 2.8 %collective-permute-done.1.refs_2_ = bf16[128,512]{1,0:T(8,128)(2,1)S(1)} collective-permute-done((bf16[128,512]{1,0:T(8,128)(2,1)S(1)}, bf16[128,512]{1,0:T(8,128)(2,1)S(1)}, u32[]{:S(2)}, u32[]{:S(2)}) %collective-permute-start.1) | collective-permute-done | bytes 131104 | tf_op jit(solution)/shard_map/ppermute | solution.py:130
  18.5 3.3 %collective-permute-start.6 = (bf16[128,512]{1,0:T(8,128)(2,1)S(1)}, bf16[128,512]{1,0:T(8,128)(2,1)S(1)}, u32[]{:S(2)}, u32[]{:S(2)}) collective-permute-start(bf16[128,512]{1,0:T(8,128)(2,1)S(1)} %collective-permute-done.5.refs_6_), channel_id=1, source_target_pairs={{0,7},{1,0},{2,1},{3,2},{4,3},{5,4},{6,5},{7,6},{8,15},{9,8},{10,9... | collective-permute-start | bytes 393224 | tf_op jit(solution)/shard_map/ppermute | solution.py:132
  24.4 4.5 %collective-permute-done.3.refs_4_ = bf16[128,512]{1,0:T(8,128)(2,1)S(1)} collective-permute-done((bf16[128,512]{1,0:T(8,128)(2,1)S(1)}, bf16[128,512]{1,0:T(8,128)(2,1)S(1)}, u32[]{:S(2)}, u32[]{:S(2)}) %collective-permute-start.3) | collective-permute-done | bytes 131104 | tf_op jit(solution)/shard_map/ppermute | solution.py:130
  29.5 6.3 %project.1 = (bf16[1024,512]{1,0:T(8,128)(2,1)}, bf16[1024,128]{1,0:T(8,128)(2,1)}, bf16[8,128,128]{2,1,0:T(8,128)(2,1)}, bf16[64,128,128]{2,1,0:T(8,128)(2,1)}) custom-call(s32[1]{0:T(128)} %bitcast.col_ref.refs_0_, s32[64]{0:T(128)} %broadcast_minimum_fusion.send_ref, bf16[128,512]{1,0:T(8,128)(2,1)} %refs_16_.1, bf16[128,512]{1,0:T(8,128)(2,1)} %copy-done.19, ...), custom_call_target="tpu_custom_call" | custom-call | flops 268435456 | bytes 1048576 | tf_op jit(solution)/shard_map/project/pallas_call | solution.py:467
  35.8 7.8 %all-to-all-start = ((bf16[64,128,128]{2,1,0:T(8,128)(2,1)}), bf16[64,128,128]{2,1,0:T(8,128)(2,1)S(1)}, u32[]{:S(2)}, u32[]{:S(2)}) async-start(bf16[64,128,128]{2,1,0:T(8,128)(2,1)} %get-tuple-element.44), calls=%async_computation | async-start | bytes 4194304 | tf_op jit(solution)/shard_map/all_to_all | solution.py:481
  43.8 3.3 %collective-permute-start.11 = (bf16[128,512]{1,0:T(8,128)(2,1)S(1)}, bf16[128,512]{1,0:T(8,128)(2,1)S(1)}, u32[]{:S(2)}, u32[]{:S(2)}) collective-permute-start(bf16[128,512]{1,0:T(8,128)(2,1)S(1)} %copy-done.4), channel_id=1, source_target_pairs={{0,7},{1,0},{2,1},{3,2},{4,3},{5,4},{6,5},{7,6},{8,15},{9,8},{10,9... | collective-permute-start | bytes 393224 | tf_op jit(solution)/shard_map/ppermute | solution.py:132
  47.1 3.3 %collective-permute-done.7.refs_2_.refs_9_ = bf16[128,512]{1,0:T(8,128)(2,1)S(1)} collective-permute-done((bf16[128,512]{1,0:T(8,128)(2,1)S(1)}, bf16[128,512]{1,0:T(8,128)(2,1)S(1)}, u32[]{:S(2)}, u32[]{:S(2)}) %collective-permute-start.7) | collective-permute-done | bytes 131104 | tf_op jit(solution)/shard_map/ppermute | solution.py:130
  50.5 3.3 %collective-permute-start.12 = (bf16[128,512]{1,0:T(8,128)(2,1)S(1)}, bf16[128,512]{1,0:T(8,128)(2,1)S(1)}, u32[]{:S(2)}, u32[]{:S(2)}) collective-permute-start(bf16[128,512]{1,0:T(8,128)(2,1)S(1)} %collective-permute-done.11.refs_8_.refs_15_), channel_id=1, source_target_pairs={{0,7},{1,0},{2,1},{3,2},{4,3},{5,4},{6,5},{7,6},{8,15},{9,8},{10,9... | collective-permute-start | bytes 393224 | tf_op jit(solution)/shard_map/ppermute | solution.py:132
  53.8 2.8 %collective-permute-done.8.refs_3_.refs_10_ = bf16[128,512]{1,0:T(8,128)(2,1)S(1)} collective-permute-done((bf16[128,512]{1,0:T(8,128)(2,1)S(1)}, bf16[128,512]{1,0:T(8,128)(2,1)S(1)}, u32[]{:S(2)}, u32[]{:S(2)}) %collective-permute-start.8) | collective-permute-done | bytes 131104 | tf_op jit(solution)/shard_map/ppermute | solution.py:130
  57.3 3.3 %collective-permute-start.13 = (bf16[128,512]{1,0:T(8,128)(2,1)S(1)}, bf16[128,512]{1,0:T(8,128)(2,1)S(1)}, u32[]{:S(2)}, u32[]{:S(2)}) collective-permute-start(bf16[128,512]{1,0:T(8,128)(2,1)S(1)} %collective-permute-done.12.refs_7_.refs_14_), channel_id=1, source_target_pairs={{0,7},{1,0},{2,1},{3,2},{4,3},{5,4},{6,5},{7,6},{8,15},{9,8},{10,9... | collective-permute-start | bytes 393224 | tf_op jit(solution)/shard_map/ppermute | solution.py:132
  63.4 4.3 %near_forward.1.num_in = f32[1024,128]{1,0:T(8,128)} custom-call(bf16[1024,128]{1,0:T(8,128)(2,1)} %get-tuple-element.42.refs_0_.query_in.refs_1_, bf16[8,128,128]{2,1,0:T(8,128)(2,1)} %get-tuple-element.45.refs_1_.refs_2_, f32[8,1024]{1,0:T(8,128)} %broadcast_bitcast_fusion.refs_2_.refs_3_), custom_call_target="tpu_custom_call" | custom-call | flops 536870912 | bytes 1048576 | tf_op jit(solution)/shard_map/near_forward/pallas_call | solution.py:484
  69.7 2.6 %attn_grad.1.ag_in = f32[1024,128]{1,0:T(8,128)} custom-call(s32[1]{0:T(128)} %bitcast.col_ref.refs_0_, bf16[128,512]{1,0:T(8,128)(2,1)} %refs_17_.1, bf16[128,512]{1,0:T(8,128)(2,1)} %copy-done.12, bf16[128,512]{1,0:T(8,128)(2,1)} %copy-done.14, bf16[128,512]{1,0:T(8,128)(2,1)} %copy-done.16, bf16[128,512]{1,0:T(8,128)(2,1)} %copy-done.18, ...), custom_call_target="tpu_custom_call" | custom-call | flops 134217728 | bytes 1048576 | tf_op jit(solution)/shard_map/attn_grad/pallas_call | solution.py:490
  73.6 8.6 %far_both.1 = (bf16[64,1024]{1,0:T(8,128)(2,1)}, bf16[1024,128]{1,0:T(8,128)(2,1)}, f32[1024,128]{1,0:T(8,128)}, bf16[64,128,128]{2,1,0:T(8,128)(2,1)}) custom-call(s32[32]{0:T(128)} %add_bitcast_fusion.place_ref, bf16[1024,128]{1,0:T(8,128)(2,1)} %get-tuple-element.42.refs_0_.query_in.refs_1_, bf16[64,128,128]{2,1,0:T(8,128)(2,1)} %copy-done.1, ...), custom_call_target="tpu_custom_call" | custom-call | flops 536870912 | bytes 1048576 | tf_op jit(solution)/shard_map/far_both/pallas_call | solution.py:496
  82.2 7.4 %all-to-all-start.1 = ((bf16[64,128,128]{2,1,0:T(8,128)(2,1)}), bf16[64,128,128]{2,1,0:T(8,128)(2,1)S(1)}, u32[]{:S(2)}, u32[]{:S(2)}) async-start(bf16[64,128,128]{2,1,0:T(8,128)(2,1)} %get-tuple-element.48), calls=%async_computation.1 | async-start | bytes 4194304 | tf_op jit(solution)/shard_map/all_to_all | solution.py:517
  89.8 3.2 %collective-permute-start.18 = (bf16[256,512]{1,0:T(8,128)(2,1)S(1)}, bf16[256,512]{1,0:T(8,128)(2,1)S(1)}, u32[]{:S(2)}, u32[]{:S(2)}) collective-permute-start(bf16[256,512]{1,0:T(8,128)(2,1)S(1)} %pad_maximum_fusion.refs_8_), channel_id=1, source_target_pairs={{0,7},{1,0},{2,1},{3,2},{4,3},{5,4},{6,5},{7,6},{8,15},{9,8},{10,9... | collective-permute-start | bytes 786440 | tf_op jit(solution)/shard_map/ppermute | solution.py:132
  93.0 6.3 %collective-permute-done.14.refs_9_ = bf16[256,512]{1,0:T(8,128)(2,1)S(1)} collective-permute-done((bf16[256,512]{1,0:T(8,128)(2,1)S(1)}, bf16[256,512]{1,0:T(8,128)(2,1)S(1)}, u32[]{:S(2)}, u32[]{:S(2)}) %collective-permute-start.14) | collective-permute-done | bytes 262176 | tf_op jit(solution)/shard_map/ppermute | solution.py:130
  99.3 3.2 %collective-permute-start.19 = (bf16[256,512]{1,0:T(8,128)(2,1)S(1)}, bf16[256,512]{1,0:T(8,128)(2,1)S(1)}, u32[]{:S(2)}, u32[]{:S(2)}) collective-permute-start(bf16[256,512]{1,0:T(8,128)(2,1)S(1)} %collective-permute-done.18.refs_15_), channel_id=1, source_target_pairs={{0,7},{1,0},{2,1},{3,2},{4,3},{5,4},{6,5},{7,6},{8,15},{9,8},{10,9... | collective-permute-start | bytes 786440 | tf_op jit(solution)/shard_map/ppermute | solution.py:132
  102.5 5.5 %collective-permute-done.15.refs_10_ = bf16[256,512]{1,0:T(8,128)(2,1)S(1)} collective-permute-done((bf16[256,512]{1,0:T(8,128)(2,1)S(1)}, bf16[256,512]{1,0:T(8,128)(2,1)S(1)}, u32[]{:S(2)}, u32[]{:S(2)}) %collective-permute-start.15) | collective-permute-done | bytes 262176 | tf_op jit(solution)/shard_map/ppermute | solution.py:130
  108.1 3.2 %collective-permute-start.20 = (bf16[256,512]{1,0:T(8,128)(2,1)S(1)}, bf16[256,512]{1,0:T(8,128)(2,1)S(1)}, u32[]{:S(2)}, u32[]{:S(2)}) collective-permute-start(bf16[256,512]{1,0:T(8,128)(2,1)S(1)} %collective-permute-done.19.refs_14_), channel_id=1, source_target_pairs={{0,7},{1,0},{2,1},{3,2},{4,3},{5,4},{6,5},{7,6},{8,15},{9,8},{10,9... | collective-permute-start | bytes 786440 | tf_op jit(solution)/shard_map/ppermute | solution.py:132
  111.3 4.6 %collective-permute-done.16.refs_11_ = bf16[256,512]{1,0:T(8,128)(2,1)S(1)} collective-permute-done((bf16[256,512]{1,0:T(8,128)(2,1)S(1)}, bf16[256,512]{1,0:T(8,128)(2,1)S(1)}, u32[]{:S(2)}, u32[]{:S(2)}) %collective-permute-start.16) | collective-permute-done | bytes 262176 | tf_op jit(solution)/shard_map/ppermute | solution.py:130
  115.9 7.7 %near_backward.1 = (bf16[64,1024]{1,0:T(8,128)(2,1)}, f32[8,128,128]{2,1,0:T(8,128)}, bf16[128,512]{1,0:T(8,128)(2,1)}) custom-call(s32[1]{0:T(128)} %bitcast.col_ref.refs_0_, bf16[1024,128]{1,0:T(8,128)(2,1)} %get-tuple-element.42.refs_0_.query_in.refs_1_, bf16[8,128,128]{2,1,0:T(8,128)(2,1)} %get-tuple-element.45.refs_1_.refs_2_, ...), custom_call_target="tpu_custom_call" | custom-call | flops 1342177280 | bytes 1048576 | tf_op jit(solution)/shard_map/near_backward/pallas_call | solution.py:520
  125.7 4.3 %gather_grads.1 = (bf16[256,128]{1,0:T(8,128)(2,1)}, bf16[256,128]{1,0:T(8,128)(2,1)}, bf16[256,128]{1,0:T(8,128)(2,1)}, bf16[256,128]{1,0:T(8,128)(2,1)}, bf16[...) custom-call(s32[1]{0:T(128)} %bitcast.col_ref.refs_0_, ...), custom_call_target="tpu_custom_call" | custom-call | flops 134217728 | bytes 1048576 | tf_op jit(solution)/shard_map/gather_grads/pallas_call | solution.py:534
  129.9 15.1 %all_to_all.20.share_ref = bf16[32,8,512]{2,1,0:T(8,128)(2,1)S(1)} all-to-all(bf16[32,8,512]{2,1,0:T(8,128)(2,1)} %bitcast.9), channel_id=1, replica_groups=mesh['dom'=32,'col'=8] {'dom'}, dimensions={0} | all-to-all | bytes 524288 | tf_op jit(solution)/shard_map/all_to_all | solution.py:550
  145.8 5.0 %all-to-all-start.3 = ((bf16[32,8,512]{2,1,0:T(8,128)(2,1)}), bf16[32,8,512]{2,1,0:T(8,128)(2,1)S(1)}, u32[]{:S(2)}, u32[]{:S(2)}) async-start(bf16[32,8,512]{2,1,0:T(8,128)(2,1)} %sum_shares.1), calls=%async_computation.3 | async-start | bytes 524288 | tf_op jit(solution)/shard_map/all_to_all | solution.py:562
  150.9 5.3 %collective-permute-start.22 = (bf16[256,128]{1,0:T(8,128)(2,1)}, bf16[256,128]{1,0:T(8,128)(2,1)S(1)}, u32[]{:S(2)}, u32[]{:S(2)}) collective-permute-start(bf16[256,128]{1,0:T(8,128)(2,1)} %get-tuple-element.61), channel_id=1, source_target_pairs={{0,2},{1,3},{2,4},{3,5},{4,6},{5,7},{6,0},{7,1},{8,10},{9,11},{10,... | collective-permute-start | bytes 196616 | tf_op jit(solution)/shard_map/ppermute | solution.py:138
  156.2 2.8 %collective-permute-start.24 = (bf16[256,128]{1,0:T(8,128)(2,1)}, bf16[256,128]{1,0:T(8,128)(2,1)S(1)}, u32[]{:S(2)}, u32[]{:S(2)}) collective-permute-start(bf16[256,128]{1,0:T(8,128)(2,1)} %get-tuple-element.63), channel_id=1, source_target_pairs={{0,4},{1,5},{2,6},{3,7},{4,0},{5,1},{6,2},{7,3},{8,12},{9,13},{10,... | collective-permute-start | bytes 196616 | tf_op jit(solution)/shard_map/ppermute | solution.py:138
  159.0 3.9 %collective-permute-start.25 = (bf16[256,128]{1,0:T(8,128)(2,1)}, bf16[256,128]{1,0:T(8,128)(2,1)S(1)}, u32[]{:S(2)}, u32[]{:S(2)}) collective-permute-start(bf16[256,128]{1,0:T(8,128)(2,1)} %get-tuple-element.64), channel_id=1, source_target_pairs={{0,5},{1,6},{2,7},{3,0},{4,1},{5,2},{6,3},{7,4},{8,13},{9,14},{10,... | collective-permute-start | bytes 196616 | tf_op jit(solution)/shard_map/ppermute | solution.py:138
  166.6 2.8 %collective-permute-done.25.refs_5_ = bf16[256,128]{1,0:T(8,128)(2,1)S(1)} collective-permute-done((bf16[256,128]{1,0:T(8,128)(2,1)}, bf16[256,128]{1,0:T(8,128)(2,1)S(1)}, u32[]{:S(2)}, u32[]{:S(2)}) %collective-permute-start.25) | collective-permute-done | bytes 65568 | tf_op jit(solution)/shard_map/ppermute | solution.py:138
  174.4 3.9 %finish.1 = (bf16[128,512]{1,0:T(8,128)(2,1)}, bf16[128,512]{1,0:T(8,128)(2,1)}) custom-call(bf16[256,128]{1,0:T(8,128)(2,1)} %get-tuple-element.59.refs_0_, bf16[256,128]{1,0:T(8,128)(2,1)} %copy-done.26, bf16[256,128]{1,0:T(8,128)(2,1)} %copy-done.27, bf16[256,128]{1,0:T(8,128)(2,1)} %copy-done.28, bf16[256,128]{1,0:T(8,128)(2,1)} %copy-done.29, ...), custom_call_target="tpu_custom_call" | custom-call | flops 268435456 | bytes 1048576 | tf_op jit(solution)/shard_map/finish/pallas_call | solution.py:573
  (130 shorter events, 27.5 us)
Async XLA Ops:
  0.6 9.6 %collective-permute-start = (bf16[128,512]{1,0:T(8,128)(2,1)}, bf16[128,512]{1,0:T(8,128)(2,1)S(1)}, u32[]{:S(2)}, u32[]{:S(2)}) collective-permute-start(bf16[128,512]{1,0:T(8,128)(2,1)} %refs_16_.1), channel_id=1, source_target_pairs={{0,1},{1,2},{2,3},{3,4},{4,5},{5,6},{6,7},{7,0},{8,9},{9,10},{10,1... | collective-permute-start | bytes 393224 | tf_op jit(solution)/shard_map/ppermute | solution.py:130
  2.6 7.7 %collective-permute-start.4 = (bf16[128,512]{1,0:T(8,128)(2,1)}, bf16[128,512]{1,0:T(8,128)(2,1)S(1)}, u32[]{:S(2)}, u32[]{:S(2)}) collective-permute-start(bf16[128,512]{1,0:T(8,128)(2,1)} %refs_16_.1), channel_id=1, source_target_pairs={{0,7},{1,0},{2,1},{3,2},{4,3},{5,4},{6,5},{7,6},{8,15},{9,8},{10,9... | collective-permute-start | bytes 393224 | tf_op jit(solution)/shard_map/ppermute | solution.py:132
  10.3 6.2 %collective-permute-start.1 = (bf16[128,512]{1,0:T(8,128)(2,1)S(1)}, bf16[128,512]{1,0:T(8,128)(2,1)S(1)}, u32[]{:S(2)}, u32[]{:S(2)}) collective-permute-start(bf16[128,512]{1,0:T(8,128)(2,1)S(1)} %collective-permute-done.refs_1_), channel_id=1, source_target_pairs={{0,1},{1,2},{2,3},{3,4},{4,5},{5,6},{6,7},{7,0},{8,9},{9,10},{10,1... | collective-permute-start | bytes 393224 | tf_op jit(solution)/shard_map/ppermute | solution.py:130
  10.3 8.2 %collective-permute-start.5 = (bf16[128,512]{1,0:T(8,128)(2,1)S(1)}, bf16[128,512]{1,0:T(8,128)(2,1)S(1)}, u32[]{:S(2)}, u32[]{:S(2)}) collective-permute-start(bf16[128,512]{1,0:T(8,128)(2,1)S(1)} %collective-permute-done.4.refs_7_), channel_id=1, source_target_pairs={{0,7},{1,0},{2,1},{3,2},{4,3},{5,4},{6,5},{7,6},{8,15},{9,8},{10,9... | collective-permute-start | bytes 393224 | tf_op jit(solution)/shard_map/ppermute | solution.py:132
  16.5 6.2 %collective-permute-start.2 = (bf16[128,512]{1,0:T(8,128)(2,1)S(1)}, bf16[128,512]{1,0:T(8,128)(2,1)S(1)}, u32[]{:S(2)}, u32[]{:S(2)}) collective-permute-start(bf16[128,512]{1,0:T(8,128)(2,1)S(1)} %collective-permute-done.1.refs_2_), channel_id=1, source_target_pairs={{0,1},{1,2},{2,3},{3,4},{4,5},{5,6},{6,7},{7,0},{8,9},{9,10},{10,1... | collective-permute-start | bytes 393224 | tf_op jit(solution)/shard_map/ppermute | solution.py:130
  18.5 5.8 %collective-permute-start.6 = (bf16[128,512]{1,0:T(8,128)(2,1)S(1)}, bf16[128,512]{1,0:T(8,128)(2,1)S(1)}, u32[]{:S(2)}, u32[]{:S(2)}) collective-permute-start(bf16[128,512]{1,0:T(8,128)(2,1)S(1)} %collective-permute-done.5.refs_6_), channel_id=1, source_target_pairs={{0,7},{1,0},{2,1},{3,2},{4,3},{5,4},{6,5},{7,6},{8,15},{9,8},{10,9... | collective-permute-start | bytes 393224 | tf_op jit(solution)/shard_map/ppermute | solution.py:132
  22.6 6.2 %collective-permute-start.3 = (bf16[128,512]{1,0:T(8,128)(2,1)S(1)}, bf16[128,512]{1,0:T(8,128)(2,1)S(1)}, u32[]{:S(2)}, u32[]{:S(2)}) collective-permute-start(bf16[128,512]{1,0:T(8,128)(2,1)S(1)} %collective-permute-done.2.refs_3_), channel_id=1, source_target_pairs={{0,1},{1,2},{2,3},{3,4},{4,5},{5,6},{6,7},{7,0},{8,9},{9,10},{10,1... | collective-permute-start | bytes 393224 | tf_op jit(solution)/shard_map/ppermute | solution.py:130
  35.8 36.5 %all-to-all-start = ((bf16[64,128,128]{2,1,0:T(8,128)(2,1)}), bf16[64,128,128]{2,1,0:T(8,128)(2,1)S(1)}, u32[]{:S(2)}, u32[]{:S(2)}) async-start(bf16[64,128,128]{2,1,0:T(8,128)(2,1)} %get-tuple-element.44), calls=%async_computation | async-start | bytes 4194304 | tf_op jit(solution)/shard_map/all_to_all | solution.py:481
  43.6 6.8 %collective-permute-start.7 = (bf16[128,512]{1,0:T(8,128)(2,1)S(1)}, bf16[128,512]{1,0:T(8,128)(2,1)S(1)}, u32[]{:S(2)}, u32[]{:S(2)}) collective-permute-start(bf16[128,512]{1,0:T(8,128)(2,1)S(1)} %copy-done.4), channel_id=1, source_target_pairs={{0,1},{1,2},{2,3},{3,4},{4,5},{5,6},{6,7},{7,0},{8,9},{9,10},{10,1... | collective-permute-start | bytes 393224 | tf_op jit(solution)/shard_map/ppermute | solution.py:130
  43.8 6.7 %collective-permute-start.11 = (bf16[128,512]{1,0:T(8,128)(2,1)S(1)}, bf16[128,512]{1,0:T(8,128)(2,1)S(1)}, u32[]{:S(2)}, u32[]{:S(2)}) collective-permute-start(bf16[128,512]{1,0:T(8,128)(2,1)S(1)} %copy-done.4), channel_id=1, source_target_pairs={{0,7},{1,0},{2,1},{3,2},{4,3},{5,4},{6,5},{7,6},{8,15},{9,8},{10,9... | collective-permute-start | bytes 393224 | tf_op jit(solution)/shard_map/ppermute | solution.py:132
  50.4 6.2 %collective-permute-start.8 = (bf16[128,512]{1,0:T(8,128)(2,1)S(1)}, bf16[128,512]{1,0:T(8,128)(2,1)S(1)}, u32[]{:S(2)}, u32[]{:S(2)}) collective-permute-start(bf16[128,512]{1,0:T(8,128)(2,1)S(1)} %collective-permute-done.7.refs_2_.refs_9_), channel_id=1, source_target_pairs={{0,1},{1,2},{2,3},{3,4},{4,5},{5,6},{6,7},{7,0},{8,9},{9,10},{10,1... | collective-permute-start | bytes 393224 | tf_op jit(solution)/shard_map/ppermute | solution.py:130
  50.5 6.8 %collective-permute-start.12 = (bf16[128,512]{1,0:T(8,128)(2,1)S(1)}, bf16[128,512]{1,0:T(8,128)(2,1)S(1)}, u32[]{:S(2)}, u32[]{:S(2)}) collective-permute-start(bf16[128,512]{1,0:T(8,128)(2,1)S(1)} %collective-permute-done.11.refs_8_.refs_15_), channel_id=1, source_target_pairs={{0,7},{1,0},{2,1},{3,2},{4,3},{5,4},{6,5},{7,6},{8,15},{9,8},{10,9... | collective-permute-start | bytes 393224 | tf_op jit(solution)/shard_map/ppermute | solution.py:132
  56.6 6.2 %collective-permute-start.9 = (bf16[128,512]{1,0:T(8,128)(2,1)S(1)}, bf16[128,512]{1,0:T(8,128)(2,1)S(1)}, u32[]{:S(2)}, u32[]{:S(2)}) collective-permute-start(bf16[128,512]{1,0:T(8,128)(2,1)S(1)} %collective-permute-done.8.refs_3_.refs_10_), channel_id=1, source_target_pairs={{0,1},{1,2},{2,3},{3,4},{4,5},{5,6},{6,7},{7,0},{8,9},{9,10},{10,1... | collective-permute-start | bytes 393224 | tf_op jit(solution)/shard_map/ppermute | solution.py:130
  57.3 32.4 %copy-start.2 = (bf16[256,512]{1,0:T(8,128)(2,1)}, bf16[256,512]{1,0:T(8,128)(2,1)S(1)}, u32[]{:S(2)}) copy-start(bf16[256,512]{1,0:T(8,128)(2,1)S(1)} %pad_maximum_fusion.refs_8_) | copy-start | bytes 786436
  57.3 10.4 %collective-permute-start.13 = (bf16[128,512]{1,0:T(8,128)(2,1)S(1)}, bf16[128,512]{1,0:T(8,128)(2,1)S(1)}, u32[]{:S(2)}, u32[]{:S(2)}) collective-permute-start(bf16[128,512]{1,0:T(8,128)(2,1)S(1)} %collective-permute-done.12.refs_7_.refs_14_), channel_id=1, source_target_pairs={{0,7},{1,0},{2,1},{3,2},{4,3},{5,4},{6,5},{7,6},{8,15},{9,8},{10,9... | collective-permute-start | bytes 393224 | tf_op jit(solution)/shard_map/ppermute | solution.py:132
  62.8 6.2 %collective-permute-start.10 = (bf16[128,512]{1,0:T(8,128)(2,1)S(1)}, bf16[128,512]{1,0:T(8,128)(2,1)S(1)}, u32[]{:S(2)}, u32[]{:S(2)}) collective-permute-start(bf16[128,512]{1,0:T(8,128)(2,1)S(1)} %collective-permute-done.9.refs_4_.refs_11_), channel_id=1, source_target_pairs={{0,1},{1,2},{2,3},{3,4},{4,5},{5,6},{6,7},{7,0},{8,9},{9,10},{10,1... | collective-permute-start | bytes 393224 | tf_op jit(solution)/shard_map/ppermute | solution.py:130
  82.2 42.1 %all-to-all-start.1 = ((bf16[64,128,128]{2,1,0:T(8,128)(2,1)}), bf16[64,128,128]{2,1,0:T(8,128)(2,1)S(1)}, u32[]{:S(2)}, u32[]{:S(2)}) async-start(bf16[64,128,128]{2,1,0:T(8,128)(2,1)} %get-tuple-element.48), calls=%async_computation.1 | async-start | bytes 4194304 | tf_op jit(solution)/shard_map/all_to_all | solution.py:517
  89.7 9.6 %collective-permute-start.14 = (bf16[256,512]{1,0:T(8,128)(2,1)S(1)}, bf16[256,512]{1,0:T(8,128)(2,1)S(1)}, u32[]{:S(2)}, u32[]{:S(2)}) collective-permute-start(bf16[256,512]{1,0:T(8,128)(2,1)S(1)} %pad_maximum_fusion.refs_8_), channel_id=1, source_target_pairs={{0,1},{1,2},{2,3},{3,4},{4,5},{5,6},{6,7},{7,0},{8,9},{9,10},{10,1... | collective-permute-start | bytes 786440 | tf_op jit(solution)/shard_map/ppermute | solution.py:130
  89.8 9.6 %collective-permute-start.18 = (bf16[256,512]{1,0:T(8,128)(2,1)S(1)}, bf16[256,512]{1,0:T(8,128)(2,1)S(1)}, u32[]{:S(2)}, u32[]{:S(2)}) collective-permute-start(bf16[256,512]{1,0:T(8,128)(2,1)S(1)} %pad_maximum_fusion.refs_8_), channel_id=1, source_target_pairs={{0,7},{1,0},{2,1},{3,2},{4,3},{5,4},{6,5},{7,6},{8,15},{9,8},{10,9... | collective-permute-start | bytes 786440 | tf_op jit(solution)/shard_map/ppermute | solution.py:132
  99.3 8.7 %collective-permute-start.15 = (bf16[256,512]{1,0:T(8,128)(2,1)S(1)}, bf16[256,512]{1,0:T(8,128)(2,1)S(1)}, u32[]{:S(2)}, u32[]{:S(2)}) collective-permute-start(bf16[256,512]{1,0:T(8,128)(2,1)S(1)} %collective-permute-done.14.refs_9_), channel_id=1, source_target_pairs={{0,1},{1,2},{2,3},{3,4},{4,5},{5,6},{6,7},{7,0},{8,9},{9,10},{10,1... | collective-permute-start | bytes 786440 | tf_op jit(solution)/shard_map/ppermute | solution.py:130
  99.3 8.7 %collective-permute-start.19 = (bf16[256,512]{1,0:T(8,128)(2,1)S(1)}, bf16[256,512]{1,0:T(8,128)(2,1)S(1)}, u32[]{:S(2)}, u32[]{:S(2)}) collective-permute-start(bf16[256,512]{1,0:T(8,128)(2,1)S(1)} %collective-permute-done.18.refs_15_), channel_id=1, source_target_pairs={{0,7},{1,0},{2,1},{3,2},{4,3},{5,4},{6,5},{7,6},{8,15},{9,8},{10,9... | collective-permute-start | bytes 786440 | tf_op jit(solution)/shard_map/ppermute | solution.py:132
  108.0 7.8 %collective-permute-start.16 = (bf16[256,512]{1,0:T(8,128)(2,1)S(1)}, bf16[256,512]{1,0:T(8,128)(2,1)S(1)}, u32[]{:S(2)}, u32[]{:S(2)}) collective-permute-start(bf16[256,512]{1,0:T(8,128)(2,1)S(1)} %collective-permute-done.15.refs_10_), channel_id=1, source_target_pairs={{0,1},{1,2},{2,3},{3,4},{4,5},{5,6},{6,7},{7,0},{8,9},{9,10},{10,1... | collective-permute-start | bytes 786440 | tf_op jit(solution)/shard_map/ppermute | solution.py:130
  108.1 15.5 %collective-permute-start.20 = (bf16[256,512]{1,0:T(8,128)(2,1)S(1)}, bf16[256,512]{1,0:T(8,128)(2,1)S(1)}, u32[]{:S(2)}, u32[]{:S(2)}) collective-permute-start(bf16[256,512]{1,0:T(8,128)(2,1)S(1)} %collective-permute-done.19.refs_14_), channel_id=1, source_target_pairs={{0,7},{1,0},{2,1},{3,2},{4,3},{5,4},{6,5},{7,6},{8,15},{9,8},{10,9... | collective-permute-start | bytes 786440 | tf_op jit(solution)/shard_map/ppermute | solution.py:132
  115.9 8.4 %collective-permute-start.17 = (bf16[256,512]{1,0:T(8,128)(2,1)S(1)}, bf16[256,512]{1,0:T(8,128)(2,1)}, u32[]{:S(2)}, u32[]{:S(2)}) collective-permute-start(bf16[256,512]{1,0:T(8,128)(2,1)S(1)} %collective-permute-done.16.refs_11_), channel_id=1, source_target_pairs={{0,1},{1,2},{2,3},{3,4},{4,5},{5,6},{6,7},{7,0},{8,9},{9,10},{10,1... | collective-permute-start | bytes 786440 | tf_op jit(solution)/shard_map/ppermute | solution.py:130
  145.8 32.5 %all-to-all-start.3 = ((bf16[32,8,512]{2,1,0:T(8,128)(2,1)}), bf16[32,8,512]{2,1,0:T(8,128)(2,1)S(1)}, u32[]{:S(2)}, u32[]{:S(2)}) async-start(bf16[32,8,512]{2,1,0:T(8,128)(2,1)} %sum_shares.1), calls=%async_computation.3 | async-start | bytes 524288 | tf_op jit(solution)/shard_map/all_to_all | solution.py:562
  150.8 12.1 %collective-permute-start.21 = (bf16[256,128]{1,0:T(8,128)(2,1)}, bf16[256,128]{1,0:T(8,128)(2,1)S(1)}, u32[]{:S(2)}, u32[]{:S(2)}) collective-permute-start(bf16[256,128]{1,0:T(8,128)(2,1)} %get-tuple-element.60), channel_id=1, source_target_pairs={{0,1},{1,2},{2,3},{3,4},{4,5},{5,6},{6,7},{7,0},{8,9},{9,10},{10,1... | collective-permute-start | bytes 196616 | tf_op jit(solution)/shard_map/ppermute | solution.py:138
  150.9 13.9 %collective-permute-start.22 = (bf16[256,128]{1,0:T(8,128)(2,1)}, bf16[256,128]{1,0:T(8,128)(2,1)S(1)}, u32[]{:S(2)}, u32[]{:S(2)}) collective-permute-start(bf16[256,128]{1,0:T(8,128)(2,1)} %get-tuple-element.61), channel_id=1, source_target_pairs={{0,2},{1,3},{2,4},{3,5},{4,6},{5,7},{6,0},{7,1},{8,10},{9,11},{10,... | collective-permute-start | bytes 196616 | tf_op jit(solution)/shard_map/ppermute | solution.py:138
  156.2 10.4 %collective-permute-start.23 = (bf16[256,128]{1,0:T(8,128)(2,1)}, bf16[256,128]{1,0:T(8,128)(2,1)S(1)}, u32[]{:S(2)}, u32[]{:S(2)}) collective-permute-start(bf16[256,128]{1,0:T(8,128)(2,1)} %get-tuple-element.62), channel_id=1, source_target_pairs={{0,3},{1,4},{2,5},{3,6},{4,7},{5,0},{6,1},{7,2},{8,11},{9,12},{10,... | collective-permute-start | bytes 196616 | tf_op jit(solution)/shard_map/ppermute | solution.py:138
  156.2 10.4 %collective-permute-start.24 = (bf16[256,128]{1,0:T(8,128)(2,1)}, bf16[256,128]{1,0:T(8,128)(2,1)S(1)}, u32[]{:S(2)}, u32[]{:S(2)}) collective-permute-start(bf16[256,128]{1,0:T(8,128)(2,1)} %get-tuple-element.63), channel_id=1, source_target_pairs={{0,4},{1,5},{2,6},{3,7},{4,0},{5,1},{6,2},{7,3},{8,12},{9,13},{10,... | collective-permute-start | bytes 196616 | tf_op jit(solution)/shard_map/ppermute | solution.py:138
  159.0 10.5 %collective-permute-start.25 = (bf16[256,128]{1,0:T(8,128)(2,1)}, bf16[256,128]{1,0:T(8,128)(2,1)S(1)}, u32[]{:S(2)}, u32[]{:S(2)}) collective-permute-start(bf16[256,128]{1,0:T(8,128)(2,1)} %get-tuple-element.64), channel_id=1, source_target_pairs={{0,5},{1,6},{2,7},{3,0},{4,1},{5,2},{6,3},{7,4},{8,13},{9,14},{10,... | collective-permute-start | bytes 196616 | tf_op jit(solution)/shard_map/ppermute | solution.py:138
  162.9 9.1 %collective-permute-start.26 = (bf16[256,128]{1,0:T(8,128)(2,1)}, bf16[256,128]{1,0:T(8,128)(2,1)S(1)}, u32[]{:S(2)}, u32[]{:S(2)}) collective-permute-start(bf16[256,128]{1,0:T(8,128)(2,1)} %get-tuple-element.65), channel_id=1, source_target_pairs={{0,6},{1,7},{2,0},{3,1},{4,2},{5,3},{6,4},{7,5},{8,14},{9,15},{10,... | collective-permute-start | bytes 196616 | tf_op jit(solution)/shard_map/ppermute | solution.py:138
  164.8 8.9 %collective-permute-start.27 = (bf16[256,128]{1,0:T(8,128)(2,1)}, bf16[256,128]{1,0:T(8,128)(2,1)S(1)}, u32[]{:S(2)}, u32[]{:S(2)}) collective-permute-start(bf16[256,128]{1,0:T(8,128)(2,1)} %get-tuple-element.66), channel_id=1, source_target_pairs={{0,7},{1,0},{2,1},{3,2},{4,3},{5,4},{6,5},{7,6},{8,15},{9,8},{10,9... | collective-permute-start | bytes 196616 | tf_op jit(solution)/shard_map/ppermute | solution.py:138
  (35 other events, 355.8 us)

commit v3 on v1

v3 whole, which is shorter than its diff:
```python
import functools
import math

import jax
import jax.numpy as jnp
from jax import lax
from jax.experimental import pallas as pl
from jax.experimental.pallas import tpu as pltpu
from jax.sharding import PartitionSpec as P

D = 512
HD = 64
BLK = 128
NB = 8
DEG = 4
CAP = 2
ROWS = NB * BLK
EPS = 1e-06
SCALE = 1.0 / math.sqrt(HD)

F32 = jnp.float32
BF16 = jnp.bfloat16
MIB = 1024 * 1024
LIMIT = 64
ORDER = (0, 1, 7, 2, 6, 3, 5, 4)

NT = (((1,), (1,)), ((), ()))
TN = (((0,), (0,)), ((), ()))


def dot(a, b):
    return jnp.dot(a, b, preferred_element_type=F32)


def dot_nt(a, b):
    return lax.dot_general(a, b, NT, preferred_element_type=F32)


def whole():
    return pl.BlockSpec(memory_space=pltpu.VMEM)


def scalars():
    return pl.BlockSpec(memory_space=pltpu.SMEM)


def left():
    return pl.BlockSpec(memory_space=pl.ANY)


def shaped(*dims, kind=BF16):
    return jax.ShapeDtypeStruct(dims, kind)


def call(body, outs, ins, scratch=(), flops=0, name=None, out_specs=None, limit=LIMIT, aliases=None):
    return pl.pallas_call(
        body,
        out_shape=outs,
        in_specs=ins,
        out_specs=out_specs or [left() for _ in outs],
        scratch_shapes=list(scratch),
        input_output_aliases=aliases or {},
        compiler_params=pltpu.CompilerParams(vmem_limit_bytes=limit * MIB),
        cost_estimate=pl.CostEstimate(flops=flops, bytes_accessed=1 << 20, transcendentals=0),
        name=name,
    )


def held(*shapes):
    return [pltpu.VMEM(s.shape, s.dtype) for s in shapes]


def dma_sems(n):
    return pltpu.SemaphoreType.DMA((n,))


def copies(sources, targets, sems):
    return [
        pltpu.make_async_copy(a, b, sems.at[i]) for i, (a, b) in enumerate(zip(sources, targets, strict=True))
    ]


def start_all(jobs):
    for job in jobs:
        job.start()


def wait_all(jobs):
    for job in jobs:
        job.wait()


def lanes_low(shape):
    return lax.broadcasted_iota(jnp.int32, shape, len(shape) - 1) < HD


def rows_at(i):
    return slice(i * BLK, (i + 1) * BLK)


def shifted(x, k):
    return lax.ppermute(x, "col", [(i, (i + k) % NB) for i in range(NB)])


def ring_round(behind, ahead):
    return shifted(behind, 1), shifted(ahead, -1)


def block_at(col, i):
    return lax.rem(col + NB - ORDER[i], NB)


def tables_body(where_ref, owner_ref, slot_ref, near_ref, live_ref, place_ref, home_ref, count_ref):
    me, col = where_ref[0], where_ref[1]
    owner = owner_ref[...]
    lane = lax.broadcasted_iota(jnp.int32, owner.shape, 1)
    row = lax.rem(lane, NB)
    rank = jnp.zeros_like(owner)
    for d in range(1, NB):
        earlier = pltpu.roll(owner, d, 1)
        for j in range(DEG):
            same = (owner == earlier[j : j + 1, :]) & (row >= d)
            rank += same.astype(jnp.int32)
    place_ref[...] = owner * CAP + rank
    wanted = jnp.zeros_like(owner)
    for i in range(NB):
        wanted += jnp.where(slot_ref[...] == block_at(col, i), i, 0)
    for c in range(CAP):
        asked = jnp.where((owner == me) & (rank == c), wanted, NB)
        least = asked[0:1, :]
        for j in range(1, DEG):
            least = jnp.minimum(least, asked[j : j + 1, :])
        for d in (1, 2, 4):
            least = jnp.minimum(least, pltpu.roll(least, d, 1))
        home_ref[c : c + 1, :] = least
    near, live = near_ref[...], live_ref[...]
    own = lax.broadcasted_iota(jnp.int32, (NB, 1), 0)
    for i in range(NB):
        block = block_at(col, i)
        hits = ((near == block) & (live != 0)).astype(F32)
        count = jnp.sum(hits, axis=1, keepdims=True) + (own == block).astype(F32)
        count_ref[:, rows_at(i)] = jnp.broadcast_to(count, (NB, BLK))


def asked(home_ref, s):
    return home_ref[s % CAP, (s // CAP) * NB + NB - 1]


def normed(x_low, gain):
    x = x_low.astype(F32)
    inv = lax.rsqrt(jnp.mean(x * x, axis=1, keepdims=True) + EPS)
    return (x * inv * gain).astype(BF16)


def project(x_low, gain, wide):
    proj = dot_nt(normed(x_low, gain), wide).astype(BF16)
    return proj[:, :BLK] * jnp.asarray(SCALE, BF16), proj[:, BLK:]


def wide_weight(weight):
    return jnp.concatenate([weight[:HD], jnp.zeros((HD, D), BF16), weight[HD:]], axis=0)


def project_most_body(send_ref, *refs):
    chunk_ins, refs = refs[: NB - 1], refs[NB - 1 :]
    gain_in, weight_in, query_out, kv_out, sent_out, *refs = refs
    chunk_ref, gain_ref, weight_ref, hidden_ref, query_ref, kv_ref, sent_ref, *refs = refs
    in_sems, out_sems, sent_sems = refs
    loads = copies(
        [weight_in, gain_in, *chunk_ins],
        [weight_ref, gain_ref, *(chunk_ref.at[i] for i in range(NB - 1))],
        in_sems,
    )
    start_all(loads)
    wait_all(loads[:2])
    gain = gain_ref[...]
    wide = wide_weight(weight_ref[...])
    for i in range(NB - 1):
        loads[2 + i].wait()
        hidden_ref[rows_at(i), :] = normed(chunk_ref[i], gain)
    proj = dot_nt(hidden_ref[...], wide).astype(BF16)
    for i in range(NB - 1):
        query_ref[i] = proj[rows_at(i), :BLK] * jnp.asarray(SCALE, BF16)
        kv_ref[i] = proj[rows_at(i), BLK:]
    most = pl.ds(0, NB - 1)
    parts = sent_sems.shape[0]
    step = sent_ref.shape[0] // parts
    sends = copies(
        [sent_ref.at[pl.ds(i * step, step)] for i in range(parts)],
        [sent_out.at[pl.ds(i * step, step)] for i in range(parts)],
        sent_sems,
    )
    stores = copies([query_ref, kv_ref], [query_out.at[most], kv_out.at[most]], out_sems)
    start_all(stores)
    for i in range(parts):

        def fill(s, _):
            sent_ref[i * step + s] = kv_ref[jnp.minimum(asked(send_ref, i * step + s), NB - 2)]
            return 0

        lax.fori_loop(0, step, fill, 0, unroll=True)
        sends[i].start()
    wait_all(stores)
    wait_all(sends)


def project_last_body(send_ref, chunk_in, gain_in, weight_in, query_in, kv_in, sent_in, *refs):
    query_out, kv_out, sent_out, *refs = refs
    chunk_ref, gain_ref, weight_ref, query_ref, kv_ref, in_sems, out_sems, sent_sems = refs
    loads = copies([chunk_in, gain_in, weight_in], [chunk_ref, gain_ref, weight_ref], in_sems)
    start_all(loads)
    wait_all(loads)
    query_ref[...], kv_ref[...] = project(chunk_ref[...], gain_ref[...], wide_weight(weight_ref[...]))

    def over_slots(act):
        for slot in range(sent_sems.shape[0]):

            @pl.when(asked(send_ref, slot) == NB - 1)
            def _():
                act(pltpu.make_async_copy(kv_ref, sent_out.at[slot], sent_sems.at[slot]))

    over_slots(lambda job: job.start())
    stores = copies([query_ref, kv_ref], [query_out.at[NB - 1], kv_out.at[NB - 1]], out_sems)
    start_all(stores)
    over_slots(lambda job: job.wait())
    wait_all(stores)


def attn_grad_body(*refs):
    n = NB - 1
    chunk_ins, refs = refs[:n], refs[n:]
    weight_in, ag_out, chunk_ref, weight_ref, ag_ref, sems, out_sems = refs
    loads = copies([weight_in, *chunk_ins], [weight_ref, *(chunk_ref.at[i] for i in range(n))], sems)
    start_all(loads)
    wait_all(loads)
    wide = jnp.concatenate([jnp.zeros((HD, D), BF16), weight_ref[...]], axis=0)
    ag_ref[...] = dot_nt(chunk_ref[...].reshape(n * BLK, D), wide).reshape(n, BLK, BLK)
    store = pltpu.make_async_copy(ag_ref, ag_out.at[pl.ds(0, n)], out_sems.at[0])
    store.start()
    store.wait()


def attn_grad_last_body(chunk_in, weight_in, ag_in, ag_out, chunk_ref, weight_ref, ag_ref, sems, out_sems):
    loads = copies([chunk_in, weight_in], [chunk_ref, weight_ref], sems)
    start_all(loads)
    wait_all(loads)
    wide = jnp.concatenate([jnp.zeros((HD, D), BF16), weight_ref[...]], axis=0)
    ag_ref[...] = dot_nt(chunk_ref[...], wide)
    store = pltpu.make_async_copy(ag_ref, ag_out.at[NB - 1], out_sems.at[0])
    store.start()
    store.wait()


def near_forward_body(col_ref, query_in, kv_in, count_in, num_out, *refs):
    query_ref, kv_ref, count_ref, num_ref, ones_ref, in_sems, out_sems = refs
    loads = copies([kv_in, query_in, count_in], [kv_ref, query_ref, count_ref], in_sems)
    start_all(loads)
    wait_all(loads)
    kv = kv_ref[...].reshape(ROWS, BLK)
    ones_ref[...] = jnp.where(lanes_low(kv.shape), jnp.asarray(1, BF16), kv)
    stores = copies([num_ref.at[i] for i in range(NB)], [num_out.at[i] for i in range(NB)], out_sems)
    for i in range(NB):
        score = dot_nt(query_ref[i], kv_ref[...].reshape(ROWS, BLK))
        prob = jnp.exp(score) * count_ref[pl.ds(block_at(col_ref[0], i), 1), :]
        num_ref[i] = dot(prob.astype(BF16), ones_ref[...])
        stores[i].start()
    wait_all(stores)


def far_body(where_ref, place_ref, query_in, far_in, num_in, ag_in, *refs):
    attn_out, scaled_out, extra_out, back_out, *refs = refs
    query_ref, far_ref, num_ref, ag_ref, *refs = refs
    attn_ref, scaled_ref, extra_ref, prob_ref, prob_low_ref, diff_ref, den_ref, both_ref, stage_ref, *refs = refs
    far_sems, in_sems, out_sems, extra_sems, back_sems = refs
    me, col = where_ref[0], where_ref[1]
    places = [place_ref[j, me * NB + block_at(col, i)] for i in range(NB) for j in range(DEG)]
    parts = far_sems.shape[0]
    step = far_in.shape[0] // parts
    fetches = copies(
        [far_in.at[pl.ds(i * step, step)] for i in range(parts)],
        [far_ref.at[pl.ds(i * step, step)] for i in range(parts)],
        far_sems,
    )
    loads = copies([query_in, ag_in, num_in], [query_ref, ag_ref, num_ref], in_sems)
    loads[0].start()
    start_all(fetches)
    start_all(loads[1:])

    def keys(i):
        return jnp.concatenate([far_ref[places[i * DEG + j]] for j in range(DEG)], axis=0)

    wait_all(loads[:1])
    wait_all(fetches)
    wait_all(loads[1:2])
    for i in range(NB):
        kv = keys(i)
        both = jnp.concatenate([query_ref[i], ag_ref[i].astype(BF16)], axis=0)
        score = dot_nt(both, kv)
        prob = jnp.exp(score[:BLK])
        prob_ref[i] = prob
        diff_ref[i] = score[BLK:]
        prob_low = prob.astype(BF16)
        prob_low_ref[i] = prob_low
        values = jnp.where(lanes_low(kv.shape), jnp.asarray(1, BF16), kv)
        extra_ref[i] = dot(prob_low, values)
    loads[2].wait()
    stores = copies([attn_ref, scaled_ref], [attn_out, scaled_out], out_sems)
    for i in range(NB):
        num = num_ref[i] + extra_ref[i]
        den = jnp.where(lanes_low(num.shape), num, pltpu.roll(num, HD, 1))
        inv = 1.0 / den
        attn = num * inv
        grad = ag_ref[i]
        scaled = (grad * inv).astype(BF16)
        scaled_ref[i] = scaled
        den_ref[i] = inv
        extra_ref[i] = jnp.sum(grad * attn, axis=1, keepdims=True) * inv
        attn_ref[:, rows_at(i)] = attn.T[HD:].astype(BF16)
        both_ref[i] = (query_ref[i] + scaled).astype(F32).T.astype(BF16)
    start_all(stores)
    jobs = []
    for i in range(NB):
        kv = keys(i)
        corr = extra_ref[i]
        diff = diff_ref[i] * den_ref[i, :, :1] - corr[:, :1]
        score_grad = (prob_ref[i] * diff).astype(BF16)
        extra_ref[i] = jnp.where(lanes_low(corr.shape), dot(score_grad, kv), corr)
        key_grad = dot(both_ref[i, :HD], score_grad).astype(BF16)
        value_grad = dot(both_ref[i, HD:], prob_low_ref[i]).astype(BF16)
        for j in range(DEG):
            e = i * DEG + j
            stage_ref[e, :HD, :] = key_grad[:, rows_at(j)]
            stage_ref[e, HD:, :] = value_grad[:, rows_at(j)]
            jobs.append(pltpu.make_async_copy(stage_ref.at[e], back_out.at[places[e]], back_sems.at[e]))
            jobs[-1].start()
        jobs.append(pltpu.make_async_copy(extra_ref.at[i], extra_out.at[i], extra_sems.at[i]))
        jobs[-1].start()
    wait_all(stores)
    wait_all(jobs)


def near_backward_body(col_ref, *refs):
    grad_ins, state_ins, refs = refs[:NB], refs[NB : 2 * NB], refs[2 * NB :]
    gain_in, query_in, kv_in, count_in, scaled_in, extra_in, attn_in, *refs = refs
    query_grad_out, near_out, part_out, hidden_out, *refs = refs
    grad_ref, state_ref, gain_ref, query_ref, kv_ref, count_ref, scaled_ref, extra_ref, attn_ref, hidden_ref, *refs = refs
    query_grad_ref, near_ref, part_ref, acc_ref, in_sems, late_sems, out_sems = refs
    loads = copies(
        [kv_in, query_in, count_in, scaled_in, extra_in],
        [kv_ref, query_ref, count_ref, scaled_ref, extra_ref],
        in_sems,
    )
    late = copies(
        [gain_in, *state_ins, attn_in, *grad_ins],
        [
            gain_ref,
            *(state_ref.at[i] for i in range(NB)),
            attn_ref,
            *(grad_ref.at[i] for i in range(NB)),
        ],
        late_sems,
    )
    start_all(loads)
    start_all(late)
    wait_all(loads)
    acc_ref[...] = jnp.zeros_like(acc_ref)
    col = col_ref[0]
    for i in range(NB):
        query, scaled, extra = query_ref[i], scaled_ref[i], extra_ref[i]
        kv = kv_ref[...].reshape(ROWS, BLK)
        prob = jnp.exp(dot_nt(query, kv)) * count_ref[pl.ds(block_at(col, i), 1), :]
        diff = dot_nt(scaled, kv) - extra[:, HD : HD + 1]
        score_grad = (prob * diff).astype(BF16)
        query_grad = dot(score_grad, kv) + extra
        query_grad_ref[:, rows_at(i)] = (query_grad.T[:HD] * SCALE).astype(BF16)
        both = (query + scaled).astype(F32).T.astype(BF16)
        acc_ref[:HD, :] += dot(both[:HD], score_grad)
        acc_ref[HD:, :] += dot(both[HD:], prob.astype(BF16))
    for i in range(NB):
        near_ref[i] = acc_ref[:, rows_at(i)]
    stores = copies(
        [query_grad_ref, near_ref, hidden_ref, part_ref],
        [query_grad_out, near_out, hidden_out, part_out],
        out_sems,
    )
    start_all(stores[:2])
    wait_all(late)
    gain = gain_ref[...]
    for i in range(NB):
        hidden_ref[i] = normed(state_ref[i], gain)
    stores[2].start()
    part_ref[:HD, :] = dot(query_grad_ref[...], hidden_ref[...].reshape(ROWS, D)).astype(BF16)
    part_ref[HD:, :] = dot(attn_ref[...], grad_ref[...].reshape(ROWS, D)).astype(BF16)
    stores[3].start()
    wait_all(stores)


def gather_grads_body(home_ref, returned_in, near_in, query_grad_in, attn_in, hidden_in, early_in, *refs):
    piece_refs, refs = refs[:NB], refs[NB:]
    part_out, returned_ref, near_ref, even_ref, odd_ref, proj_ref, hidden_ref, part_ref, *refs = refs
    far_sems, in_sems, out_sems = refs
    parts = far_sems.shape[0]
    step = returned_in.shape[0] // parts
    fetches = copies(
        [returned_in.at[pl.ds(i * step, step)] for i in range(parts)],
        [returned_ref.at[pl.ds(i * step, step)] for i in range(parts)],
        far_sems,
    )
    loads = copies(
        [
            near_in,
            hidden_in,
            query_grad_in,
            attn_in,
            early_in.at[pl.ds(0, HD)],
            early_in.at[pl.ds(HD, HD)],
        ],
        [
            near_ref,
            hidden_ref,
            proj_ref.at[pl.ds(0, HD)],
            proj_ref.at[pl.ds(3 * HD, HD)],
            part_ref.at[pl.ds(0, HD)],
            part_ref.at[pl.ds(3 * HD, HD)],
        ],
        in_sems,
    )
    start_all(fetches)
    start_all(loads)
    even_ref[...] = jnp.zeros_like(even_ref)
    odd_ref[...] = jnp.zeros_like(odd_ref)
    for i in range(parts):
        fetches[i].wait()

        def add(s, _):
            at = i * step + 2 * s
            even, odd = asked(home_ref, at), asked(home_ref, at + 1)
            even_ref[even] += returned_ref[at].astype(F32)
            odd_ref[odd] += returned_ref[at + 1].astype(F32)
            return 0

        lax.fori_loop(0, step // 2, add, 0, unroll=True)
    wait_all(loads)
    for i in range(NB):
        proj_ref[HD : 3 * HD, rows_at(i)] = (near_ref[i] + (even_ref[i] + odd_ref[i])).astype(BF16)
    at = [ORDER.index((NB - k) % NB) for k in range(NB)]
    stores = copies(
        [part_ref, *(proj_ref.at[:, pl.ds(at[k] * BLK, BLK)] for k in range(NB))],
        [part_out, *piece_refs],
        out_sems,
    )
    start_all(stores[1:])
    hidden = hidden_ref[...].reshape(ROWS, D)
    part_ref[HD : 3 * HD, :] = dot(proj_ref[HD : 3 * HD, :], hidden).astype(BF16)
    stores[0].start()
    wait_all(stores)


def sum_body(share_ref, total_ref):
    total = jnp.sum(share_ref[...].astype(F32), axis=0).astype(BF16)
    total_ref[...] = jnp.broadcast_to(total[None], total_ref.shape)


def add_heads(piece_ins, weight_ins, piece_ref, weight_ref, piece_sems, weight_sems):
    n = len(piece_ins)
    pieces = copies(piece_ins, [piece_ref.at[k] for k in range(n)], piece_sems)
    weights = copies(weight_ins, [weight_ref.at[k] for k in range(n)], weight_sems)
    for k in range(n):
        pieces[k].start()
        weights[k].start()
    out = jnp.zeros((BLK, D), F32)
    back = jnp.zeros((BLK, D), F32)
    for k in range(n):
        pieces[k].wait()
        terms = piece_ref[k].astype(F32).T.astype(BF16)
        weights[k].wait()
        back += dot(terms[:, : 3 * HD], weight_ref[k, : 3 * HD, :])
        out += dot(terms[:, 3 * HD :], weight_ref[k, 3 * HD :, :])
    return out, back


def first_heads_body(n, *refs):
    piece_ins, weight_ins, (sum_out, piece_ref, weight_ref, sum_ref, *sems, out_sem) = (
        refs[:n],
        refs[n : 2 * n],
        refs[2 * n :],
    )
    sum_ref[0], sum_ref[1] = add_heads(piece_ins, weight_ins, piece_ref, weight_ref, *sems)
    store = pltpu.make_async_copy(sum_ref, sum_out, out_sem.at[0])
    store.start()
    store.wait()


def finish_body(inv_root, n, *refs):
    piece_ins, weight_ins, refs = refs[:n], refs[n : 2 * n], refs[2 * n :]
    sum_in, state_in, grad_in, gain_in, total_in, layer_out, back_out, qkv_out, weight_out, *refs = refs
    piece_ref, weight_ref, sum_ref, state_ref, grad_ref, gain_ref, total_ref, layer_ref, back_ref, scaled_ref, *refs = refs
    piece_sems, weight_sems, in_sems, out_sems = refs
    loads = copies(
        [total_in, sum_in, state_in, grad_in, gain_in],
        [total_ref, sum_ref, state_ref, grad_ref, gain_ref],
        in_sems,
    )
    stores = copies(
        [scaled_ref.at[pl.ds(0, 3 * HD)], scaled_ref.at[pl.ds(3 * HD, HD)], layer_ref, back_ref],
        [qkv_out, weight_out, layer_out, back_out],
        out_sems,
    )
    start_all(loads)
    out, back = add_heads(piece_ins, weight_ins, piece_ref, weight_ref, piece_sems, weight_sems)
    loads[0].wait()
    scaled_ref[...] = total_ref[...].astype(F32) * inv_root
    start_all(stores[:2])
    wait_all(loads[1:])
    out += sum_ref[0]
    back += sum_ref[1]
    state = state_ref[...].astype(F32)
    gain = gain_ref[...]
    layer_ref[...] = (state + out).astype(BF16)
    stores[2].start()
    inv = lax.rsqrt(jnp.mean(state * state, axis=1, keepdims=True) + EPS)
    stat = jnp.sum(gain * back * state, axis=1, keepdims=True)
    back_ref[...] = (
        grad_ref[...].astype(F32) + inv * gain * back - state * (inv * inv * inv * stat / D)
    ).astype(BF16)
    stores[3].start()
    wait_all(stores)


def shards(
    node_states,
    norm_gain,
    qkv_weight,
    out_weight,
    local_slots,
    local_live,
    far_owner,
    far_slot,
    out_grad,
):
    doms = lax.axis_size("dom")
    me = lax.axis_index("dom")
    col_index = lax.axis_index("col").astype(jnp.int32)
    col = col_index.reshape(1)
    slots = doms * CAP
    entries = NB * DEG
    gain = norm_gain[None]

    where = jnp.stack([me.astype(jnp.int32), col_index])
    names = shaped(*far_owner.shape[::-1], kind=jnp.int32)
    places, home, count = call(
        tables_body,
        (names, shaped(CAP, far_owner.shape[0], kind=jnp.int32), shaped(NB, ROWS, kind=F32)),
        [scalars()] + [whole()] * 4,
        out_specs=[whole()] * 3,
        name="tables",
    )(where, far_owner.T, far_slot.T, local_slots, local_live)

    unit = 2 * ROWS * ROWS * BLK
    node = shaped(BLK, D)
    across = shaped(HD, ROWS)
    block, blocks, blocks_float = shaped(BLK, BLK), shaped(NB, BLK, BLK), shaped(NB, BLK, BLK, kind=F32)
    blocks_most = shaped(NB - 1, BLK, BLK)
    wide, wide_float = shaped(NB, BLK, DEG * BLK), shaped(NB, BLK, DEG * BLK, kind=F32)
    exchanged = shaped(slots, BLK, BLK)
    row = shaped(1, D, kind=F32)
    counts = shaped(NB, ROWS, kind=F32)
    states, states_most = shaped(NB, BLK, D), shaped(NB - 1, BLK, D)
    piece = shaped(4 * HD, BLK)
    head_weight, out_piece = shaped(3 * HD, D), shaped(HD, D)

    x1, x7 = ring_round(node_states, node_states)
    x1, x7, home, places, count = lax.optimization_barrier((x1, x7, home, places, count))
    x2, x6 = ring_round(x1, x7)
    x3, x5 = ring_round(x2, x6)
    x4 = shifted(x3, 1)
    state_chunks = (node_states, x1, x7, x2, x6, x3, x5, x4)
    projected = call(
        project_most_body,
        (blocks, blocks, exchanged),
        [scalars()] + [left()] * (NB + 1),
        scratch=[
            *held(states_most, row, head_weight, shaped((NB - 1) * BLK, D), blocks_most, blocks_most, exchanged),
            dma_sems(NB + 1),
            dma_sems(2),
            dma_sems(4),
        ],
        flops=2 * ROWS * D * 256,
        name="project_most",
    )(home, node_states, x1, x7, x2, x6, x3, x5, gain, qkv_weight)
    query, kv, outgoing = call(
        project_last_body,
        (blocks, blocks, exchanged),
        [scalars()] + [left()] * 6,
        scratch=[
            *held(node, row, head_weight, block, block),
            dma_sems(3),
            dma_sems(2),
            dma_sems(slots),
        ],
        flops=2 * BLK * D * 256,
        name="project_last",
        aliases={4: 0, 5: 1, 6: 2},
    )(home, x4, gain, qkv_weight, *projected)

    outgoing, grad_own = lax.optimization_barrier((outgoing, out_grad))
    fetched = lax.all_to_all(outgoing, "dom", 0, 0, tiled=True)
    g1, g7 = ring_round(grad_own, grad_own)
    g2, g6 = ring_round(g1, g7)
    g3, g5 = ring_round(g2, g6)
    g4 = shifted(g3, 1)
    grad_chunks = (out_grad, g1, g7, g2, g6, g3, g5, g4)

    (attn_grad,) = call(
        attn_grad_body,
        (blocks_float,),
        [left()] * NB,
        scratch=[
            *held(states_most, out_piece, shaped(NB - 1, BLK, BLK, kind=F32)),
            dma_sems(NB),
            dma_sems(1),
        ],
        flops=2 * ROWS * D * BLK,
        name="attn_grad",
    )(*grad_chunks[:-1], out_weight)

    (near,) = call(
        near_forward_body,
        (blocks_float,),
        [scalars()] + [left()] * 3,
        scratch=[*held(blocks, blocks, counts, blocks_float, shaped(ROWS, BLK)), dma_sems(3), dma_sems(NB)],
        flops=2 * unit,
        name="near_forward",
    )(col, query, kv, count)

    (attn_grad,) = call(
        attn_grad_last_body,
        (blocks_float,),
        [left()] * 3,
        scratch=[*held(node, out_piece, shaped(BLK, BLK, kind=F32)), dma_sems(2), dma_sems(1)],
        flops=2 * BLK * D * BLK,
        name="attn_grad_last",
        aliases={2: 0},
    )(g4, out_weight, attn_grad)

    attn, scaled, extra, outgoing_back = call(
        far_body,
        (across, blocks, blocks_float, exchanged),
        [scalars()] * 2 + [left()] * 4,
        scratch=[
            *held(blocks, exchanged, blocks_float, blocks_float),
            *held(across, blocks, blocks_float, wide_float, wide, wide_float, blocks_float),
            *held(blocks, shaped(entries, BLK, BLK)),
            dma_sems(4),
            dma_sems(3),
            dma_sems(2),
            dma_sems(NB),
            dma_sems(entries),
        ],
        flops=2 * unit,
        name="far_both",
    )(where, places, query, fetched, near, attn_grad)

    outgoing_back, weights_own = lax.optimization_barrier(
        (outgoing_back, jnp.concatenate([qkv_weight, out_weight], axis=0))
    )
    returned = lax.all_to_all(outgoing_back, "dom", 0, 0, tiled=True)
    w1, w7 = ring_round(weights_own, weights_own)
    w2, w6 = ring_round(w1, w7)

    query_grad, near_grad, early, hidden = call(
        near_backward_body,
        (across, blocks_float, shaped(2 * HD, D), states),
        [scalars()] + [left()] * (2 * NB + 7),
        scratch=[
            *held(states, states, row, blocks, blocks, counts, blocks, blocks_float, across, states),
            *held(across, blocks_float, shaped(2 * HD, D), shaped(BLK, ROWS, kind=F32)),
            dma_sems(5),
            dma_sems(2 * NB + 2),
            dma_sems(4),
        ],
        flops=5 * unit,
        name="near_backward",
    )(col, *grad_chunks, *state_chunks, gain, query, kv, count, scaled, extra, attn)

    w2, w6, near_grad = lax.optimization_barrier((w2, w6, near_grad))
    w3, w5 = ring_round(w2, w6)
    returned, w3, w5 = lax.optimization_barrier((returned, w3, w5))
    w4 = shifted(w3, 1)

    *pieces, part = call(
        gather_grads_body,
        (piece,) * NB + (shaped(4 * HD, D),),
        [scalars()] + [left()] * 6,
        scratch=[
            *held(exchanged, blocks_float, shaped(NB + 1, BLK, BLK, kind=F32)),
            *held(shaped(NB + 1, BLK, BLK, kind=F32), shaped(4 * HD, ROWS), states, shaped(4 * HD, D)),
            dma_sems(4),
            dma_sems(6),
            dma_sems(1 + NB),
        ],
        flops=2 * ROWS * D * 128,
        name="gather_grads",
    )(home, returned, near_grad, query_grad, attn, hidden, early)

    share_rows = 4 * HD // doms
    shares = lax.all_to_all(part.reshape(doms, share_rows, D), "dom", 0, 0, tiled=True)
    arrived = [pieces[0], *(shifted(pieces[k], k) for k in range(1, NB))]

    (totals,) = call(
        sum_body,
        (shaped(doms, share_rows, D),),
        [whole()],
        out_specs=[whole()],
        name="sum_shares",
        limit=4,
    )(shares)
    total = lax.all_to_all(totals, "dom", 0, 0, tiled=True).reshape(4 * HD, D)
    weights = (weights_own, w1, w2, w3, w4, w5, w6, w7)
    cut = 5
    sums = shaped(2, BLK, D, kind=F32)
    (first,) = call(
        functools.partial(first_heads_body, cut),
        (sums,),
        [left()] * (2 * cut),
        scratch=[
            *held(shaped(cut, 4 * HD, BLK), shaped(cut, 4 * HD, D), sums),
            dma_sems(cut),
            dma_sems(cut),
            dma_sems(1),
        ],
        flops=2 * BLK * D * 256 * cut,
        name="first_heads",
    )(*arrived[:cut], *weights[:cut])
    rest = NB - cut
    total_shape, total_float = shaped(4 * HD, D), shaped(4 * HD, D, kind=F32)
    layer_out, state_grad, qkv_grad, out_weight_grad = call(
        functools.partial(finish_body, 1.0 / math.sqrt(far_owner.shape[0] * BLK), rest),
        (node, node, shaped(3 * HD, D, kind=F32), shaped(HD, D, kind=F32)),
        [left()] * (2 * rest + 5),
        scratch=[
            *held(shaped(rest, 4 * HD, BLK), shaped(rest, 4 * HD, D), sums, node, node, row, total_shape),
            *held(node, node, total_float),
            dma_sems(rest),
            dma_sems(rest),
            dma_sems(5),
            dma_sems(4),
        ],
        flops=2 * BLK * D * 256 * rest,
        name="finish",
    )(*arrived[cut:], *weights[cut:], first, node_states, out_grad, gain, total)

    return (layer_out, state_grad, qkv_grad, out_weight_grad)


def solution(mesh):
    placed = (
        P(("dom", "col"), None),
        P(),
        P("col", None),
        P("col", None),
        P("dom", None),
        P("dom", None),
        P(),
        P(),
        P(("dom", "col"), None),
    )
    return jax.shard_map(
        shards,
        mesh=mesh,
        in_specs=placed,
        out_specs=(
            P(("dom", "col"), None),
            P(("dom", "col"), None),
            P("col", None),
            P("col", None),
        ),
        check_vma=False,
    )
```

time: 226 us -> 167 us (0.74)
  blocking collectives: 60.9 us -> 0 us
  starting transfers between devices: 28.1 us -> 75 us
  waiting for transfers between devices: 78.7 us -> 42.6 us
  Pallas kernels: 19.6 us -> 42.9 us
  local copies, waits for them, and re-layouts: 21.3 us -> 2.61 us
  between operations: 14.3 us -> 1.09 us
    ppermute x0 -> x28, starting transfers between devices: none -> 46.5 us  [shifted(): return lax.ppermute(x, 'col', [(i, (i + k) % NB) for i in range(NB)])]
    ppermute x0 -> x28, waiting for transfers between devices: none -> 35.6 us  [shifted(): return lax.ppermute(x, 'col', [(i, (i + k) % NB) for i in range(NB)])]
    all_gather x1 -> x0, blocking collectives: 34.7 us -> none  [shards(): out_weight_whole = lax.all_gather(out_weight, 'col', axis=0)]
    all_gather x2 -> x0, waiting for transfers between devices: 33.8 us -> none  [the longest x1 33.8 us: shards(): grad_whole = lax.all_gather(out_grad, 'col', axis=0)]
    all_to_all x2 -> x0, blocking collectives: 26.2 us -> none  [the longest x1 13.6 us: shards(): lax.all_to_all(part.reshape(doms, share_rows, D), 'dom', 0, 0, tiled=True)]
    pallas_call x7 -> x12, Pallas kernels: 19.6 us -> 42.9 us  [the longest x1 7.54 us: shards(): call(far_body, (across, blocks, blocks_float, exchanged), [scalars()] * 2...]
    all_to_all x2, waiting for transfers between devices: 27.1 us -> 7.02 us  [the longest x1 7.02 us: shards(): lax.all_to_all(part.reshape(doms, share_rows, D), 'dom', 0, 0, tiled=True)]
    all_to_all x1, waiting for transfers between devices: 16.5 us -> 0.01 us  [shards(): returned = lax.all_to_all(outgoing_back, 'dom', 0, 0, tiled=True)]
  transfers between devices with their start and end apart: 6 -> 32, of which waited for: 3 -> 13; matrix products, arithmetic and copies ran while one was open for 1% -> 1% of each run, Pallas kernels for 4% -> 15%
where the time goes in v3:
time: 167 us; the launch traced here: 166 us
  starting transfers between devices  75 us (45%)
  Pallas kernels  42.9 us (26%)
  waiting for transfers between devices  42.6 us (26%)
  local copies, waits for them, and re-layouts  2.61 us (2%)
    ppermute x28, starting transfers between devices, shifted(): return lax.ppermute(x, 'col', [(i, (i + k) % NB) for i in range(NB)])  46.5 us
    ppermute x28, waiting for transfers between devices, shifted(): return lax.ppermute(x, 'col', [(i, (i + k) % NB) for i in range(NB)])  35.6 us
    all_to_all x1, starting transfers between devices, shards(): fetched = lax.all_to_all(outgoing, 'dom', 0, 0, tiled=True)  7.82 us
    all_to_all x1, starting transfers between devices, shards(): returned = lax.all_to_all(outgoing_back, 'dom', 0, 0, tiled=True)  7.57 us
    pallas_call x1, Pallas kernels, shards(): call(far_body, (across, blocks, blocks_float, exchanged), [scalars()] * 2...  7.54 us
    all_to_all x1, starting transfers between devices, shards(): lax.all_to_all(part.reshape(doms, share_rows, D), 'dom', 0, 0, tiled=True)  7.4 us
    pallas_call x1, Pallas kernels, shards(): call(near_backward_body, (across, blocks_float, shaped(2 * HD, D), states...  7.19 us
    all_to_all x1, waiting for transfers between devices, shards(): lax.all_to_all(part.reshape(doms, share_rows, D), 'dom', 0, 0, tiled=True)  7.02 us
  transfers between devices with their start and end apart: 32, of which 13 were waited for; matrix products, arithmetic and copies ran while one was open for 1% of the time, Pallas kernels for 15%

profile of v3, /device:TPU:2, one launch (start us, length us, event | category | flops | bytes accessed | tf_op | source)
XLA Modules:
  0.0 165.6 jit_solution(9774832144473795920)
XLA Ops:
  2.6 4.0 %collective-permute-start.1 = (bf16[128,512]{1,0:T(8,128)(2,1)}, bf16[128,512]{1,0:T(8,128)(2,1)}, u32[]{:S(2)}, u32[]{:S(2)}) collective-permute-start(bf16[128,512]{1,0:T(8,128)(2,1)} %refs_7_.3), channel_id=1, source_target_pairs={{0,7},{1,0},{2,1},{3,2},{4,3},{5,4},{6,5},{7,6},{8,15},{9,8},{10,9... | collective-permute-start | bytes 393224 | tf_op jit(solution)/shard_map/ppermute | solution.py:102
  10.4 3.2 %collective-permute-start.5 = (bf16[128,512]{1,0:T(8,128)(2,1)}, bf16[128,512]{1,0:T(8,128)(2,1)S(1)}, u32[]{:S(2)}, u32[]{:S(2)}) collective-permute-start(bf16[128,512]{1,0:T(8,128)(2,1)} %collective-permute-done.1.refs_2_.refs_10_), channel_id=1, source_target_pairs={{0,7},{1,0},{2,1},{3,2},{4,3},{5,4},{6,5},{7,6},{8,15},{9,8},{10,9... | collective-permute-start | bytes 393224 | tf_op jit(solution)/shard_map/ppermute | solution.py:102
  13.6 3.2 %collective-permute-done.2.refs_3_.refs_11_ = bf16[128,512]{1,0:T(8,128)(2,1)S(1)} collective-permute-done((bf16[128,512]{1,0:T(8,128)(2,1)}, bf16[128,512]{1,0:T(8,128)(2,1)S(1)}, u32[]{:S(2)}, u32[]{:S(2)}) %collective-permute-start.2) | collective-permute-done | bytes 131104 | tf_op jit(solution)/shard_map/ppermute | solution.py:102
  17.4 3.2 %collective-permute-start.6 = (bf16[128,512]{1,0:T(8,128)(2,1)S(1)}, bf16[128,512]{1,0:T(8,128)(2,1)S(1)}, u32[]{:S(2)}, u32[]{:S(2)}) collective-permute-start(bf16[128,512]{1,0:T(8,128)(2,1)S(1)} %collective-permute-done.5.refs_4_.refs_12_), channel_id=1, source_target_pairs={{0,7},{1,0},{2,1},{3,2},{4,3},{5,4},{6,5},{7,6},{8,15},{9,8},{10,9... | collective-permute-start | bytes 393224 | tf_op jit(solution)/shard_map/ppermute | solution.py:102
  20.7 3.0 %collective-permute-done.3.refs_5_.refs_13_ = bf16[128,512]{1,0:T(8,128)(2,1)} collective-permute-done((bf16[128,512]{1,0:T(8,128)(2,1)S(1)}, bf16[128,512]{1,0:T(8,128)(2,1)}, u32[]{:S(2)}, u32[]{:S(2)}) %collective-permute-start.3) | collective-permute-done | bytes 131104 | tf_op jit(solution)/shard_map/ppermute | solution.py:102
  24.4 4.5 %project_most.1 = (bf16[8,128,128]{2,1,0:T(8,128)(2,1)}, bf16[8,128,128]{2,1,0:T(8,128)(2,1)}, bf16[64,128,128]{2,1,0:T(8,128)(2,1)}) custom-call(s32[2,256]{1,0:T(2,128)} %get-tuple-element.48.send_ref.home_ref, bf16[128,512]{1,0:T(8,128)(2,1)} %refs_7_.3, bf16[128,512]{1,0:T(8,128)(2,1)} %collective-permute-done.refs_1_.refs_9_, ...), custom_call_target="tpu_custom_call" | custom-call | flops 268435456 | bytes 1048576 | tf_op jit(solution)/shard_map/project_most/pallas_call | solution.py:578
  30.2 3.2 %project_last.1 = (bf16[8,128,128]{2,1,0:T(8,128)(2,1)}, bf16[8,128,128]{2,1,0:T(8,128)(2,1)}, bf16[64,128,128]{2,1,0:T(8,128)(2,1)}) custom-call(s32[2,256]{1,0:T(2,128)} %get-tuple-element.48.send_ref.home_ref, bf16[128,512]{1,0:T(8,128)(2,1)} %collective-permute-done.4.chunk_in.refs_15_, ...), custom_call_target="tpu_custom_call", output_to_operand_aliasing={{0}: (4, {}), {1}: (5, {}), {2}: (6, {})} | custom-call | flops 33554432 | bytes 1048576 | tf_op jit(solution)/shard_map/project_last/pallas_call | solution.py:591
  33.5 7.8 %all-to-all-start = ((bf16[64,128,128]{2,1,0:T(8,128)(2,1)}), bf16[64,128,128]{2,1,0:T(8,128)(2,1)}, u32[]{:S(2)}, u32[]{:S(2)}) async-start(bf16[64,128,128]{2,1,0:T(8,128)(2,1)} %get-tuple-element.57), calls=%async_computation | async-start | bytes 4194304 | tf_op jit(solution)/shard_map/all_to_all | solution.py:607
  41.9 2.8 %collective-permute-start.11 = (bf16[128,512]{1,0:T(8,128)(2,1)S(1)}, bf16[128,512]{1,0:T(8,128)(2,1)S(1)}, u32[]{:S(2)}, u32[]{:S(2)}) collective-permute-start(bf16[128,512]{1,0:T(8,128)(2,1)S(1)} %copy-done.3), channel_id=1, source_target_pairs={{0,7},{1,0},{2,1},{3,2},{4,3},{5,4},{6,5},{7,6},{8,15},{9,8},{10,9... | collective-permute-start | bytes 393224 | tf_op jit(solution)/shard_map/ppermute | solution.py:102
  44.7 3.5 %collective-permute-done.7.refs_1_ = bf16[128,512]{1,0:T(8,128)(2,1)S(1)} collective-permute-done((bf16[128,512]{1,0:T(8,128)(2,1)S(1)}, bf16[128,512]{1,0:T(8,128)(2,1)S(1)}, u32[]{:S(2)}, u32[]{:S(2)}) %collective-permute-start.7) | collective-permute-done | bytes 131104 | tf_op jit(solution)/shard_map/ppermute | solution.py:102
  51.5 2.9 %collective-permute-done.8.refs_3_ = bf16[128,512]{1,0:T(8,128)(2,1)S(1)} collective-permute-done((bf16[128,512]{1,0:T(8,128)(2,1)S(1)}, bf16[128,512]{1,0:T(8,128)(2,1)S(1)}, u32[]{:S(2)}, u32[]{:S(2)}) %collective-permute-start.8) | collective-permute-done | bytes 131104 | tf_op jit(solution)/shard_map/ppermute | solution.py:102
  55.0 2.8 %collective-permute-start.13 = (bf16[128,512]{1,0:T(8,128)(2,1)}, bf16[128,512]{1,0:T(8,128)(2,1)}, u32[]{:S(2)}, u32[]{:S(2)}) collective-permute-start(bf16[128,512]{1,0:T(8,128)(2,1)} %collective-permute-done.12.refs_4_), channel_id=1, source_target_pairs={{0,7},{1,0},{2,1},{3,2},{4,3},{5,4},{6,5},{7,6},{8,15},{9,8},{10,9... | collective-permute-start | bytes 393224 | tf_op jit(solution)/shard_map/ppermute | solution.py:102
  57.8 2.9 %collective-permute-done.9.refs_5_ = bf16[128,512]{1,0:T(8,128)(2,1)} collective-permute-done((bf16[128,512]{1,0:T(8,128)(2,1)S(1)}, bf16[128,512]{1,0:T(8,128)(2,1)}, u32[]{:S(2)}, u32[]{:S(2)}) %collective-permute-start.9) | collective-permute-done | bytes 131104 | tf_op jit(solution)/shard_map/ppermute | solution.py:102
  61.4 3.7 %near_forward.1.num_in = f32[8,128,128]{2,1,0:T(8,128)} custom-call(s32[1]{0:T(128)} %bitcast.1.col_ref, bf16[8,128,128]{2,1,0:T(8,128)(2,1)} %get-tuple-element.55.query_in.refs_17_, bf16[8,128,128]{2,1,0:T(8,128)(2,1)} %get-tuple-element.58.kv_in.refs_18_, f32[8,1024]{1,0:T(8,128)} %get-tuple-element.59.count_in.refs_19_), custom_call_target="tpu_custom_call" | custom-call | flops 536870912 | bytes 1048576 | tf_op jit(solution)/shard_map/near_forward/pallas_call | solution.py:627
  69.4 7.5 %far_both.1 = (bf16[64,1024]{1,0:T(8,128)(2,1)}, bf16[8,128,128]{2,1,0:T(8,128)(2,1)}, f32[8,128,128]{2,1,0:T(8,128)}, bf16[64,128,128]{2,1,0:T(8,128)(2,1)}) custom-call(s32[2]{0:T(128)} %pad_add_fusion.where_ref, s32[4,256]{1,0:T(4,128)} %get-tuple-element.49.place_ref, bf16[8,128,128]{2,1,0:T(8,128)(2,1)} %get-tuple-element.55.query_in.refs_17_, ...), custom_call_target="tpu_custom_call" | custom-call | flops 536870912 | bytes 1048576 | tf_op jit(solution)/shard_map/far_both/pallas_call | solution.py:646
  77.0 7.6 %all-to-all-start.1 = ((bf16[64,128,128]{2,1,0:T(8,128)(2,1)}), bf16[64,128,128]{2,1,0:T(8,128)(2,1)}, u32[]{:S(2)}, u32[]{:S(2)}) async-start(bf16[64,128,128]{2,1,0:T(8,128)(2,1)} %get-tuple-element.62), calls=%async_computation.1 | async-start | bytes 4194304 | tf_op jit(solution)/shard_map/all_to_all | solution.py:667
  84.6 3.3 %collective-permute-start.16 = (bf16[256,512]{1,0:T(8,128)(2,1)S(1)}, bf16[256,512]{1,0:T(8,128)(2,1)}, u32[]{:S(2)}, u32[]{:S(2)}) collective-permute-start(bf16[256,512]{1,0:T(8,128)(2,1)S(1)} %copy-done.1), channel_id=1, source_target_pairs={{0,7},{1,0},{2,1},{3,2},{4,3},{5,4},{6,5},{7,6},{8,15},{9,8},{10,9... | collective-permute-start | bytes 786440 | tf_op jit(solution)/shard_map/ppermute | solution.py:102
  87.9 6.6 %collective-permute-done.14.refs_6_ = bf16[256,512]{1,0:T(8,128)(2,1)} collective-permute-done((bf16[256,512]{1,0:T(8,128)(2,1)S(1)}, bf16[256,512]{1,0:T(8,128)(2,1)}, u32[]{:S(2)}, u32[]{:S(2)}) %collective-permute-start.14) | collective-permute-done | bytes 262176 | tf_op jit(solution)/shard_map/ppermute | solution.py:102
  94.6 3.2 %collective-permute-start.17 = (bf16[256,512]{1,0:T(8,128)(2,1)}, bf16[256,512]{1,0:T(8,128)(2,1)}, u32[]{:S(2)}, u32[]{:S(2)}) collective-permute-start(bf16[256,512]{1,0:T(8,128)(2,1)} %collective-permute-done.16.refs_5_), channel_id=1, source_target_pairs={{0,7},{1,0},{2,1},{3,2},{4,3},{5,4},{6,5},{7,6},{8,15},{9,8},{10,9... | collective-permute-start | bytes 786440 | tf_op jit(solution)/shard_map/ppermute | solution.py:102
  97.8 7.2 %near_backward.1 = (bf16[64,1024]{1,0:T(8,128)(2,1)}, f32[8,128,128]{2,1,0:T(8,128)}, bf16[128,512]{1,0:T(8,128)(2,1)}, bf16[8,128,512]{2,1,0:T(8,128)(2,1)}) custom-call(s32[1]{0:T(128)} %bitcast.1.col_ref, bf16[128,512]{1,0:T(8,128)(2,1)} %refs_8_.5, bf16[128,512]{1,0:T(8,128)(2,1)} %copy-done.7, bf16[128,512]{1,0:T(8,128)(2,1)} %copy-done.8, ...), custom_call_target="tpu_custom_call" | custom-call | flops 1342177280 | bytes 1048576 | tf_op jit(solution)/shard_map/near_backward/pallas_call | solution.py:671
  105.1 3.2 %collective-permute-start.19 = (bf16[256,512]{1,0:T(8,128)(2,1)}, bf16[256,512]{1,0:T(8,128)(2,1)}, u32[]{:S(2)}, u32[]{:S(2)}) collective-permute-start(bf16[256,512]{1,0:T(8,128)(2,1)} %collective-permute-done.17.refs_4_), channel_id=1, source_target_pairs={{0,7},{1,0},{2,1},{3,2},{4,3},{5,4},{6,5},{7,6},{8,15},{9,8},{10,9... | collective-permute-start | bytes 786440 | tf_op jit(solution)/shard_map/ppermute | solution.py:102
  108.3 5.6 %collective-permute-done.18.refs_8_ = bf16[256,512]{1,0:T(8,128)(2,1)} collective-permute-done((bf16[256,512]{1,0:T(8,128)(2,1)}, bf16[256,512]{1,0:T(8,128)(2,1)}, u32[]{:S(2)}, u32[]{:S(2)}) %collective-permute-start.18) | collective-permute-done | bytes 262176 | tf_op jit(solution)/shard_map/ppermute | solution.py:102
  113.9 4.1 %gather_grads.1 = (bf16[256,128]{1,0:T(8,128)(2,1)}, bf16[256,128]{1,0:T(8,128)(2,1)}, bf16[256,128]{1,0:T(8,128)(2,1)}, bf16[256,128]{1,0:T(8,128)(2,1)}, bf16[...) custom-call(s32[2,256]{1,0:T(2,128)} %get-tuple-element.48.send_ref., ...), custom_call_target="tpu_custom_call" | custom-call | flops 134217728 | bytes 1048576 | tf_op jit(solution)/shard_map/gather_grads/pallas_call | solution.py:691
  118.0 7.4 %all-to-all-start.2 = ((bf16[32,8,512]{2,1,0:T(8,128)(2,1)}), bf16[32,8,512]{2,1,0:T(8,128)(2,1)S(1)}, u32[]{:S(2)}, u32[]{:S(2)}) async-start(bf16[32,8,512]{2,1,0:T(8,128)(2,1)} %bitcast.7), calls=%async_computation.2 | async-start | bytes 524288 | tf_op jit(solution)/shard_map/all_to_all | solution.py:707
  126.2 7.0 %all-to-all-done.2.share_ref = bf16[32,8,512]{2,1,0:T(8,128)(2,1)S(1)} async-done(((bf16[32,8,512]{2,1,0:T(8,128)(2,1)}), bf16[32,8,512]{2,1,0:T(8,128)(2,1)S(1)}, u32[]{:S(2)}, u32[]{:S(2)}) %all-to-all-start.2) | async-done | bytes 262176 | tf_op jit(solution)/shard_map/all_to_all | solution.py:707
  133.9 5.7 %all-to-all-start.3 = ((bf16[32,8,512]{2,1,0:T(8,128)(2,1)}), bf16[32,8,512]{2,1,0:T(8,128)(2,1)}, u32[]{:S(2)}, u32[]{:S(2)}) async-start(bf16[32,8,512]{2,1,0:T(8,128)(2,1)} %sum_shares.1), calls=%async_computation.3 | async-start | bytes 524288 | tf_op jit(solution)/shard_map/all_to_all | solution.py:718
  140.3 4.5 %collective-permute-start.24 = (bf16[256,128]{1,0:T(8,128)(2,1)}, bf16[256,128]{1,0:T(8,128)(2,1)}, u32[]{:S(2)}, u32[]{:S(2)}) collective-permute-start(bf16[256,128]{1,0:T(8,128)(2,1)} %get-tuple-element.81), channel_id=1, source_target_pairs={{0,2},{1,3},{2,4},{3,5},{4,6},{5,7},{6,0},{7,1},{8,10},{9,11},{10,... | collective-permute-start | bytes 196616 | tf_op jit(solution)/shard_map/ppermute | solution.py:102
  144.8 3.5 %collective-permute-start.26 = (bf16[256,128]{1,0:T(8,128)(2,1)}, bf16[256,128]{1,0:T(8,128)(2,1)}, u32[]{:S(2)}, u32[]{:S(2)}) collective-permute-start(bf16[256,128]{1,0:T(8,128)(2,1)} %get-tuple-element.83), channel_id=1, source_target_pairs={{0,4},{1,5},{2,6},{3,7},{4,0},{5,1},{6,2},{7,3},{8,12},{9,13},{10,... | collective-permute-start | bytes 196616 | tf_op jit(solution)/shard_map/ppermute | solution.py:102
  148.4 3.1 %collective-permute-start.20 = (bf16[256,128]{1,0:T(8,128)(2,1)}, bf16[256,128]{1,0:T(8,128)(2,1)}, u32[]{:S(2)}, u32[]{:S(2)}) collective-permute-start(bf16[256,128]{1,0:T(8,128)(2,1)} %get-tuple-element.75), channel_id=1, source_target_pairs={{0,5},{1,6},{2,7},{3,0},{4,1},{5,2},{6,3},{7,4},{8,13},{9,14},{10,... | collective-permute-start | bytes 196616 | tf_op jit(solution)/shard_map/ppermute | solution.py:102
  151.5 2.8 %collective-permute-start.21 = (bf16[256,128]{1,0:T(8,128)(2,1)}, bf16[256,128]{1,0:T(8,128)(2,1)}, u32[]{:S(2)}, u32[]{:S(2)}) collective-permute-start(bf16[256,128]{1,0:T(8,128)(2,1)} %get-tuple-element.76), channel_id=1, source_target_pairs={{0,6},{1,7},{2,0},{3,1},{4,2},{5,3},{6,4},{7,5},{8,14},{9,15},{10,... | collective-permute-start | bytes 196616 | tf_op jit(solution)/shard_map/ppermute | solution.py:102
  155.5 3.0 %first_heads.1.refs_6_ = f32[2,128,512]{2,1,0:T(8,128)} custom-call(bf16[256,128]{1,0:T(8,128)(2,1)} %get-tuple-element.79.refs_0_, bf16[256,128]{1,0:T(8,128)(2,1)} %collective-permute-done.23.refs_1_, bf16[256,128]{1,0:T(8,128)(2,1)} %collective-permute-done.24.refs_2_, bf16[256,128]{1,0:T(8,128)(2,1)} %collective-permute-done.25.refs_3_, ...), custom_call_target="tpu_custom_call" | custom-call | flops 167772160 | bytes 1048576 | tf_op jit(solution)/shard_map/first_heads/pallas_call | solution.py:722
  162.5 2.9 %finish.1 = (bf16[128,512]{1,0:T(8,128)(2,1)}, bf16[128,512]{1,0:T(8,128)(2,1)}, f32[192,512]{1,0:T(8,128)}, f32[64,512]{1,0:T(8,128)}) custom-call(bf16[256,128]{1,0:T(8,128)(2,1)} %collective-permute-done.20.refs_0_, bf16[256,128]{1,0:T(8,128)(2,1)} %collective-permute-done.21.refs_1_, bf16[256,128]{1,0:T(8,128)(2,1)} %collective-permute-done.22.refs_2_, ...), custom_call_target="tpu_custom_call" | custom-call | flops 100663296 | bytes 1048576 | tf_op jit(solution)/shard_map/finish/pallas_call | solution.py:737
  (66 shorter events, 25.5 us)
Async XLA Ops:
  0.6 9.7 %collective-permute-start = (bf16[128,512]{1,0:T(8,128)(2,1)}, bf16[128,512]{1,0:T(8,128)(2,1)}, u32[]{:S(2)}, u32[]{:S(2)}) collective-permute-start(bf16[128,512]{1,0:T(8,128)(2,1)} %refs_7_.3), channel_id=1, source_target_pairs={{0,1},{1,2},{2,3},{3,4},{4,5},{5,6},{6,7},{7,0},{8,9},{9,10},{10,1... | collective-permute-start | bytes 393224 | tf_op jit(solution)/shard_map/ppermute | solution.py:102
  2.6 7.8 %collective-permute-start.1 = (bf16[128,512]{1,0:T(8,128)(2,1)}, bf16[128,512]{1,0:T(8,128)(2,1)}, u32[]{:S(2)}, u32[]{:S(2)}) collective-permute-start(bf16[128,512]{1,0:T(8,128)(2,1)} %refs_7_.3), channel_id=1, source_target_pairs={{0,7},{1,0},{2,1},{3,2},{4,3},{5,4},{6,5},{7,6},{8,15},{9,8},{10,9... | collective-permute-start | bytes 393224 | tf_op jit(solution)/shard_map/ppermute | solution.py:102
  10.4 6.4 %collective-permute-start.2 = (bf16[128,512]{1,0:T(8,128)(2,1)}, bf16[128,512]{1,0:T(8,128)(2,1)S(1)}, u32[]{:S(2)}, u32[]{:S(2)}) collective-permute-start(bf16[128,512]{1,0:T(8,128)(2,1)} %collective-permute-done.refs_1_.refs_9_), channel_id=1, source_target_pairs={{0,1},{1,2},{2,3},{3,4},{4,5},{5,6},{6,7},{7,0},{8,9},{9,10},{10,1... | collective-permute-start | bytes 393224 | tf_op jit(solution)/shard_map/ppermute | solution.py:102
  10.4 7.0 %collective-permute-start.5 = (bf16[128,512]{1,0:T(8,128)(2,1)}, bf16[128,512]{1,0:T(8,128)(2,1)S(1)}, u32[]{:S(2)}, u32[]{:S(2)}) collective-permute-start(bf16[128,512]{1,0:T(8,128)(2,1)} %collective-permute-done.1.refs_2_.refs_10_), channel_id=1, source_target_pairs={{0,7},{1,0},{2,1},{3,2},{4,3},{5,4},{6,5},{7,6},{8,15},{9,8},{10,9... | collective-permute-start | bytes 393224 | tf_op jit(solution)/shard_map/ppermute | solution.py:102
  17.4 6.3 %collective-permute-start.3 = (bf16[128,512]{1,0:T(8,128)(2,1)S(1)}, bf16[128,512]{1,0:T(8,128)(2,1)}, u32[]{:S(2)}, u32[]{:S(2)}) collective-permute-start(bf16[128,512]{1,0:T(8,128)(2,1)S(1)} %collective-permute-done.2.refs_3_.refs_11_), channel_id=1, source_target_pairs={{0,1},{1,2},{2,3},{3,4},{4,5},{5,6},{6,7},{7,0},{8,9},{9,10},{10,1... | collective-permute-start | bytes 393224 | tf_op jit(solution)/shard_map/ppermute | solution.py:102
  17.4 6.3 %collective-permute-start.6 = (bf16[128,512]{1,0:T(8,128)(2,1)S(1)}, bf16[128,512]{1,0:T(8,128)(2,1)S(1)}, u32[]{:S(2)}, u32[]{:S(2)}) collective-permute-start(bf16[128,512]{1,0:T(8,128)(2,1)S(1)} %collective-permute-done.5.refs_4_.refs_12_), channel_id=1, source_target_pairs={{0,7},{1,0},{2,1},{3,2},{4,3},{5,4},{6,5},{7,6},{8,15},{9,8},{10,9... | collective-permute-start | bytes 393224 | tf_op jit(solution)/shard_map/ppermute | solution.py:102
  23.7 6.5 %collective-permute-start.4 = (bf16[128,512]{1,0:T(8,128)(2,1)}, bf16[128,512]{1,0:T(8,128)(2,1)}, u32[]{:S(2)}, u32[]{:S(2)}) collective-permute-start(bf16[128,512]{1,0:T(8,128)(2,1)} %collective-permute-done.3.refs_5_.refs_13_), channel_id=1, source_target_pairs={{0,1},{1,2},{2,3},{3,4},{4,5},{5,6},{6,7},{7,0},{8,9},{9,10},{10,1... | collective-permute-start | bytes 393224 | tf_op jit(solution)/shard_map/ppermute | solution.py:102
  33.5 35.9 %all-to-all-start = ((bf16[64,128,128]{2,1,0:T(8,128)(2,1)}), bf16[64,128,128]{2,1,0:T(8,128)(2,1)}, u32[]{:S(2)}, u32[]{:S(2)}) async-start(bf16[64,128,128]{2,1,0:T(8,128)(2,1)} %get-tuple-element.57), calls=%async_computation | async-start | bytes 4194304 | tf_op jit(solution)/shard_map/all_to_all | solution.py:607
  41.3 6.8 %collective-permute-start.7 = (bf16[128,512]{1,0:T(8,128)(2,1)S(1)}, bf16[128,512]{1,0:T(8,128)(2,1)S(1)}, u32[]{:S(2)}, u32[]{:S(2)}) collective-permute-start(bf16[128,512]{1,0:T(8,128)(2,1)S(1)} %copy-done.3), channel_id=1, source_target_pairs={{0,1},{1,2},{2,3},{3,4},{4,5},{5,6},{6,7},{7,0},{8,9},{9,10},{10,1... | collective-permute-start | bytes 393224 | tf_op jit(solution)/shard_map/ppermute | solution.py:102
  41.9 6.3 %collective-permute-start.11 = (bf16[128,512]{1,0:T(8,128)(2,1)S(1)}, bf16[128,512]{1,0:T(8,128)(2,1)S(1)}, u32[]{:S(2)}, u32[]{:S(2)}) collective-permute-start(bf16[128,512]{1,0:T(8,128)(2,1)S(1)} %copy-done.3), channel_id=1, source_target_pairs={{0,7},{1,0},{2,1},{3,2},{4,3},{5,4},{6,5},{7,6},{8,15},{9,8},{10,9... | collective-permute-start | bytes 393224 | tf_op jit(solution)/shard_map/ppermute | solution.py:102
  48.2 6.2 %collective-permute-start.8 = (bf16[128,512]{1,0:T(8,128)(2,1)S(1)}, bf16[128,512]{1,0:T(8,128)(2,1)S(1)}, u32[]{:S(2)}, u32[]{:S(2)}) collective-permute-start(bf16[128,512]{1,0:T(8,128)(2,1)S(1)} %collective-permute-done.7.refs_1_), channel_id=1, source_target_pairs={{0,1},{1,2},{2,3},{3,4},{4,5},{5,6},{6,7},{7,0},{8,9},{9,10},{10,1... | collective-permute-start | bytes 393224 | tf_op jit(solution)/shard_map/ppermute | solution.py:102
  48.8 5.5 %collective-permute-start.12 = (bf16[128,512]{1,0:T(8,128)(2,1)S(1)}, bf16[128,512]{1,0:T(8,128)(2,1)}, u32[]{:S(2)}, u32[]{:S(2)}) collective-permute-start(bf16[128,512]{1,0:T(8,128)(2,1)S(1)} %collective-permute-done.11.refs_2_), channel_id=1, source_target_pairs={{0,7},{1,0},{2,1},{3,2},{4,3},{5,4},{6,5},{7,6},{8,15},{9,8},{10,9... | collective-permute-start | bytes 393224 | tf_op jit(solution)/shard_map/ppermute | solution.py:102
  54.4 6.3 %collective-permute-start.9 = (bf16[128,512]{1,0:T(8,128)(2,1)S(1)}, bf16[128,512]{1,0:T(8,128)(2,1)}, u32[]{:S(2)}, u32[]{:S(2)}) collective-permute-start(bf16[128,512]{1,0:T(8,128)(2,1)S(1)} %collective-permute-done.8.refs_3_), channel_id=1, source_target_pairs={{0,1},{1,2},{2,3},{3,4},{4,5},{5,6},{6,7},{7,0},{8,9},{9,10},{10,1... | collective-permute-start | bytes 393224 | tf_op jit(solution)/shard_map/ppermute | solution.py:102
  55.0 10.1 %collective-permute-start.13 = (bf16[128,512]{1,0:T(8,128)(2,1)}, bf16[128,512]{1,0:T(8,128)(2,1)}, u32[]{:S(2)}, u32[]{:S(2)}) collective-permute-start(bf16[128,512]{1,0:T(8,128)(2,1)} %collective-permute-done.12.refs_4_), channel_id=1, source_target_pairs={{0,7},{1,0},{2,1},{3,2},{4,3},{5,4},{6,5},{7,6},{8,15},{9,8},{10,9... | collective-permute-start | bytes 393224 | tf_op jit(solution)/shard_map/ppermute | solution.py:102
  60.6 7.0 %collective-permute-start.10 = (bf16[128,512]{1,0:T(8,128)(2,1)}, bf16[128,512]{1,0:T(8,128)(2,1)}, u32[]{:S(2)}, u32[]{:S(2)}) collective-permute-start(bf16[128,512]{1,0:T(8,128)(2,1)} %collective-permute-done.9.refs_5_), channel_id=1, source_target_pairs={{0,1},{1,2},{2,3},{3,4},{4,5},{5,6},{6,7},{7,0},{8,9},{9,10},{10,1... | collective-permute-start | bytes 393224 | tf_op jit(solution)/shard_map/ppermute | solution.py:102
  77.0 37.0 %all-to-all-start.1 = ((bf16[64,128,128]{2,1,0:T(8,128)(2,1)}), bf16[64,128,128]{2,1,0:T(8,128)(2,1)}, u32[]{:S(2)}, u32[]{:S(2)}) async-start(bf16[64,128,128]{2,1,0:T(8,128)(2,1)} %get-tuple-element.62), calls=%async_computation.1 | async-start | bytes 4194304 | tf_op jit(solution)/shard_map/all_to_all | solution.py:667
  84.6 10.0 %collective-permute-start.14 = (bf16[256,512]{1,0:T(8,128)(2,1)S(1)}, bf16[256,512]{1,0:T(8,128)(2,1)}, u32[]{:S(2)}, u32[]{:S(2)}) collective-permute-start(bf16[256,512]{1,0:T(8,128)(2,1)S(1)} %copy-done.1), channel_id=1, source_target_pairs={{0,1},{1,2},{2,3},{3,4},{4,5},{5,6},{6,7},{7,0},{8,9},{9,10},{10,1... | collective-permute-start | bytes 786440 | tf_op jit(solution)/shard_map/ppermute | solution.py:102
  84.6 9.9 %collective-permute-start.16 = (bf16[256,512]{1,0:T(8,128)(2,1)S(1)}, bf16[256,512]{1,0:T(8,128)(2,1)}, u32[]{:S(2)}, u32[]{:S(2)}) collective-permute-start(bf16[256,512]{1,0:T(8,128)(2,1)S(1)} %copy-done.1), channel_id=1, source_target_pairs={{0,7},{1,0},{2,1},{3,2},{4,3},{5,4},{6,5},{7,6},{8,15},{9,8},{10,9... | collective-permute-start | bytes 786440 | tf_op jit(solution)/shard_map/ppermute | solution.py:102
  94.6 10.4 %collective-permute-start.15 = (bf16[256,512]{1,0:T(8,128)(2,1)}, bf16[256,512]{1,0:T(8,128)(2,1)}, u32[]{:S(2)}, u32[]{:S(2)}) collective-permute-start(bf16[256,512]{1,0:T(8,128)(2,1)} %collective-permute-done.14.refs_6_), channel_id=1, source_target_pairs={{0,1},{1,2},{2,3},{3,4},{4,5},{5,6},{6,7},{7,0},{8,9},{9,10},{10,1... | collective-permute-start | bytes 786440 | tf_op jit(solution)/shard_map/ppermute | solution.py:102
  94.6 10.4 %collective-permute-start.17 = (bf16[256,512]{1,0:T(8,128)(2,1)}, bf16[256,512]{1,0:T(8,128)(2,1)}, u32[]{:S(2)}, u32[]{:S(2)}) collective-permute-start(bf16[256,512]{1,0:T(8,128)(2,1)} %collective-permute-done.16.refs_5_), channel_id=1, source_target_pairs={{0,7},{1,0},{2,1},{3,2},{4,3},{5,4},{6,5},{7,6},{8,15},{9,8},{10,9... | collective-permute-start | bytes 786440 | tf_op jit(solution)/shard_map/ppermute | solution.py:102
  105.0 8.9 %collective-permute-start.18 = (bf16[256,512]{1,0:T(8,128)(2,1)}, bf16[256,512]{1,0:T(8,128)(2,1)}, u32[]{:S(2)}, u32[]{:S(2)}) collective-permute-start(bf16[256,512]{1,0:T(8,128)(2,1)} %collective-permute-done.15.refs_7_), channel_id=1, source_target_pairs={{0,1},{1,2},{2,3},{3,4},{4,5},{5,6},{6,7},{7,0},{8,9},{9,10},{10,1... | collective-permute-start | bytes 786440 | tf_op jit(solution)/shard_map/ppermute | solution.py:102
  105.1 8.8 %collective-permute-start.19 = (bf16[256,512]{1,0:T(8,128)(2,1)}, bf16[256,512]{1,0:T(8,128)(2,1)}, u32[]{:S(2)}, u32[]{:S(2)}) collective-permute-start(bf16[256,512]{1,0:T(8,128)(2,1)} %collective-permute-done.17.refs_4_), channel_id=1, source_target_pairs={{0,7},{1,0},{2,1},{3,2},{4,3},{5,4},{6,5},{7,6},{8,15},{9,8},{10,9... | collective-permute-start | bytes 786440 | tf_op jit(solution)/shard_map/ppermute | solution.py:102
  118.0 15.1 %all-to-all-start.2 = ((bf16[32,8,512]{2,1,0:T(8,128)(2,1)}), bf16[32,8,512]{2,1,0:T(8,128)(2,1)S(1)}, u32[]{:S(2)}, u32[]{:S(2)}) async-start(bf16[32,8,512]{2,1,0:T(8,128)(2,1)} %bitcast.7), calls=%async_computation.2 | async-start | bytes 524288 | tf_op jit(solution)/shard_map/all_to_all | solution.py:707
  125.5 30.0 %collective-permute-start.27 = (bf16[256,512]{1,0:T(8,128)(2,1)}, bf16[256,512]{1,0:T(8,128)(2,1)}, u32[]{:S(2)}, u32[]{:S(2)}) collective-permute-start(bf16[256,512]{1,0:T(8,128)(2,1)} %collective-permute-done.18.refs_8_), channel_id=1, source_target_pairs={{0,1},{1,2},{2,3},{3,4},{4,5},{5,6},{6,7},{7,0},{8,9},{9,10},{10,1... | collective-permute-start | bytes 786440 | tf_op jit(solution)/shard_map/ppermute | solution.py:102
  133.9 28.5 %all-to-all-start.3 = ((bf16[32,8,512]{2,1,0:T(8,128)(2,1)}), bf16[32,8,512]{2,1,0:T(8,128)(2,1)}, u32[]{:S(2)}, u32[]{:S(2)}) async-start(bf16[32,8,512]{2,1,0:T(8,128)(2,1)} %sum_shares.1), calls=%async_computation.3 | async-start | bytes 524288 | tf_op jit(solution)/shard_map/all_to_all | solution.py:718
  139.6 8.7 %collective-permute-start.23 = (bf16[256,128]{1,0:T(8,128)(2,1)}, bf16[256,128]{1,0:T(8,128)(2,1)}, u32[]{:S(2)}, u32[]{:S(2)}) collective-permute-start(bf16[256,128]{1,0:T(8,128)(2,1)} %get-tuple-element.80), channel_id=1, source_target_pairs={{0,1},{1,2},{2,3},{3,4},{4,5},{5,6},{6,7},{7,0},{8,9},{9,10},{10,1... | collective-permute-start | bytes 196616 | tf_op jit(solution)/shard_map/ppermute | solution.py:102
  140.3 11.2 %collective-permute-start.24 = (bf16[256,128]{1,0:T(8,128)(2,1)}, bf16[256,128]{1,0:T(8,128)(2,1)}, u32[]{:S(2)}, u32[]{:S(2)}) collective-permute-start(bf16[256,128]{1,0:T(8,128)(2,1)} %get-tuple-element.81), channel_id=1, source_target_pairs={{0,2},{1,3},{2,4},{3,5},{4,6},{5,7},{6,0},{7,1},{8,10},{9,11},{10,... | collective-permute-start | bytes 196616 | tf_op jit(solution)/shard_map/ppermute | solution.py:102
  144.8 10.7 %collective-permute-start.25 = (bf16[256,128]{1,0:T(8,128)(2,1)}, bf16[256,128]{1,0:T(8,128)(2,1)}, u32[]{:S(2)}, u32[]{:S(2)}) collective-permute-start(bf16[256,128]{1,0:T(8,128)(2,1)} %get-tuple-element.82), channel_id=1, source_target_pairs={{0,3},{1,4},{2,5},{3,6},{4,7},{5,0},{6,1},{7,2},{8,11},{9,12},{10,... | collective-permute-start | bytes 196616 | tf_op jit(solution)/shard_map/ppermute | solution.py:102
  144.8 10.7 %collective-permute-start.26 = (bf16[256,128]{1,0:T(8,128)(2,1)}, bf16[256,128]{1,0:T(8,128)(2,1)}, u32[]{:S(2)}, u32[]{:S(2)}) collective-permute-start(bf16[256,128]{1,0:T(8,128)(2,1)} %get-tuple-element.83), channel_id=1, source_target_pairs={{0,4},{1,5},{2,6},{3,7},{4,0},{5,1},{6,2},{7,3},{8,12},{9,13},{10,... | collective-permute-start | bytes 196616 | tf_op jit(solution)/shard_map/ppermute | solution.py:102
  148.4 10.1 %collective-permute-start.20 = (bf16[256,128]{1,0:T(8,128)(2,1)}, bf16[256,128]{1,0:T(8,128)(2,1)}, u32[]{:S(2)}, u32[]{:S(2)}) collective-permute-start(bf16[256,128]{1,0:T(8,128)(2,1)} %get-tuple-element.75), channel_id=1, source_target_pairs={{0,5},{1,6},{2,7},{3,0},{4,1},{5,2},{6,3},{7,4},{8,13},{9,14},{10,... | collective-permute-start | bytes 196616 | tf_op jit(solution)/shard_map/ppermute | solution.py:102
  151.5 9.2 %collective-permute-start.21 = (bf16[256,128]{1,0:T(8,128)(2,1)}, bf16[256,128]{1,0:T(8,128)(2,1)}, u32[]{:S(2)}, u32[]{:S(2)}) collective-permute-start(bf16[256,128]{1,0:T(8,128)(2,1)} %get-tuple-element.76), channel_id=1, source_target_pairs={{0,6},{1,7},{2,0},{3,1},{4,2},{5,3},{6,4},{7,5},{8,14},{9,15},{10,... | collective-permute-start | bytes 196616 | tf_op jit(solution)/shard_map/ppermute | solution.py:102
  155.5 7.0 %collective-permute-start.22 = (bf16[256,128]{1,0:T(8,128)(2,1)}, bf16[256,128]{1,0:T(8,128)(2,1)}, u32[]{:S(2)}, u32[]{:S(2)}) collective-permute-start(bf16[256,128]{1,0:T(8,128)(2,1)} %get-tuple-element.77), channel_id=1, source_target_pairs={{0,7},{1,0},{2,1},{3,2},{4,3},{5,4},{6,5},{7,6},{8,15},{9,8},{10,9... | collective-permute-start | bytes 196616 | tf_op jit(solution)/shard_map/ppermute | solution.py:102
  (10 other events, 84.2 us)

commit v4 on v3

--- a/solution.py
+++ b/solution.py
@@ -104,6 +104,10 @@
 
 def ring_round(behind, ahead):
     return shifted(behind, 1), shifted(ahead, -1)
+
+
+def paired(x):
+    return lax.ppermute(x, "col", [(i, i ^ 1) for i in range(NB)])
 
 
 def block_at(col, i):
@@ -395,9 +399,10 @@
     wait_all(stores)
 
 
-def gather_grads_body(home_ref, returned_in, near_in, query_grad_in, attn_in, hidden_in, early_in, *refs):
-    piece_refs, refs = refs[:NB], refs[NB:]
-    part_out, returned_ref, near_ref, even_ref, odd_ref, proj_ref, hidden_ref, part_ref, *refs = refs
+def gather_grads_body(col_ref, home_ref, returned_in, near_in, query_grad_in, attn_in, hidden_in, early_in, *refs):
+    *pair_outs, part_out = refs[: 1 + NB // 2]
+    refs = refs[1 + NB // 2 :]
+    returned_ref, near_ref, even_ref, odd_ref, proj_ref, hidden_ref, part_ref, *refs = refs
     far_sems, in_sems, out_sems = refs
     parts = far_sems.shape[0]
     step = returned_in.shape[0] // parts
@@ -443,10 +448,17 @@
     wait_all(loads)
     for i in range(NB):
         proj_ref[HD : 3 * HD, rows_at(i)] = (near_ref[i] + (even_ref[i] + odd_ref[i])).astype(BF16)
-    at = [ORDER.index((NB - k) % NB) for k in range(NB)]
+    odd_place = lax.rem(col_ref[0], 2)
+    far_pieces, near_pieces = [], []
+    for j in range(NB // 2):
+        at = ORDER.index((NB - 2 * j) % NB)
+        near_pieces.append(proj_ref.at[:, pl.ds(at * BLK, BLK)])
+        next_at, last_at = ORDER.index((NB - 1 - 2 * j) % NB), ORDER.index((NB + 1 - 2 * j) % NB)
+        at = jnp.where(odd_place == 1, last_at, next_at)
+        far_pieces.append(proj_ref.at[:, pl.ds(pl.multiple_of(at * BLK, BLK), BLK)])
     stores = copies(
-        [part_ref, *(proj_ref.at[:, pl.ds(at[k] * BLK, BLK)] for k in range(NB))],
-        [part_out, *piece_refs],
+        [part_ref, *far_pieces, *near_pieces],
+        [part_out, *(out.at[1] for out in pair_outs), *(out.at[0] for out in pair_outs)],
         out_sems,
     )
     start_all(stores[1:])
@@ -461,69 +473,51 @@
     total_ref[...] = jnp.broadcast_to(total[None], total_ref.shape)
 
 
-def add_heads(piece_ins, weight_ins, piece_ref, weight_ref, piece_sems, weight_sems):
-    n = len(piece_ins)
-    pieces = copies(piece_ins, [piece_ref.at[k] for k in range(n)], piece_sems)
-    weights = copies(weight_ins, [weight_ref.at[k] for k in range(n)], weight_sems)
-    for k in range(n):
-        pieces[k].start()
-        weights[k].start()
+def scale_body(inv_root, total_ref, qkv_ref, out_ref):
+    total = total_ref[...].astype(F32) * inv_root
+    qkv_ref[...] = total[: 3 * HD]
+    out_ref[...] = total[3 * HD :]
+
+
+def finish_body(col_ref, *refs):
+    half = NB // 2
+    pair_ins, beside_in, weight_ins, refs = refs[:half], refs[half], refs[half + 1 : half + 1 + NB], refs[half + 1 + NB :]
+    state_in, grad_in, gain_in, layer_out, back_out, *refs = refs
+    piece_ref, weight_ref, state_ref, grad_ref, gain_ref, layer_ref, back_ref, *refs = refs
+    piece_sems, weight_sems, in_sems, out_sems = refs
+    pieces = copies(
+        [*(pair.at[0] for pair in pair_ins), beside_in],
+        [*(piece_ref.at[0, j] for j in range(half)), piece_ref.at[1]],
+        piece_sems,
+    )
+    weights = copies(weight_ins, [weight_ref.at[k] for k in range(NB)], weight_sems)
+    loads = copies([state_in, grad_in, gain_in], [state_ref, grad_ref, gain_ref], in_sems)
+    start_all(pieces)
+    start_all(weights)
+    start_all(loads)
+    wait_all(pieces)
+    wait_all(weights)
+    odd_place = lax.rem(col_ref[0], 2)
     out = jnp.zeros((BLK, D), F32)
     back = jnp.zeros((BLK, D), F32)
-    for k in range(n):
-        pieces[k].wait()
-        terms = piece_ref[k].astype(F32).T.astype(BF16)
-        weights[k].wait()
-        back += dot(terms[:, : 3 * HD], weight_ref[k, : 3 * HD, :])
-        out += dot(terms[:, 3 * HD :], weight_ref[k, 3 * HD :, :])
-    return out, back
-
-
-def first_heads_body(n, *refs):
-    piece_ins, weight_ins, (sum_out, piece_ref, weight_ref, sum_ref, *sems, out_sem) = (
-        refs[:n],
-        refs[n : 2 * n],
-        refs[2 * n :],
-    )
-    sum_ref[0], sum_ref[1] = add_heads(piece_ins, weight_ins, piece_ref, weight_ref, *sems)
-    store = pltpu.make_async_copy(sum_ref, sum_out, out_sem.at[0])
-    store.start()
-    store.wait()
-
-
-def finish_body(inv_root, n, *refs):
-    piece_ins, weight_ins, refs = refs[:n], refs[n : 2 * n], refs[2 * n :]
-    sum_in, state_in, grad_in, gain_in, total_in, layer_out, back_out, qkv_out, weight_out, *refs = refs
-    piece_ref, weight_ref, sum_ref, state_ref, grad_ref, gain_ref, total_ref, layer_ref, back_ref, scaled_ref, *refs = refs
-    piece_sems, weight_sems, in_sems, out_sems = refs
-    loads = copies(
-        [total_in, sum_in, state_in, grad_in, gain_in],
-        [total_ref, sum_ref, state_ref, grad_ref, gain_ref],
-        in_sems,
-    )
-    stores = copies(
-        [scaled_ref.at[pl.ds(0, 3 * HD)], scaled_ref.at[pl.ds(3 * HD, HD)], layer_ref, back_ref],
-        [qkv_out, weight_out, layer_out, back_out],
-        out_sems,
-    )
-    start_all(loads)
-    out, back = add_heads(piece_ins, weight_ins, piece_ref, weight_ref, piece_sems, weight_sems)
-    loads[0].wait()
-    scaled_ref[...] = total_ref[...].astype(F32) * inv_root
-    start_all(stores[:2])
-    wait_all(loads[1:])
-    out += sum_ref[0]
-    back += sum_ref[1]
+    for j in range(half):
+        beside = jnp.where(odd_place == 1, (2 * j + 1) % NB, (2 * j + NB - 1) % NB)
+        for own, head in ((0, 2 * j), (1, beside)):
+            terms = piece_ref[own, j].astype(F32).T.astype(BF16)
+            back += dot(terms[:, : 3 * HD], weight_ref[head, : 3 * HD, :])
+            out += dot(terms[:, 3 * HD :], weight_ref[head, 3 * HD :, :])
+    wait_all(loads)
     state = state_ref[...].astype(F32)
     gain = gain_ref[...]
     layer_ref[...] = (state + out).astype(BF16)
-    stores[2].start()
+    stores = copies([layer_ref, back_ref], [layer_out, back_out], out_sems)
+    stores[0].start()
     inv = lax.rsqrt(jnp.mean(state * state, axis=1, keepdims=True) + EPS)
     stat = jnp.sum(gain * back * state, axis=1, keepdims=True)
     back_ref[...] = (
         grad_ref[...].astype(F32) + inv * gain * back - state * (inv * inv * inv * stat / D)
     ).astype(BF16)
-    stores[3].start()
+    stores[1].start()
     wait_all(stores)
 
 
@@ -566,7 +560,6 @@
     row = shaped(1, D, kind=F32)
     counts = shaped(NB, ROWS, kind=F32)
     states, states_most = shaped(NB, BLK, D), shaped(NB - 1, BLK, D)
-    piece = shaped(4 * HD, BLK)
     head_weight, out_piece = shaped(3 * HD, D), shaped(HD, D)
 
     x1, x7 = ring_round(node_states, node_states)
@@ -688,10 +681,11 @@
     returned, w3, w5 = lax.optimization_barrier((returned, w3, w5))
     w4 = shifted(w3, 1)
 
-    *pieces, part = call(
+    half = NB // 2
+    *pairs, part = call(
         gather_grads_body,
-        (piece,) * NB + (shaped(4 * HD, D),),
-        [scalars()] + [left()] * 6,
+        (*(shaped(2, 4 * HD, BLK),) * half, shaped(4 * HD, D)),
+        [scalars()] * 2 + [left()] * 6,
         scratch=[
             *held(exchanged, blocks_float, shaped(NB + 1, BLK, BLK, kind=F32)),
             *held(shaped(NB + 1, BLK, BLK, kind=F32), shaped(4 * HD, ROWS), states, shaped(4 * HD, D)),
@@ -701,12 +695,12 @@
         ],
         flops=2 * ROWS * D * 128,
         name="gather_grads",
-    )(home, returned, near_grad, query_grad, attn, hidden, early)
+    )(col, home, returned, near_grad, query_grad, attn, hidden, early)
 
     share_rows = 4 * HD // doms
     shares = lax.all_to_all(part.reshape(doms, share_rows, D), "dom", 0, 0, tiled=True)
-    arrived = [pieces[0], *(shifted(pieces[k], k) for k in range(1, NB))]
-
+    pairs = [pairs[0], *(shifted(pairs[j], 2 * j) for j in range(1, half))]
+    beside = paired(jnp.stack([pair[1] for pair in pairs]))
     (totals,) = call(
         sum_body,
         (shaped(doms, share_rows, D),),
@@ -717,38 +711,29 @@
     )(shares)
     total = lax.all_to_all(totals, "dom", 0, 0, tiled=True).reshape(4 * HD, D)
     weights = (weights_own, w1, w2, w3, w4, w5, w6, w7)
-    cut = 5
-    sums = shaped(2, BLK, D, kind=F32)
-    (first,) = call(
-        functools.partial(first_heads_body, cut),
-        (sums,),
-        [left()] * (2 * cut),
+    layer_out, state_grad = call(
+        finish_body,
+        (node, node),
+        [scalars()] + [left()] * (half + 1 + NB + 3),
         scratch=[
-            *held(shaped(cut, 4 * HD, BLK), shaped(cut, 4 * HD, D), sums),
-            dma_sems(cut),
-            dma_sems(cut),
-            dma_sems(1),
-        ],
-        flops=2 * BLK * D * 256 * cut,
-        name="first_heads",
-    )(*arrived[:cut], *weights[:cut])
-    rest = NB - cut
-    total_shape, total_float = shaped(4 * HD, D), shaped(4 * HD, D, kind=F32)
-    layer_out, state_grad, qkv_grad, out_weight_grad = call(
-        functools.partial(finish_body, 1.0 / math.sqrt(far_owner.shape[0] * BLK), rest),
-        (node, node, shaped(3 * HD, D, kind=F32), shaped(HD, D, kind=F32)),
-        [left()] * (2 * rest + 5),
-        scratch=[
-            *held(shaped(rest, 4 * HD, BLK), shaped(rest, 4 * HD, D), sums, node, node, row, total_shape),
-            *held(node, node, total_float),
-            dma_sems(rest),
-            dma_sems(rest),
-            dma_sems(5),
-            dma_sems(4),
-        ],
-        flops=2 * BLK * D * 256 * rest,
+            *held(shaped(2, half, 4 * HD, BLK), shaped(NB, 4 * HD, D), node, node, row, node, node),
+            dma_sems(half + 1),
+            dma_sems(NB),
+            dma_sems(3),
+            dma_sems(2),
+        ],
+        flops=2 * BLK * D * 2048,
         name="finish",
-    )(*arrived[cut:], *weights[cut:], first, node_states, out_grad, gain, total)
+    )(col, *pairs, beside, *weights, node_states, out_grad, gain)
+    total, layer_out, state_grad = lax.optimization_barrier((total, layer_out, state_grad))
+    qkv_grad, out_weight_grad = call(
+        functools.partial(scale_body, 1.0 / math.sqrt(far_owner.shape[0] * BLK)),
+        (shaped(3 * HD, D, kind=F32), shaped(HD, D, kind=F32)),
+        [whole()],
+        out_specs=[whole()] * 2,
+        name="scale",
+        limit=4,
+    )(total)
 
     return (layer_out, state_grad, qkv_grad, out_weight_grad)
 

time: 167 us -> 161 us (0.964); the launches traced: 166 us -> 158 us
  starting transfers between devices: 75 us -> 69.5 us
  waiting for transfers between devices: 42.6 us -> 39.7 us
    ppermute x28 -> x24, starting transfers between devices: 46.5 us -> 40.1 us  [shifted(): return lax.ppermute(x, 'col', [(i, (i + k) % NB) for i in range(NB)])]
    ppermute x28 -> x24, waiting for transfers between devices: 35.6 us -> 30.4 us  [shifted(): return lax.ppermute(x, 'col', [(i, (i + k) % NB) for i in range(NB)])]
    all_to_all x1, waiting for transfers between devices: 0.01 us -> 3.95 us  [shards(): total = lax.all_to_all(totals, 'dom', 0, 0, tiled=True).reshape(4 * HD, D)]
  transfers between devices with their start and end apart: 32 -> 29, of which waited for: 13 -> 11; matrix products, arithmetic and copies ran while one was open for 1% -> 1% of each run, Pallas kernels for 15% -> 16%
where the time goes in v4:
time: 161 us; the launch traced here: 158 us
  starting transfers between devices  69.5 us (43%)
  Pallas kernels  42.7 us (27%)
  waiting for transfers between devices  39.7 us (25%)
  local copies, waits for them, and re-layouts  3.48 us (2%)
    ppermute x24, starting transfers between devices, shifted(): return lax.ppermute(x, 'col', [(i, (i + k) % NB) for i in range(NB)])  40.1 us
    ppermute x24, waiting for transfers between devices, shifted(): return lax.ppermute(x, 'col', [(i, (i + k) % NB) for i in range(NB)])  30.4 us
    all_to_all x1, starting transfers between devices, shards(): fetched = lax.all_to_all(outgoing, 'dom', 0, 0, tiled=True)  7.82 us
    all_to_all x1, starting transfers between devices, shards(): returned = lax.all_to_all(outgoing_back, 'dom', 0, 0, tiled=True)  7.57 us
    pallas_call x1, Pallas kernels, shards(): call(far_body, (across, blocks, blocks_float, exchanged), [scalars()] * 2...  7.53 us
    all_to_all x1, starting transfers between devices, shards(): lax.all_to_all(part.reshape(doms, share_rows, D), 'dom', 0, 0, tiled=True)  7.39 us
    pallas_call x1, Pallas kernels, shards(): call(near_backward_body, (across, blocks_float, shaped(2 * HD, D), states...  7.17 us
    all_to_all x1, starting transfers between devices, shards(): total = lax.all_to_all(totals, 'dom', 0, 0, tiled=True).reshape(4 * HD, D)  5.68 us
  transfers between devices with their start and end apart: 29, of which 11 were waited for; matrix products, arithmetic and copies ran while one was open for 1% of the time, Pallas kernels for 16%

profile of v4, /device:TPU:2, one launch (start us, length us, event | category | flops | bytes accessed | tf_op | source)
XLA Modules:
  0.0 157.7 jit_solution(14225924498218694670)
XLA Ops:
  2.6 4.0 %collective-permute-start.1 = (bf16[128,512]{1,0:T(8,128)(2,1)}, bf16[128,512]{1,0:T(8,128)(2,1)}, u32[]{:S(2)}, u32[]{:S(2)}) collective-permute-start(bf16[128,512]{1,0:T(8,128)(2,1)} %refs_13_.1), channel_id=1, source_target_pairs={{0,7},{1,0},{2,1},{3,2},{4,3},{5,4},{6,5},{7,6},{8,15},{9,8},{10,9... | collective-permute-start | bytes 393224 | tf_op jit(solution)/shard_map/ppermute | solution.py:102
  10.4 3.2 %collective-permute-start.5 = (bf16[128,512]{1,0:T(8,128)(2,1)}, bf16[128,512]{1,0:T(8,128)(2,1)S(1)}, u32[]{:S(2)}, u32[]{:S(2)}) collective-permute-start(bf16[128,512]{1,0:T(8,128)(2,1)} %collective-permute-done.1.refs_2_.refs_10_), channel_id=1, source_target_pairs={{0,7},{1,0},{2,1},{3,2},{4,3},{5,4},{6,5},{7,6},{8,15},{9,8},{10,9... | collective-permute-start | bytes 393224 | tf_op jit(solution)/shard_map/ppermute | solution.py:102
  13.6 3.2 %collective-permute-done.2.refs_3_.refs_11_ = bf16[128,512]{1,0:T(8,128)(2,1)S(1)} collective-permute-done((bf16[128,512]{1,0:T(8,128)(2,1)}, bf16[128,512]{1,0:T(8,128)(2,1)S(1)}, u32[]{:S(2)}, u32[]{:S(2)}) %collective-permute-start.2) | collective-permute-done | bytes 131104 | tf_op jit(solution)/shard_map/ppermute | solution.py:102
  17.4 3.2 %collective-permute-start.6 = (bf16[128,512]{1,0:T(8,128)(2,1)S(1)}, bf16[128,512]{1,0:T(8,128)(2,1)S(1)}, u32[]{:S(2)}, u32[]{:S(2)}) collective-permute-start(bf16[128,512]{1,0:T(8,128)(2,1)S(1)} %collective-permute-done.5.refs_4_.refs_12_), channel_id=1, source_target_pairs={{0,7},{1,0},{2,1},{3,2},{4,3},{5,4},{6,5},{7,6},{8,15},{9,8},{10,9... | collective-permute-start | bytes 393224 | tf_op jit(solution)/shard_map/ppermute | solution.py:102
  20.7 3.0 %collective-permute-done.3.refs_5_.refs_13_ = bf16[128,512]{1,0:T(8,128)(2,1)} collective-permute-done((bf16[128,512]{1,0:T(8,128)(2,1)S(1)}, bf16[128,512]{1,0:T(8,128)(2,1)}, u32[]{:S(2)}, u32[]{:S(2)}) %collective-permute-start.3) | collective-permute-done | bytes 131104 | tf_op jit(solution)/shard_map/ppermute | solution.py:102
  24.4 4.5 %project_most.1 = (bf16[8,128,128]{2,1,0:T(8,128)(2,1)}, bf16[8,128,128]{2,1,0:T(8,128)(2,1)}, bf16[64,128,128]{2,1,0:T(8,128)(2,1)}) custom-call(s32[2,256]{1,0:T(2,128)} %get-tuple-element.51.send_ref.home_ref, bf16[128,512]{1,0:T(8,128)(2,1)} %refs_13_.1, bf16[128,512]{1,0:T(8,128)(2,1)} %collective-permute-done.refs_1_.refs_9_, ...), custom_call_target="tpu_custom_call" | custom-call | flops 268435456 | bytes 1048576 | tf_op jit(solution)/shard_map/project_most/pallas_call | solution.py:571
  30.2 3.2 %project_last.1 = (bf16[8,128,128]{2,1,0:T(8,128)(2,1)}, bf16[8,128,128]{2,1,0:T(8,128)(2,1)}, bf16[64,128,128]{2,1,0:T(8,128)(2,1)}) custom-call(s32[2,256]{1,0:T(2,128)} %get-tuple-element.51.send_ref.home_ref, bf16[128,512]{1,0:T(8,128)(2,1)} %collective-permute-done.4.chunk_in.refs_15_, ...), custom_call_target="tpu_custom_call", output_to_operand_aliasing={{0}: (4, {}), {1}: (5, {}), {2}: (6, {})} | custom-call | flops 33554432 | bytes 1048576 | tf_op jit(solution)/shard_map/project_last/pallas_call | solution.py:584
  33.5 7.8 %all-to-all-start = ((bf16[64,128,128]{2,1,0:T(8,128)(2,1)}), bf16[64,128,128]{2,1,0:T(8,128)(2,1)}, u32[]{:S(2)}, u32[]{:S(2)}) async-start(bf16[64,128,128]{2,1,0:T(8,128)(2,1)} %get-tuple-element.60), calls=%async_computation | async-start | bytes 4194304 | tf_op jit(solution)/shard_map/all_to_all | solution.py:600
  41.9 2.8 %collective-permute-start.11 = (bf16[128,512]{1,0:T(8,128)(2,1)S(1)}, bf16[128,512]{1,0:T(8,128)(2,1)S(1)}, u32[]{:S(2)}, u32[]{:S(2)}) collective-permute-start(bf16[128,512]{1,0:T(8,128)(2,1)S(1)} %copy-done.3), channel_id=1, source_target_pairs={{0,7},{1,0},{2,1},{3,2},{4,3},{5,4},{6,5},{7,6},{8,15},{9,8},{10,9... | collective-permute-start | bytes 393224 | tf_op jit(solution)/shard_map/ppermute | solution.py:102
  44.7 3.5 %collective-permute-done.7.refs_1_ = bf16[128,512]{1,0:T(8,128)(2,1)S(1)} collective-permute-done((bf16[128,512]{1,0:T(8,128)(2,1)S(1)}, bf16[128,512]{1,0:T(8,128)(2,1)S(1)}, u32[]{:S(2)}, u32[]{:S(2)}) %collective-permute-start.7) | collective-permute-done | bytes 131104 | tf_op jit(solution)/shard_map/ppermute | solution.py:102
  48.8 2.7 %collective-permute-start.12 = (bf16[128,512]{1,0:T(8,128)(2,1)S(1)}, bf16[128,512]{1,0:T(8,128)(2,1)}, u32[]{:S(2)}, u32[]{:S(2)}) collective-permute-start(bf16[128,512]{1,0:T(8,128)(2,1)S(1)} %collective-permute-done.11.refs_2_), channel_id=1, source_target_pairs={{0,7},{1,0},{2,1},{3,2},{4,3},{5,4},{6,5},{7,6},{8,15},{9,8},{10,9... | collective-permute-start | bytes 393224 | tf_op jit(solution)/shard_map/ppermute | solution.py:102
  51.5 2.9 %collective-permute-done.8.refs_3_ = bf16[128,512]{1,0:T(8,128)(2,1)S(1)} collective-permute-done((bf16[128,512]{1,0:T(8,128)(2,1)S(1)}, bf16[128,512]{1,0:T(8,128)(2,1)S(1)}, u32[]{:S(2)}, u32[]{:S(2)}) %collective-permute-start.8) | collective-permute-done | bytes 131104 | tf_op jit(solution)/shard_map/ppermute | solution.py:102
  55.0 2.8 %collective-permute-start.13 = (bf16[128,512]{1,0:T(8,128)(2,1)}, bf16[128,512]{1,0:T(8,128)(2,1)}, u32[]{:S(2)}, u32[]{:S(2)}) collective-permute-start(bf16[128,512]{1,0:T(8,128)(2,1)} %collective-permute-done.12.refs_4_), channel_id=1, source_target_pairs={{0,7},{1,0},{2,1},{3,2},{4,3},{5,4},{6,5},{7,6},{8,15},{9,8},{10,9... | collective-permute-start | bytes 393224 | tf_op jit(solution)/shard_map/ppermute | solution.py:102
  57.8 2.9 %collective-permute-done.9.refs_5_ = bf16[128,512]{1,0:T(8,128)(2,1)} collective-permute-done((bf16[128,512]{1,0:T(8,128)(2,1)S(1)}, bf16[128,512]{1,0:T(8,128)(2,1)}, u32[]{:S(2)}, u32[]{:S(2)}) %collective-permute-start.9) | collective-permute-done | bytes 131104 | tf_op jit(solution)/shard_map/ppermute | solution.py:102
  61.4 3.7 %near_forward.1.num_in = f32[8,128,128]{2,1,0:T(8,128)} custom-call(s32[1]{0:T(128)} %bitcast.col_ref, bf16[8,128,128]{2,1,0:T(8,128)(2,1)} %get-tuple-element.58.query_in.refs_17_, bf16[8,128,128]{2,1,0:T(8,128)(2,1)} %get-tuple-element.61.kv_in.refs_18_, f32[8,1024]{1,0:T(8,128)} %get-tuple-element.62.count_in.refs_19_), custom_call_target="tpu_custom_call" | custom-call | flops 536870912 | bytes 1048576 | tf_op jit(solution)/shard_map/near_forward/pallas_call | solution.py:620
  65.1 2.5 %attn_grad.1.ag_in = f32[8,128,128]{2,1,0:T(8,128)} custom-call(bf16[128,512]{1,0:T(8,128)(2,1)} %refs_14_.1, bf16[128,512]{1,0:T(8,128)(2,1)} %copy-done.10, bf16[128,512]{1,0:T(8,128)(2,1)} %copy-done.11, bf16[128,512]{1,0:T(8,128)(2,1)} %copy-done.12, bf16[128,512]{1,0:T(8,128)(2,1)} %collective-permute-done.12.refs_4_, ...), custom_call_target="tpu_custom_call" | custom-call | flops 134217728 | bytes 1048576 | tf_op jit(solution)/shard_map/attn_grad/pallas_call | solution.py:607
  69.4 7.5 %far_both.1 = (bf16[64,1024]{1,0:T(8,128)(2,1)}, bf16[8,128,128]{2,1,0:T(8,128)(2,1)}, f32[8,128,128]{2,1,0:T(8,128)}, bf16[64,128,128]{2,1,0:T(8,128)(2,1)}) custom-call(s32[2]{0:T(128)} %pad_add_fusion.where_ref, s32[4,256]{1,0:T(4,128)} %get-tuple-element.52.place_ref, bf16[8,128,128]{2,1,0:T(8,128)(2,1)} %get-tuple-element.58.query_in.refs_17_, ...), custom_call_target="tpu_custom_call" | custom-call | flops 536870912 | bytes 1048576 | tf_op jit(solution)/shard_map/far_both/pallas_call | solution.py:639
  77.0 7.6 %all-to-all-start.1 = ((bf16[64,128,128]{2,1,0:T(8,128)(2,1)}), bf16[64,128,128]{2,1,0:T(8,128)(2,1)}, u32[]{:S(2)}, u32[]{:S(2)}) async-start(bf16[64,128,128]{2,1,0:T(8,128)(2,1)} %get-tuple-element.65), calls=%async_computation.1 | async-start | bytes 4194304 | tf_op jit(solution)/shard_map/all_to_all | solution.py:660
  84.6 3.3 %collective-permute-start.16 = (bf16[256,512]{1,0:T(8,128)(2,1)S(1)}, bf16[256,512]{1,0:T(8,128)(2,1)}, u32[]{:S(2)}, u32[]{:S(2)}) collective-permute-start(bf16[256,512]{1,0:T(8,128)(2,1)S(1)} %copy-done.1), channel_id=1, source_target_pairs={{0,7},{1,0},{2,1},{3,2},{4,3},{5,4},{6,5},{7,6},{8,15},{9,8},{10,9... | collective-permute-start | bytes 786440 | tf_op jit(solution)/shard_map/ppermute | solution.py:102
  87.9 6.6 %collective-permute-done.14.refs_6_ = bf16[256,512]{1,0:T(8,128)(2,1)} collective-permute-done((bf16[256,512]{1,0:T(8,128)(2,1)S(1)}, bf16[256,512]{1,0:T(8,128)(2,1)}, u32[]{:S(2)}, u32[]{:S(2)}) %collective-permute-start.14) | collective-permute-done | bytes 262176 | tf_op jit(solution)/shard_map/ppermute | solution.py:102
  94.6 3.2 %collective-permute-start.17 = (bf16[256,512]{1,0:T(8,128)(2,1)}, bf16[256,512]{1,0:T(8,128)(2,1)}, u32[]{:S(2)}, u32[]{:S(2)}) collective-permute-start(bf16[256,512]{1,0:T(8,128)(2,1)} %collective-permute-done.16.refs_12_), channel_id=1, source_target_pairs={{0,7},{1,0},{2,1},{3,2},{4,3},{5,4},{6,5},{7,6},{8,15},{9,8},{10,9... | collective-permute-start | bytes 786440 | tf_op jit(solution)/shard_map/ppermute | solution.py:102
  97.8 7.2 %near_backward.1 = (bf16[64,1024]{1,0:T(8,128)(2,1)}, f32[8,128,128]{2,1,0:T(8,128)}, bf16[128,512]{1,0:T(8,128)(2,1)}, bf16[8,128,512]{2,1,0:T(8,128)(2,1)}) custom-call(s32[1]{0:T(128)} %bitcast.col_ref, bf16[128,512]{1,0:T(8,128)(2,1)} %refs_14_.1, bf16[128,512]{1,0:T(8,128)(2,1)} %copy-done.10, bf16[128,512]{1,0:T(8,128)(2,1)} %copy-done.11, ...), custom_call_target="tpu_custom_call" | custom-call | flops 1342177280 | bytes 1048576 | tf_op jit(solution)/shard_map/near_backward/pallas_call | solution.py:664
  105.1 3.2 %collective-permute-start.19 = (bf16[256,512]{1,0:T(8,128)(2,1)}, bf16[256,512]{1,0:T(8,128)(2,1)}, u32[]{:S(2)}, u32[]{:S(2)}) collective-permute-start(bf16[256,512]{1,0:T(8,128)(2,1)} %collective-permute-done.17.refs_11_), channel_id=1, source_target_pairs={{0,7},{1,0},{2,1},{3,2},{4,3},{5,4},{6,5},{7,6},{8,15},{9,8},{10,9... | collective-permute-start | bytes 786440 | tf_op jit(solution)/shard_map/ppermute | solution.py:102
  108.3 5.6 %collective-permute-done.18.refs_8_ = bf16[256,512]{1,0:T(8,128)(2,1)} collective-permute-done((bf16[256,512]{1,0:T(8,128)(2,1)}, bf16[256,512]{1,0:T(8,128)(2,1)}, u32[]{:S(2)}, u32[]{:S(2)}) %collective-permute-start.18) | collective-permute-done | bytes 262176 | tf_op jit(solution)/shard_map/ppermute | solution.py:102
  113.9 4.1 %gather_grads.1 = (bf16[2,256,128]{2,1,0:T(8,128)(2,1)}, bf16[2,256,128]{2,1,0:T(8,128)(2,1)}, bf16[2,256,128]{2,1,0:T(8,128)(2,1)}, bf16[2,256,128]{2,1,0:T(8,128)(2,1)}, bf16[256,512]{1,0:T(8,128)(2,1)}) custom-call(s32[1]{0:T(128)} %bitcast.col_ref, s32[2,256]{1,0:T(2,128)} %get-tuple-element.51.send_ref.home_ref, ...), custom_call_target="tpu_custom_call" | custom-call | flops 134217728 | bytes 1048576 | tf_op jit(solution)/shard_map/gather_grads/pallas_call | solution.py:685
  118.0 2.3 %collective-permute-start.20 = (bf16[2,256,128]{2,1,0:T(8,128)(2,1)}, bf16[2,256,128]{2,1,0:T(8,128)(2,1)S(1)}, u32[]{:S(2)}, u32[]{:S(2)}) collective-permute-start(bf16[2,256,128]{2,1,0:T(8,128)(2,1)} %get-tuple-element.80), channel_id=1, source_target_pairs={{0,2},{1,3},{2,4},{3,5},{4,6},{5,7},{6,0},{7,1},{8,10},{9,11},{10,... | collective-permute-start | bytes 393224 | tf_op jit(solution)/shard_map/ppermute | solution.py:102
  122.5 4.0 %collective-permute-start.22 = (bf16[2,256,128]{2,1,0:T(8,128)(2,1)}, bf16[2,256,128]{2,1,0:T(8,128)(2,1)S(1)}, u32[]{:S(2)}, u32[]{:S(2)}) collective-permute-start(bf16[2,256,128]{2,1,0:T(8,128)(2,1)} %get-tuple-element.82), channel_id=1, source_target_pairs={{0,6},{1,7},{2,0},{3,1},{4,2},{5,3},{6,4},{7,5},{8,14},{9,15},{10,... | collective-permute-start | bytes 393224 | tf_op jit(solution)/shard_map/ppermute | solution.py:102
  126.5 7.4 %all-to-all-start.2 = ((bf16[32,8,512]{2,1,0:T(8,128)(2,1)}), bf16[32,8,512]{2,1,0:T(8,128)(2,1)S(1)}, u32[]{:S(2)}, u32[]{:S(2)}) async-start(bf16[32,8,512]{2,1,0:T(8,128)(2,1)} %bitcast.7), calls=%async_computation.2 | async-start | bytes 524288 | tf_op jit(solution)/shard_map/all_to_all | solution.py:701
  136.2 5.4 %all-to-all-done.2.share_ref = bf16[32,8,512]{2,1,0:T(8,128)(2,1)S(1)} async-done(((bf16[32,8,512]{2,1,0:T(8,128)(2,1)}), bf16[32,8,512]{2,1,0:T(8,128)(2,1)S(1)}, u32[]{:S(2)}, u32[]{:S(2)}) %all-to-all-start.2) | async-done | bytes 262176 | tf_op jit(solution)/shard_map/all_to_all | solution.py:701
  142.4 5.7 %all-to-all-start.3 = ((bf16[32,8,512]{2,1,0:T(8,128)(2,1)}), bf16[32,8,512]{2,1,0:T(8,128)(2,1)}, u32[]{:S(2)}, u32[]{:S(2)}) async-start(bf16[32,8,512]{2,1,0:T(8,128)(2,1)} %sum_shares.1), calls=%async_computation.3 | async-start | bytes 524288 | tf_op jit(solution)/shard_map/all_to_all | solution.py:712
  148.1 3.9 %finish.1 = (bf16[128,512]{1,0:T(8,128)(2,1)}, bf16[128,512]{1,0:T(8,128)(2,1)}) custom-call(s32[1]{0:T(128)} %bitcast.col_ref, bf16[2,256,128]{2,1,0:T(8,128)(2,1)} %get-tuple-element.79.refs_0_, bf16[2,256,128]{2,1,0:T(8,128)(2,1)} %copy-done.4, bf16[2,256,128]{2,1,0:T(8,128)(2,1)} %copy-done.5, bf16[2,256,128]{2,1,0:T(8,128)(2,1)} %copy-done.6, ...), custom_call_target="tpu_custom_call" | custom-call | flops 268435456 | bytes 1048576 | tf_op jit(solution)/shard_map/finish/pallas_call | solution.py:714
  152.0 3.9 %all-to-all-done.3 = bf16[32,8,512]{2,1,0:T(8,128)(2,1)} async-done(((bf16[32,8,512]{2,1,0:T(8,128)(2,1)}), bf16[32,8,512]{2,1,0:T(8,128)(2,1)}, u32[]{:S(2)}, u32[]{:S(2)}) %all-to-all-start.3) | async-done | bytes 262176 | tf_op jit(solution)/shard_map/all_to_all | solution.py:712
  (71 shorter events, 19.8 us)
Async XLA Ops:
  0.6 9.7 %collective-permute-start = (bf16[128,512]{1,0:T(8,128)(2,1)}, bf16[128,512]{1,0:T(8,128)(2,1)}, u32[]{:S(2)}, u32[]{:S(2)}) collective-permute-start(bf16[128,512]{1,0:T(8,128)(2,1)} %refs_13_.1), channel_id=1, source_target_pairs={{0,1},{1,2},{2,3},{3,4},{4,5},{5,6},{6,7},{7,0},{8,9},{9,10},{10,1... | collective-permute-start | bytes 393224 | tf_op jit(solution)/shard_map/ppermute | solution.py:102
  2.6 7.8 %collective-permute-start.1 = (bf16[128,512]{1,0:T(8,128)(2,1)}, bf16[128,512]{1,0:T(8,128)(2,1)}, u32[]{:S(2)}, u32[]{:S(2)}) collective-permute-start(bf16[128,512]{1,0:T(8,128)(2,1)} %refs_13_.1), channel_id=1, source_target_pairs={{0,7},{1,0},{2,1},{3,2},{4,3},{5,4},{6,5},{7,6},{8,15},{9,8},{10,9... | collective-permute-start | bytes 393224 | tf_op jit(solution)/shard_map/ppermute | solution.py:102
  10.4 6.4 %collective-permute-start.2 = (bf16[128,512]{1,0:T(8,128)(2,1)}, bf16[128,512]{1,0:T(8,128)(2,1)S(1)}, u32[]{:S(2)}, u32[]{:S(2)}) collective-permute-start(bf16[128,512]{1,0:T(8,128)(2,1)} %collective-permute-done.refs_1_.refs_9_), channel_id=1, source_target_pairs={{0,1},{1,2},{2,3},{3,4},{4,5},{5,6},{6,7},{7,0},{8,9},{9,10},{10,1... | collective-permute-start | bytes 393224 | tf_op jit(solution)/shard_map/ppermute | solution.py:102
  10.4 7.0 %collective-permute-start.5 = (bf16[128,512]{1,0:T(8,128)(2,1)}, bf16[128,512]{1,0:T(8,128)(2,1)S(1)}, u32[]{:S(2)}, u32[]{:S(2)}) collective-permute-start(bf16[128,512]{1,0:T(8,128)(2,1)} %collective-permute-done.1.refs_2_.refs_10_), channel_id=1, source_target_pairs={{0,7},{1,0},{2,1},{3,2},{4,3},{5,4},{6,5},{7,6},{8,15},{9,8},{10,9... | collective-permute-start | bytes 393224 | tf_op jit(solution)/shard_map/ppermute | solution.py:102
  17.4 6.3 %collective-permute-start.3 = (bf16[128,512]{1,0:T(8,128)(2,1)S(1)}, bf16[128,512]{1,0:T(8,128)(2,1)}, u32[]{:S(2)}, u32[]{:S(2)}) collective-permute-start(bf16[128,512]{1,0:T(8,128)(2,1)S(1)} %collective-permute-done.2.refs_3_.refs_11_), channel_id=1, source_target_pairs={{0,1},{1,2},{2,3},{3,4},{4,5},{5,6},{6,7},{7,0},{8,9},{9,10},{10,1... | collective-permute-start | bytes 393224 | tf_op jit(solution)/shard_map/ppermute | solution.py:102
  17.4 6.3 %collective-permute-start.6 = (bf16[128,512]{1,0:T(8,128)(2,1)S(1)}, bf16[128,512]{1,0:T(8,128)(2,1)S(1)}, u32[]{:S(2)}, u32[]{:S(2)}) collective-permute-start(bf16[128,512]{1,0:T(8,128)(2,1)S(1)} %collective-permute-done.5.refs_4_.refs_12_), channel_id=1, source_target_pairs={{0,7},{1,0},{2,1},{3,2},{4,3},{5,4},{6,5},{7,6},{8,15},{9,8},{10,9... | collective-permute-start | bytes 393224 | tf_op jit(solution)/shard_map/ppermute | solution.py:102
  23.7 6.5 %collective-permute-start.4 = (bf16[128,512]{1,0:T(8,128)(2,1)}, bf16[128,512]{1,0:T(8,128)(2,1)}, u32[]{:S(2)}, u32[]{:S(2)}) collective-permute-start(bf16[128,512]{1,0:T(8,128)(2,1)} %collective-permute-done.3.refs_5_.refs_13_), channel_id=1, source_target_pairs={{0,1},{1,2},{2,3},{3,4},{4,5},{5,6},{6,7},{7,0},{8,9},{9,10},{10,1... | collective-permute-start | bytes 393224 | tf_op jit(solution)/shard_map/ppermute | solution.py:102
  33.5 7.9 %copy-start.3 = (bf16[128,512]{1,0:T(8,128)(2,1)S(1)}, bf16[128,512]{1,0:T(8,128)(2,1)}, u32[]{:S(2)}) copy-start(bf16[128,512]{1,0:T(8,128)(2,1)} %refs_14_.1) | copy-start | bytes 393220
  33.5 27.2 %copy-start = (bf16[192,512]{1,0:T(8,128)(2,1)S(1)}, bf16[192,512]{1,0:T(8,128)(2,1)}, u32[]{:S(2)}) copy-start(bf16[192,512]{1,0:T(8,128)(2,1)} %weight_in.2) | copy-start | bytes 589828
  33.5 27.2 %copy-start.2 = (bf16[64,512]{1,0:T(8,128)(2,1)S(1)}, bf16[64,512]{1,0:T(8,128)(2,1)}, u32[]{:S(2)}) copy-start(bf16[64,512]{1,0:T(8,128)(2,1)} %weight_in.3) | copy-start | bytes 196612
  33.5 35.9 %all-to-all-start = ((bf16[64,128,128]{2,1,0:T(8,128)(2,1)}), bf16[64,128,128]{2,1,0:T(8,128)(2,1)}, u32[]{:S(2)}, u32[]{:S(2)}) async-start(bf16[64,128,128]{2,1,0:T(8,128)(2,1)} %get-tuple-element.60), calls=%async_computation | async-start | bytes 4194304 | tf_op jit(solution)/shard_map/all_to_all | solution.py:600
  41.3 6.8 %collective-permute-start.7 = (bf16[128,512]{1,0:T(8,128)(2,1)S(1)}, bf16[128,512]{1,0:T(8,128)(2,1)S(1)}, u32[]{:S(2)}, u32[]{:S(2)}) collective-permute-start(bf16[128,512]{1,0:T(8,128)(2,1)S(1)} %copy-done.3), channel_id=1, source_target_pairs={{0,1},{1,2},{2,3},{3,4},{4,5},{5,6},{6,7},{7,0},{8,9},{9,10},{10,1... | collective-permute-start | bytes 393224 | tf_op jit(solution)/shard_map/ppermute | solution.py:102
  41.9 6.3 %collective-permute-start.11 = (bf16[128,512]{1,0:T(8,128)(2,1)S(1)}, bf16[128,512]{1,0:T(8,128)(2,1)S(1)}, u32[]{:S(2)}, u32[]{:S(2)}) collective-permute-start(bf16[128,512]{1,0:T(8,128)(2,1)S(1)} %copy-done.3), channel_id=1, source_target_pairs={{0,7},{1,0},{2,1},{3,2},{4,3},{5,4},{6,5},{7,6},{8,15},{9,8},{10,9... | collective-permute-start | bytes 393224 | tf_op jit(solution)/shard_map/ppermute | solution.py:102
  48.2 6.2 %collective-permute-start.8 = (bf16[128,512]{1,0:T(8,128)(2,1)S(1)}, bf16[128,512]{1,0:T(8,128)(2,1)S(1)}, u32[]{:S(2)}, u32[]{:S(2)}) collective-permute-start(bf16[128,512]{1,0:T(8,128)(2,1)S(1)} %collective-permute-done.7.refs_1_), channel_id=1, source_target_pairs={{0,1},{1,2},{2,3},{3,4},{4,5},{5,6},{6,7},{7,0},{8,9},{9,10},{10,1... | collective-permute-start | bytes 393224 | tf_op jit(solution)/shard_map/ppermute | solution.py:102
  48.8 5.5 %collective-permute-start.12 = (bf16[128,512]{1,0:T(8,128)(2,1)S(1)}, bf16[128,512]{1,0:T(8,128)(2,1)}, u32[]{:S(2)}, u32[]{:S(2)}) collective-permute-start(bf16[128,512]{1,0:T(8,128)(2,1)S(1)} %collective-permute-done.11.refs_2_), channel_id=1, source_target_pairs={{0,7},{1,0},{2,1},{3,2},{4,3},{5,4},{6,5},{7,6},{8,15},{9,8},{10,9... | collective-permute-start | bytes 393224 | tf_op jit(solution)/shard_map/ppermute | solution.py:102
  54.4 6.3 %collective-permute-start.9 = (bf16[128,512]{1,0:T(8,128)(2,1)S(1)}, bf16[128,512]{1,0:T(8,128)(2,1)}, u32[]{:S(2)}, u32[]{:S(2)}) collective-permute-start(bf16[128,512]{1,0:T(8,128)(2,1)S(1)} %collective-permute-done.8.refs_3_), channel_id=1, source_target_pairs={{0,1},{1,2},{2,3},{3,4},{4,5},{5,6},{6,7},{7,0},{8,9},{9,10},{10,1... | collective-permute-start | bytes 393224 | tf_op jit(solution)/shard_map/ppermute | solution.py:102
  55.0 10.1 %collective-permute-start.13 = (bf16[128,512]{1,0:T(8,128)(2,1)}, bf16[128,512]{1,0:T(8,128)(2,1)}, u32[]{:S(2)}, u32[]{:S(2)}) collective-permute-start(bf16[128,512]{1,0:T(8,128)(2,1)} %collective-permute-done.12.refs_4_), channel_id=1, source_target_pairs={{0,7},{1,0},{2,1},{3,2},{4,3},{5,4},{6,5},{7,6},{8,15},{9,8},{10,9... | collective-permute-start | bytes 393224 | tf_op jit(solution)/shard_map/ppermute | solution.py:102
  60.6 7.0 %collective-permute-start.10 = (bf16[128,512]{1,0:T(8,128)(2,1)}, bf16[128,512]{1,0:T(8,128)(2,1)}, u32[]{:S(2)}, u32[]{:S(2)}) collective-permute-start(bf16[128,512]{1,0:T(8,128)(2,1)} %collective-permute-done.9.refs_5_), channel_id=1, source_target_pairs={{0,1},{1,2},{2,3},{3,4},{4,5},{5,6},{6,7},{7,0},{8,9},{9,10},{10,1... | collective-permute-start | bytes 393224 | tf_op jit(solution)/shard_map/ppermute | solution.py:102
  77.0 36.9 %all-to-all-start.1 = ((bf16[64,128,128]{2,1,0:T(8,128)(2,1)}), bf16[64,128,128]{2,1,0:T(8,128)(2,1)}, u32[]{:S(2)}, u32[]{:S(2)}) async-start(bf16[64,128,128]{2,1,0:T(8,128)(2,1)} %get-tuple-element.65), calls=%async_computation.1 | async-start | bytes 4194304 | tf_op jit(solution)/shard_map/all_to_all | solution.py:660
  84.5 10.0 %collective-permute-start.14 = (bf16[256,512]{1,0:T(8,128)(2,1)S(1)}, bf16[256,512]{1,0:T(8,128)(2,1)}, u32[]{:S(2)}, u32[]{:S(2)}) collective-permute-start(bf16[256,512]{1,0:T(8,128)(2,1)S(1)} %copy-done.1), channel_id=1, source_target_pairs={{0,1},{1,2},{2,3},{3,4},{4,5},{5,6},{6,7},{7,0},{8,9},{9,10},{10,1... | collective-permute-start | bytes 786440 | tf_op jit(solution)/shard_map/ppermute | solution.py:102
  84.6 9.9 %collective-permute-start.16 = (bf16[256,512]{1,0:T(8,128)(2,1)S(1)}, bf16[256,512]{1,0:T(8,128)(2,1)}, u32[]{:S(2)}, u32[]{:S(2)}) collective-permute-start(bf16[256,512]{1,0:T(8,128)(2,1)S(1)} %copy-done.1), channel_id=1, source_target_pairs={{0,7},{1,0},{2,1},{3,2},{4,3},{5,4},{6,5},{7,6},{8,15},{9,8},{10,9... | collective-permute-start | bytes 786440 | tf_op jit(solution)/shard_map/ppermute | solution.py:102
  94.6 10.4 %collective-permute-start.15 = (bf16[256,512]{1,0:T(8,128)(2,1)}, bf16[256,512]{1,0:T(8,128)(2,1)}, u32[]{:S(2)}, u32[]{:S(2)}) collective-permute-start(bf16[256,512]{1,0:T(8,128)(2,1)} %collective-permute-done.14.refs_6_), channel_id=1, source_target_pairs={{0,1},{1,2},{2,3},{3,4},{4,5},{5,6},{6,7},{7,0},{8,9},{9,10},{10,1... | collective-permute-start | bytes 786440 | tf_op jit(solution)/shard_map/ppermute | solution.py:102
  94.6 10.4 %collective-permute-start.17 = (bf16[256,512]{1,0:T(8,128)(2,1)}, bf16[256,512]{1,0:T(8,128)(2,1)}, u32[]{:S(2)}, u32[]{:S(2)}) collective-permute-start(bf16[256,512]{1,0:T(8,128)(2,1)} %collective-permute-done.16.refs_12_), channel_id=1, source_target_pairs={{0,7},{1,0},{2,1},{3,2},{4,3},{5,4},{6,5},{7,6},{8,15},{9,8},{10,9... | collective-permute-start | bytes 786440 | tf_op jit(solution)/shard_map/ppermute | solution.py:102
  105.0 8.9 %collective-permute-start.18 = (bf16[256,512]{1,0:T(8,128)(2,1)}, bf16[256,512]{1,0:T(8,128)(2,1)}, u32[]{:S(2)}, u32[]{:S(2)}) collective-permute-start(bf16[256,512]{1,0:T(8,128)(2,1)} %collective-permute-done.15.refs_7_), channel_id=1, source_target_pairs={{0,1},{1,2},{2,3},{3,4},{4,5},{5,6},{6,7},{7,0},{8,9},{9,10},{10,1... | collective-permute-start | bytes 786440 | tf_op jit(solution)/shard_map/ppermute | solution.py:102
  105.1 8.8 %collective-permute-start.19 = (bf16[256,512]{1,0:T(8,128)(2,1)}, bf16[256,512]{1,0:T(8,128)(2,1)}, u32[]{:S(2)}, u32[]{:S(2)}) collective-permute-start(bf16[256,512]{1,0:T(8,128)(2,1)} %collective-permute-done.17.refs_11_), channel_id=1, source_target_pairs={{0,7},{1,0},{2,1},{3,2},{4,3},{5,4},{6,5},{7,6},{8,15},{9,8},{10,9... | collective-permute-start | bytes 786440 | tf_op jit(solution)/shard_map/ppermute | solution.py:102
  118.0 17.2 %collective-permute-start.20 = (bf16[2,256,128]{2,1,0:T(8,128)(2,1)}, bf16[2,256,128]{2,1,0:T(8,128)(2,1)S(1)}, u32[]{:S(2)}, u32[]{:S(2)}) collective-permute-start(bf16[2,256,128]{2,1,0:T(8,128)(2,1)} %get-tuple-element.80), channel_id=1, source_target_pairs={{0,2},{1,3},{2,4},{3,5},{4,6},{5,7},{6,0},{7,1},{8,10},{9,11},{10,... | collective-permute-start | bytes 393224 | tf_op jit(solution)/shard_map/ppermute | solution.py:102
  120.3 14.9 %collective-permute-start.21 = (bf16[2,256,128]{2,1,0:T(8,128)(2,1)}, bf16[2,256,128]{2,1,0:T(8,128)(2,1)S(1)}, u32[]{:S(2)}, u32[]{:S(2)}) collective-permute-start(bf16[2,256,128]{2,1,0:T(8,128)(2,1)} %get-tuple-element.81), channel_id=1, source_target_pairs={{0,4},{1,5},{2,6},{3,7},{4,0},{5,1},{6,2},{7,3},{8,12},{9,13},{10,... | collective-permute-start | bytes 393224 | tf_op jit(solution)/shard_map/ppermute | solution.py:102
  122.5 12.7 %collective-permute-start.22 = (bf16[2,256,128]{2,1,0:T(8,128)(2,1)}, bf16[2,256,128]{2,1,0:T(8,128)(2,1)S(1)}, u32[]{:S(2)}, u32[]{:S(2)}) collective-permute-start(bf16[2,256,128]{2,1,0:T(8,128)(2,1)} %get-tuple-element.82), channel_id=1, source_target_pairs={{0,6},{1,7},{2,0},{3,1},{4,2},{5,3},{6,4},{7,5},{8,14},{9,15},{10,... | collective-permute-start | bytes 393224 | tf_op jit(solution)/shard_map/ppermute | solution.py:102
  126.5 15.1 %all-to-all-start.2 = ((bf16[32,8,512]{2,1,0:T(8,128)(2,1)}), bf16[32,8,512]{2,1,0:T(8,128)(2,1)S(1)}, u32[]{:S(2)}, u32[]{:S(2)}) async-start(bf16[32,8,512]{2,1,0:T(8,128)(2,1)} %bitcast.7), calls=%async_computation.2 | async-start | bytes 524288 | tf_op jit(solution)/shard_map/all_to_all | solution.py:701
  134.8 13.3 %collective-permute-start.24 = (bf16[256,512]{1,0:T(8,128)(2,1)}, bf16[256,512]{1,0:T(8,128)(2,1)}, u32[]{:S(2)}, u32[]{:S(2)}) collective-permute-start(bf16[256,512]{1,0:T(8,128)(2,1)} %collective-permute-done.18.refs_8_), channel_id=1, source_target_pairs={{0,1},{1,2},{2,3},{3,4},{4,5},{5,6},{6,7},{7,0},{8,9},{9,10},{10,1... | collective-permute-start | bytes 786440 | tf_op jit(solution)/shard_map/ppermute | solution.py:102
  135.3 12.8 %collective-permute-start.23 = (bf16[4,256,128]{2,1,0:T(8,128)(2,1)S(1)}, bf16[4,256,128]{2,1,0:T(8,128)(2,1)}, u32[]{:S(2)}, u32[]{:S(2)}) collective-permute-start(bf16[4,256,128]{2,1,0:T(8,128)(2,1)S(1)} %pad_maximum_fusion.1), channel_id=1, source_target_pairs={{0,1},{1,0},{2,3},{3,2},{4,5},{5,4},{6,7},{7,6},{8,9},{9,8},{10,11... | collective-permute-start | bytes 786440 | tf_op jit(solution)/shard_map/ppermute | solution.py:110
  142.4 13.5 %all-to-all-start.3 = ((bf16[32,8,512]{2,1,0:T(8,128)(2,1)}), bf16[32,8,512]{2,1,0:T(8,128)(2,1)}, u32[]{:S(2)}, u32[]{:S(2)}) async-start(bf16[32,8,512]{2,1,0:T(8,128)(2,1)} %sum_shares.1), calls=%async_computation.3 | async-start | bytes 524288 | tf_op jit(solution)/shard_map/all_to_all | solution.py:712
  (10 other events, 43.6 us)

commit v5 on v4

--- a/solution.py
+++ b/solution.py
@@ -468,6 +468,19 @@
     wait_all(stores)
 
 
+def pack_body(*refs):
+    *pair_ins, _, pack_out, pack_ref, in_sems, out_sems = refs
+    loads = copies([pair.at[1] for pair in pair_ins], [pack_ref.at[j] for j in range(NB // 2)], in_sems)
+    stores = copies(
+        [pack_ref.at[j] for j in range(NB // 2)], [pack_out.at[j] for j in range(NB // 2)], out_sems
+    )
+    start_all(loads)
+    for load, store in zip(loads, stores, strict=True):
+        load.wait()
+        store.start()
+    wait_all(stores)
+
+
 def sum_body(share_ref, total_ref):
     total = jnp.sum(share_ref[...].astype(F32), axis=0).astype(BF16)
     total_ref[...] = jnp.broadcast_to(total[None], total_ref.shape)
@@ -479,34 +492,57 @@
     out_ref[...] = total[3 * HD :]
 
 
-def finish_body(col_ref, *refs):
+def head_terms(piece, weight):
+    terms = piece.astype(F32).T.astype(BF16)
+    return dot(terms[:, 3 * HD :], weight[3 * HD :, :]), dot(terms[:, : 3 * HD], weight[: 3 * HD, :])
+
+
+def first_heads_body(*refs):
+    n = NB // 2 - 1
+    pair_ins, weight_ins, refs = refs[:n], refs[n : 2 * n], refs[2 * n :]
+    sum_out, piece_ref, weight_ref, sum_ref, piece_sems, weight_sems, out_sems = refs
+    pieces = copies([pair.at[0] for pair in pair_ins], [piece_ref.at[j] for j in range(n)], piece_sems)
+    weights = copies(weight_ins, [weight_ref.at[j] for j in range(n)], weight_sems)
+    start_all(pieces)
+    start_all(weights)
+    out = jnp.zeros((BLK, D), F32)
+    back = jnp.zeros((BLK, D), F32)
+    for j in range(n):
+        pieces[j].wait()
+        weights[j].wait()
+        out_term, back_term = head_terms(piece_ref[j], weight_ref[j])
+        out += out_term
+        back += back_term
+    sum_ref[0], sum_ref[1] = out, back
+    store = pltpu.make_async_copy(sum_ref, sum_out, out_sems.at[0])
+    store.start()
+    store.wait()
+
+
+def finish_body(col_ref, sum_in, pair_in, beside_in, *refs):
     half = NB // 2
-    pair_ins, beside_in, weight_ins, refs = refs[:half], refs[half], refs[half + 1 : half + 1 + NB], refs[half + 1 + NB :]
+    weight_ins, refs = refs[: half + 1], refs[half + 1 :]
     state_in, grad_in, gain_in, layer_out, back_out, *refs = refs
-    piece_ref, weight_ref, state_ref, grad_ref, gain_ref, layer_ref, back_ref, *refs = refs
+    sum_ref, pair_ref, piece_ref, weight_ref, state_ref, grad_ref, gain_ref, layer_ref, back_ref, *refs = refs
     piece_sems, weight_sems, in_sems, out_sems = refs
-    pieces = copies(
-        [*(pair.at[0] for pair in pair_ins), beside_in],
-        [*(piece_ref.at[0, j] for j in range(half)), piece_ref.at[1]],
-        piece_sems,
-    )
-    weights = copies(weight_ins, [weight_ref.at[k] for k in range(NB)], weight_sems)
-    loads = copies([state_in, grad_in, gain_in], [state_ref, grad_ref, gain_ref], in_sems)
+    pieces = copies([pair_in.at[0], beside_in], [pair_ref, piece_ref], piece_sems)
+    weights = copies(weight_ins, [weight_ref.at[k] for k in range(half + 1)], weight_sems)
+    loads = copies([sum_in, state_in, grad_in, gain_in], [sum_ref, state_ref, grad_ref, gain_ref], in_sems)
     start_all(pieces)
     start_all(weights)
     start_all(loads)
     wait_all(pieces)
     wait_all(weights)
     odd_place = lax.rem(col_ref[0], 2)
-    out = jnp.zeros((BLK, D), F32)
-    back = jnp.zeros((BLK, D), F32)
+    out, back = head_terms(pair_ref[...], weight_ref[half])
     for j in range(half):
-        beside = jnp.where(odd_place == 1, (2 * j + 1) % NB, (2 * j + NB - 1) % NB)
-        for own, head in ((0, 2 * j), (1, beside)):
-            terms = piece_ref[own, j].astype(F32).T.astype(BF16)
-            back += dot(terms[:, : 3 * HD], weight_ref[head, : 3 * HD, :])
-            out += dot(terms[:, 3 * HD :], weight_ref[head, 3 * HD :, :])
+        beside = jnp.where(odd_place == 1, j, (j + half - 1) % half)
+        out_term, back_term = head_terms(piece_ref[j], weight_ref[beside])
+        out += out_term
+        back += back_term
     wait_all(loads)
+    out += sum_ref[0]
+    back += sum_ref[1]
     state = state_ref[...].astype(F32)
     gain = gain_ref[...]
     layer_ref[...] = (state + out).astype(BF16)
@@ -699,8 +735,8 @@
 
     share_rows = 4 * HD // doms
     shares = lax.all_to_all(part.reshape(doms, share_rows, D), "dom", 0, 0, tiled=True)
+    *pairs, w4 = lax.optimization_barrier((*pairs, w4))
     pairs = [pairs[0], *(shifted(pairs[j], 2 * j) for j in range(1, half))]
-    beside = paired(jnp.stack([pair[1] for pair in pairs]))
     (totals,) = call(
         sum_body,
         (shaped(doms, share_rows, D),),
@@ -710,27 +746,49 @@
         limit=4,
     )(shares)
     total = lax.all_to_all(totals, "dom", 0, 0, tiled=True).reshape(4 * HD, D)
-    weights = (weights_own, w1, w2, w3, w4, w5, w6, w7)
+    packed = shaped(half, 4 * HD, BLK)
+    (beside,) = call(
+        pack_body,
+        (packed,),
+        [left()] * (half + 1),
+        scratch=[*held(packed), dma_sems(half), dma_sems(half)],
+        name="pack",
+    )(*pairs, totals)
+    beside = paired(beside)
+    sums, piece, weight = shaped(2, BLK, D, kind=F32), shaped(4 * HD, BLK), shaped(4 * HD, D)
+    (first,) = call(
+        first_heads_body,
+        (sums,),
+        [left()] * (2 * half - 2),
+        scratch=[
+            *held(shaped(half - 1, 4 * HD, BLK), shaped(half - 1, 4 * HD, D), sums),
+            dma_sems(half - 1),
+            dma_sems(half - 1),
+            dma_sems(1),
+        ],
+        flops=unit // 100,
+        name="first_heads",
+    )(pairs[0], pairs[1], pairs[3], weights_own, w2, w6)
     layer_out, state_grad = call(
         finish_body,
         (node, node),
-        [scalars()] + [left()] * (half + 1 + NB + 3),
+        [scalars()] + [left()] * (3 + half + 1 + 3),
         scratch=[
-            *held(shaped(2, half, 4 * HD, BLK), shaped(NB, 4 * HD, D), node, node, row, node, node),
+            *held(sums, piece, packed, shaped(half + 1, 4 * HD, D), node, node, row, node, node),
+            dma_sems(2),
             dma_sems(half + 1),
-            dma_sems(NB),
-            dma_sems(3),
+            dma_sems(4),
             dma_sems(2),
         ],
-        flops=2 * BLK * D * 2048,
+        flops=unit // 100,
         name="finish",
-    )(col, *pairs, beside, *weights, node_states, out_grad, gain)
-    total, layer_out, state_grad = lax.optimization_barrier((total, layer_out, state_grad))
+    )(col, first, pairs[2], beside, w1, w3, w5, w7, w4, node_states, out_grad, gain)
     qkv_grad, out_weight_grad = call(
         functools.partial(scale_body, 1.0 / math.sqrt(far_owner.shape[0] * BLK)),
         (shaped(3 * HD, D, kind=F32), shaped(HD, D, kind=F32)),
         [whole()],
         out_specs=[whole()] * 2,
+        flops=3 * unit,
         name="scale",
         limit=4,
     )(total)

time: 161 us -> 159 us (0.988); the launches traced: 158 us -> 159 us
  waiting for transfers between devices: 39.7 us -> 34.2 us
  Pallas kernels: 42.7 us -> 46.6 us
  starting transfers between devices: 69.5 us -> 72.8 us
    all_to_all x1, waiting for transfers between devices: 5.41 us -> 0.01 us  [shards(): lax.all_to_all(part.reshape(doms, share_rows, D), 'dom', 0, 0, tiled=True)]
    all_to_all x1, waiting for transfers between devices: 3.95 us -> 0.01 us  [shards(): total = lax.all_to_all(totals, 'dom', 0, 0, tiled=True).reshape(4 * HD, D)]
    pallas_call x1 -> x3, Pallas kernels: 3.87 us -> 7.74 us  [the longest x1 3.45 us: shards(): call(finish_body, (node, node), [scalars()] + [left()] * (3 + half + 1 +...]
    ppermute x24, waiting for transfers between devices: 30.4 us -> 32.3 us  [shifted(): return lax.ppermute(x, 'col', [(i, (i + k) % NB) for i in range(NB)])]
    ppermute x1, waiting for transfers between devices: 0.01 us -> 1.88 us  [paired(): return lax.ppermute(x, 'col', [(i, i ^ 1) for i in range(NB)])]
    all_to_all x1, starting transfers between devices: 5.68 us -> 7.43 us  [shards(): total = lax.all_to_all(totals, 'dom', 0, 0, tiled=True).reshape(4 * HD, D)]
  transfers between devices with their start and end apart: 29 -> 29, of which waited for: 11 -> 12; matrix products, arithmetic and copies ran while one was open for 1% -> 1% of each run, Pallas kernels for 16% -> 20%
where the time goes in v5:
time: 159 us
  starting transfers between devices  72.8 us (46%)
  Pallas kernels  46.6 us (29%)
  waiting for transfers between devices  34.2 us (22%)
  local copies, waits for them, and re-layouts  2.62 us (2%)
    ppermute x24, starting transfers between devices, shifted(): return lax.ppermute(x, 'col', [(i, (i + k) % NB) for i in range(NB)])  40.1 us
    ppermute x24, waiting for transfers between devices, shifted(): return lax.ppermute(x, 'col', [(i, (i + k) % NB) for i in range(NB)])  32.3 us
    all_to_all x1, starting transfers between devices, shards(): fetched = lax.all_to_all(outgoing, 'dom', 0, 0, tiled=True)  7.82 us
    all_to_all x1, starting transfers between devices, shards(): returned = lax.all_to_all(outgoing_back, 'dom', 0, 0, tiled=True)  7.56 us
    pallas_call x1, Pallas kernels, shards(): call(far_body, (across, blocks, blocks_float, exchanged), [scalars()] * 2...  7.55 us
    all_to_all x1, starting transfers between devices, shards(): total = lax.all_to_all(totals, 'dom', 0, 0, tiled=True).reshape(4 * HD, D)  7.43 us
    all_to_all x1, starting transfers between devices, shards(): lax.all_to_all(part.reshape(doms, share_rows, D), 'dom', 0, 0, tiled=True)  7.39 us
    pallas_call x1, Pallas kernels, shards(): call(near_backward_body, (across, blocks_float, shaped(2 * HD, D), states...  7.22 us
  transfers between devices with their start and end apart: 29, of which 12 were waited for; matrix products, arithmetic and copies ran while one was open for 1% of the time, Pallas kernels for 20%

profile of v5, /device:TPU:2, one launch (start us, length us, event | category | flops | bytes accessed | tf_op | source)
XLA Modules:
  0.0 158.7 jit_solution(12898177245881453756)
XLA Ops:
  2.6 4.0 %collective-permute-start.1 = (bf16[128,512]{1,0:T(8,128)(2,1)}, bf16[128,512]{1,0:T(8,128)(2,1)}, u32[]{:S(2)}, u32[]{:S(2)}) collective-permute-start(bf16[128,512]{1,0:T(8,128)(2,1)} %refs_5_.1), channel_id=1, source_target_pairs={{0,7},{1,0},{2,1},{3,2},{4,3},{5,4},{6,5},{7,6},{8,15},{9,8},{10,9... | collective-permute-start | bytes 393224 | tf_op jit(solution)/shard_map/ppermute | solution.py:102
  10.4 3.2 %collective-permute-start.5 = (bf16[128,512]{1,0:T(8,128)(2,1)}, bf16[128,512]{1,0:T(8,128)(2,1)S(1)}, u32[]{:S(2)}, u32[]{:S(2)}) collective-permute-start(bf16[128,512]{1,0:T(8,128)(2,1)} %collective-permute-done.1.refs_2_.refs_10_), channel_id=1, source_target_pairs={{0,7},{1,0},{2,1},{3,2},{4,3},{5,4},{6,5},{7,6},{8,15},{9,8},{10,9... | collective-permute-start | bytes 393224 | tf_op jit(solution)/shard_map/ppermute | solution.py:102
  13.6 3.2 %collective-permute-done.2.refs_3_.refs_11_ = bf16[128,512]{1,0:T(8,128)(2,1)S(1)} collective-permute-done((bf16[128,512]{1,0:T(8,128)(2,1)}, bf16[128,512]{1,0:T(8,128)(2,1)S(1)}, u32[]{:S(2)}, u32[]{:S(2)}) %collective-permute-start.2) | collective-permute-done | bytes 131104 | tf_op jit(solution)/shard_map/ppermute | solution.py:102
  17.4 3.2 %collective-permute-start.6 = (bf16[128,512]{1,0:T(8,128)(2,1)S(1)}, bf16[128,512]{1,0:T(8,128)(2,1)S(1)}, u32[]{:S(2)}, u32[]{:S(2)}) collective-permute-start(bf16[128,512]{1,0:T(8,128)(2,1)S(1)} %collective-permute-done.5.refs_4_.refs_12_), channel_id=1, source_target_pairs={{0,7},{1,0},{2,1},{3,2},{4,3},{5,4},{6,5},{7,6},{8,15},{9,8},{10,9... | collective-permute-start | bytes 393224 | tf_op jit(solution)/shard_map/ppermute | solution.py:102
  20.7 3.0 %collective-permute-done.3.refs_5_.refs_13_ = bf16[128,512]{1,0:T(8,128)(2,1)} collective-permute-done((bf16[128,512]{1,0:T(8,128)(2,1)S(1)}, bf16[128,512]{1,0:T(8,128)(2,1)}, u32[]{:S(2)}, u32[]{:S(2)}) %collective-permute-start.3) | collective-permute-done | bytes 131104 | tf_op jit(solution)/shard_map/ppermute | solution.py:102
  24.4 4.5 %project_most.1 = (bf16[8,128,128]{2,1,0:T(8,128)(2,1)}, bf16[8,128,128]{2,1,0:T(8,128)(2,1)}, bf16[64,128,128]{2,1,0:T(8,128)(2,1)}) custom-call(s32[2,256]{1,0:T(2,128)} %get-tuple-element.53.send_ref.home_ref, bf16[128,512]{1,0:T(8,128)(2,1)} %refs_5_.1, bf16[128,512]{1,0:T(8,128)(2,1)} %collective-permute-done.refs_1_.refs_9_, ...), custom_call_target="tpu_custom_call" | custom-call | flops 268435456 | bytes 1048576 | tf_op jit(solution)/shard_map/project_most/pallas_call | solution.py:607
  30.2 3.3 %project_last.1 = (bf16[8,128,128]{2,1,0:T(8,128)(2,1)}, bf16[8,128,128]{2,1,0:T(8,128)(2,1)}, bf16[64,128,128]{2,1,0:T(8,128)(2,1)}) custom-call(s32[2,256]{1,0:T(2,128)} %get-tuple-element.53.send_ref.home_ref, bf16[128,512]{1,0:T(8,128)(2,1)} %collective-permute-done.4.chunk_in.refs_15_, ...), custom_call_target="tpu_custom_call", output_to_operand_aliasing={{0}: (4, {}), {1}: (5, {}), {2}: (6, {})} | custom-call | flops 33554432 | bytes 1048576 | tf_op jit(solution)/shard_map/project_last/pallas_call | solution.py:620
  33.5 7.8 %all-to-all-start = ((bf16[64,128,128]{2,1,0:T(8,128)(2,1)}), bf16[64,128,128]{2,1,0:T(8,128)(2,1)}, u32[]{:S(2)}, u32[]{:S(2)}) async-start(bf16[64,128,128]{2,1,0:T(8,128)(2,1)} %get-tuple-element.62), calls=%async_computation | async-start | bytes 4194304 | tf_op jit(solution)/shard_map/all_to_all | solution.py:636
  41.9 2.8 %collective-permute-start.11 = (bf16[128,512]{1,0:T(8,128)(2,1)S(1)}, bf16[128,512]{1,0:T(8,128)(2,1)S(1)}, u32[]{:S(2)}, u32[]{:S(2)}) collective-permute-start(bf16[128,512]{1,0:T(8,128)(2,1)S(1)} %copy-done.3), channel_id=1, source_target_pairs={{0,7},{1,0},{2,1},{3,2},{4,3},{5,4},{6,5},{7,6},{8,15},{9,8},{10,9... | collective-permute-start | bytes 393224 | tf_op jit(solution)/shard_map/ppermute | solution.py:102
  44.7 3.5 %collective-permute-done.7.refs_1_ = bf16[128,512]{1,0:T(8,128)(2,1)S(1)} collective-permute-done((bf16[128,512]{1,0:T(8,128)(2,1)S(1)}, bf16[128,512]{1,0:T(8,128)(2,1)S(1)}, u32[]{:S(2)}, u32[]{:S(2)}) %collective-permute-start.7) | collective-permute-done | bytes 131104 | tf_op jit(solution)/shard_map/ppermute | solution.py:102
  48.8 2.7 %collective-permute-start.12 = (bf16[128,512]{1,0:T(8,128)(2,1)S(1)}, bf16[128,512]{1,0:T(8,128)(2,1)}, u32[]{:S(2)}, u32[]{:S(2)}) collective-permute-start(bf16[128,512]{1,0:T(8,128)(2,1)S(1)} %collective-permute-done.11.refs_2_), channel_id=1, source_target_pairs={{0,7},{1,0},{2,1},{3,2},{4,3},{5,4},{6,5},{7,6},{8,15},{9,8},{10,9... | collective-permute-start | bytes 393224 | tf_op jit(solution)/shard_map/ppermute | solution.py:102
  51.5 2.9 %collective-permute-done.8.refs_3_ = bf16[128,512]{1,0:T(8,128)(2,1)S(1)} collective-permute-done((bf16[128,512]{1,0:T(8,128)(2,1)S(1)}, bf16[128,512]{1,0:T(8,128)(2,1)S(1)}, u32[]{:S(2)}, u32[]{:S(2)}) %collective-permute-start.8) | collective-permute-done | bytes 131104 | tf_op jit(solution)/shard_map/ppermute | solution.py:102
  55.0 2.8 %collective-permute-start.13 = (bf16[128,512]{1,0:T(8,128)(2,1)}, bf16[128,512]{1,0:T(8,128)(2,1)}, u32[]{:S(2)}, u32[]{:S(2)}) collective-permute-start(bf16[128,512]{1,0:T(8,128)(2,1)} %collective-permute-done.12.refs_4_), channel_id=1, source_target_pairs={{0,7},{1,0},{2,1},{3,2},{4,3},{5,4},{6,5},{7,6},{8,15},{9,8},{10,9... | collective-permute-start | bytes 393224 | tf_op jit(solution)/shard_map/ppermute | solution.py:102
  57.8 2.9 %collective-permute-done.9.refs_5_ = bf16[128,512]{1,0:T(8,128)(2,1)} collective-permute-done((bf16[128,512]{1,0:T(8,128)(2,1)S(1)}, bf16[128,512]{1,0:T(8,128)(2,1)}, u32[]{:S(2)}, u32[]{:S(2)}) %collective-permute-start.9) | collective-permute-done | bytes 131104 | tf_op jit(solution)/shard_map/ppermute | solution.py:102
  61.4 3.7 %near_forward.1.num_in = f32[8,128,128]{2,1,0:T(8,128)} custom-call(s32[1]{0:T(128)} %bitcast.col_ref, bf16[8,128,128]{2,1,0:T(8,128)(2,1)} %get-tuple-element.60.query_in.refs_17_, bf16[8,128,128]{2,1,0:T(8,128)(2,1)} %get-tuple-element.63.kv_in.refs_18_, f32[8,1024]{1,0:T(8,128)} %get-tuple-element.64.count_in.refs_19_), custom_call_target="tpu_custom_call" | custom-call | flops 536870912 | bytes 1048576 | tf_op jit(solution)/shard_map/near_forward/pallas_call | solution.py:656
  65.1 2.6 %attn_grad.1.ag_in = f32[8,128,128]{2,1,0:T(8,128)} custom-call(bf16[128,512]{1,0:T(8,128)(2,1)} %refs_6_.1, bf16[128,512]{1,0:T(8,128)(2,1)} %copy-done.7, bf16[128,512]{1,0:T(8,128)(2,1)} %copy-done.8, bf16[128,512]{1,0:T(8,128)(2,1)} %copy-done.9, bf16[128,512]{1,0:T(8,128)(2,1)} %collective-permute-done.12.refs_4_, ...), custom_call_target="tpu_custom_call" | custom-call | flops 134217728 | bytes 1048576 | tf_op jit(solution)/shard_map/attn_grad/pallas_call | solution.py:643
  69.4 7.5 %far_both.1 = (bf16[64,1024]{1,0:T(8,128)(2,1)}, bf16[8,128,128]{2,1,0:T(8,128)(2,1)}, f32[8,128,128]{2,1,0:T(8,128)}, bf16[64,128,128]{2,1,0:T(8,128)(2,1)}) custom-call(s32[2]{0:T(128)} %pad_add_fusion.where_ref, s32[4,256]{1,0:T(4,128)} %get-tuple-element.54.place_ref, bf16[8,128,128]{2,1,0:T(8,128)(2,1)} %get-tuple-element.60.query_in.refs_17_, ...), custom_call_target="tpu_custom_call" | custom-call | flops 536870912 | bytes 1048576 | tf_op jit(solution)/shard_map/far_both/pallas_call | solution.py:675
  77.0 7.6 %all-to-all-start.1 = ((bf16[64,128,128]{2,1,0:T(8,128)(2,1)}), bf16[64,128,128]{2,1,0:T(8,128)(2,1)}, u32[]{:S(2)}, u32[]{:S(2)}) async-start(bf16[64,128,128]{2,1,0:T(8,128)(2,1)} %get-tuple-element.67), calls=%async_computation.1 | async-start | bytes 4194304 | tf_op jit(solution)/shard_map/all_to_all | solution.py:696
  84.7 3.3 %collective-permute-start.16 = (bf16[256,512]{1,0:T(8,128)(2,1)S(1)}, bf16[256,512]{1,0:T(8,128)(2,1)}, u32[]{:S(2)}, u32[]{:S(2)}) collective-permute-start(bf16[256,512]{1,0:T(8,128)(2,1)S(1)} %copy-done.1), channel_id=1, source_target_pairs={{0,7},{1,0},{2,1},{3,2},{4,3},{5,4},{6,5},{7,6},{8,15},{9,8},{10,9... | collective-permute-start | bytes 786440 | tf_op jit(solution)/shard_map/ppermute | solution.py:102
  87.9 6.6 %collective-permute-done.14.refs_0_ = bf16[256,512]{1,0:T(8,128)(2,1)} collective-permute-done((bf16[256,512]{1,0:T(8,128)(2,1)S(1)}, bf16[256,512]{1,0:T(8,128)(2,1)}, u32[]{:S(2)}, u32[]{:S(2)}) %collective-permute-start.14) | collective-permute-done | bytes 262176 | tf_op jit(solution)/shard_map/ppermute | solution.py:102
  94.6 3.2 %collective-permute-start.17 = (bf16[256,512]{1,0:T(8,128)(2,1)}, bf16[256,512]{1,0:T(8,128)(2,1)}, u32[]{:S(2)}, u32[]{:S(2)}) collective-permute-start(bf16[256,512]{1,0:T(8,128)(2,1)} %collective-permute-done.16.refs_3_), channel_id=1, source_target_pairs={{0,7},{1,0},{2,1},{3,2},{4,3},{5,4},{6,5},{7,6},{8,15},{9,8},{10,9... | collective-permute-start | bytes 786440 | tf_op jit(solution)/shard_map/ppermute | solution.py:102
  97.8 7.2 %near_backward.1 = (bf16[64,1024]{1,0:T(8,128)(2,1)}, f32[8,128,128]{2,1,0:T(8,128)}, bf16[128,512]{1,0:T(8,128)(2,1)}, bf16[8,128,512]{2,1,0:T(8,128)(2,1)}) custom-call(s32[1]{0:T(128)} %bitcast.col_ref, bf16[128,512]{1,0:T(8,128)(2,1)} %refs_6_.1, bf16[128,512]{1,0:T(8,128)(2,1)} %copy-done.7, bf16[128,512]{1,0:T(8,128)(2,1)} %copy-done.8, ...), custom_call_target="tpu_custom_call" | custom-call | flops 1342177280 | bytes 1048576 | tf_op jit(solution)/shard_map/near_backward/pallas_call | solution.py:700
  105.2 3.2 %collective-permute-start.19 = (bf16[256,512]{1,0:T(8,128)(2,1)}, bf16[256,512]{1,0:T(8,128)(2,1)}, u32[]{:S(2)}, u32[]{:S(2)}) collective-permute-start(bf16[256,512]{1,0:T(8,128)(2,1)} %collective-permute-done.17.refs_5_), channel_id=1, source_target_pairs={{0,7},{1,0},{2,1},{3,2},{4,3},{5,4},{6,5},{7,6},{8,15},{9,8},{10,9... | collective-permute-start | bytes 786440 | tf_op jit(solution)/shard_map/ppermute | solution.py:102
  108.4 5.5 %collective-permute-done.18.refs_1_ = bf16[256,512]{1,0:T(8,128)(2,1)} collective-permute-done((bf16[256,512]{1,0:T(8,128)(2,1)}, bf16[256,512]{1,0:T(8,128)(2,1)}, u32[]{:S(2)}, u32[]{:S(2)}) %collective-permute-start.18) | collective-permute-done | bytes 262176 | tf_op jit(solution)/shard_map/ppermute | solution.py:102
  114.7 4.1 %gather_grads.1 = (bf16[2,256,128]{2,1,0:T(8,128)(2,1)}, bf16[2,256,128]{2,1,0:T(8,128)(2,1)}, bf16[2,256,128]{2,1,0:T(8,128)(2,1)}, bf16[2,256,128]{2,1,0:T(8,128)(2,1)}, bf16[256,512]{1,0:T(8,128)(2,1)}) custom-call(s32[1]{0:T(128)} %bitcast.col_ref, s32[2,256]{1,0:T(2,128)} %get-tuple-element.53.send_ref.home_ref, ...), custom_call_target="tpu_custom_call" | custom-call | flops 134217728 | bytes 1048576 | tf_op jit(solution)/shard_map/gather_grads/pallas_call | solution.py:721
  118.8 7.4 %all-to-all-start.2 = ((bf16[32,8,512]{2,1,0:T(8,128)(2,1)}), bf16[32,8,512]{2,1,0:T(8,128)(2,1)S(1)}, u32[]{:S(2)}, u32[]{:S(2)}) async-start(bf16[32,8,512]{2,1,0:T(8,128)(2,1)} %bitcast.7), calls=%async_computation.2 | async-start | bytes 524288 | tf_op jit(solution)/shard_map/all_to_all | solution.py:737
  126.2 4.6 %collective-permute-start.21 = (bf16[2,256,128]{2,1,0:T(8,128)(2,1)}, bf16[2,256,128]{2,1,0:T(8,128)(2,1)}, u32[]{:S(2)}, u32[]{:S(2)}) collective-permute-start(bf16[2,256,128]{2,1,0:T(8,128)(2,1)} %get-tuple-element.86), channel_id=1, source_target_pairs={{0,2},{1,3},{2,4},{3,5},{4,6},{5,7},{6,0},{7,1},{8,10},{9,11},{10,... | collective-permute-start | bytes 393224 | tf_op jit(solution)/shard_map/ppermute | solution.py:102
  130.8 3.7 %collective-permute-start.23 = (bf16[2,256,128]{2,1,0:T(8,128)(2,1)}, bf16[2,256,128]{2,1,0:T(8,128)(2,1)}, u32[]{:S(2)}, u32[]{:S(2)}) collective-permute-start(bf16[2,256,128]{2,1,0:T(8,128)(2,1)} %get-tuple-element.88), channel_id=1, source_target_pairs={{0,4},{1,5},{2,6},{3,7},{4,0},{5,1},{6,2},{7,3},{8,12},{9,13},{10,... | collective-permute-start | bytes 393224 | tf_op jit(solution)/shard_map/ppermute | solution.py:102
  135.2 7.4 %all-to-all-start.3 = ((bf16[32,8,512]{2,1,0:T(8,128)(2,1)}), bf16[32,8,512]{2,1,0:T(8,128)(2,1)}, u32[]{:S(2)}, u32[]{:S(2)}) async-start(bf16[32,8,512]{2,1,0:T(8,128)(2,1)} %sum_shares.1.refs_4_), calls=%async_computation.3 | async-start | bytes 524288 | tf_op jit(solution)/shard_map/all_to_all | solution.py:748
  146.2 2.5 %collective-permute-start.24 = (bf16[4,256,128]{2,1,0:T(8,128)(2,1)}, bf16[4,256,128]{2,1,0:T(8,128)(2,1)}, u32[]{:S(2)}, u32[]{:S(2)}) collective-permute-start(bf16[4,256,128]{2,1,0:T(8,128)(2,1)} %pack.1), channel_id=1, source_target_pairs={{0,1},{1,0},{2,3},{3,2},{4,5},{5,4},{6,7},{7,6},{8,9},{9,8},{10,11... | collective-permute-start | bytes 786440 | tf_op jit(solution)/shard_map/ppermute | solution.py:110
  148.7 2.7 %first_heads.1.sum_in = f32[2,128,512]{2,1,0:T(8,128)} custom-call(bf16[2,256,128]{2,1,0:T(8,128)(2,1)} %get-tuple-element.85.refs_0_, bf16[2,256,128]{2,1,0:T(8,128)(2,1)} %collective-permute-done.21.refs_1_, bf16[2,256,128]{2,1,0:T(8,128)(2,1)} %collective-permute-done.22.refs_2_.refs_3_, bf16[256,512]{1,0:T(8,128)(2,1)} %pad_maximum_fusion.refs_3_, ...), custom_call_target="tpu_custom_call" | custom-call | flops 2684354 | bytes 1048576 | tf_op jit(solution)/shard_map/first_heads/pallas_call | solution.py:759
  155.0 3.4 %finish.1 = (bf16[128,512]{1,0:T(8,128)(2,1)}, bf16[128,512]{1,0:T(8,128)(2,1)}) custom-call(s32[1]{0:T(128)} %bitcast.col_ref, f32[2,128,512]{2,1,0:T(8,128)} %first_heads.1.sum_in, bf16[2,256,128]{2,1,0:T(8,128)(2,1)} %collective-permute-done.23.refs_2_.pair_in, bf16[4,256,128]{2,1,0:T(8,128)(2,1)} %collective-permute-done.24.beside_in, ...), custom_call_target="tpu_custom_call" | custom-call | flops 2684354 | bytes 1048576 | tf_op jit(solution)/shard_map/finish/pallas_call | solution.py:772
  (62 shorter events, 21.6 us)
Async XLA Ops:
  0.6 9.7 %collective-permute-start = (bf16[128,512]{1,0:T(8,128)(2,1)}, bf16[128,512]{1,0:T(8,128)(2,1)}, u32[]{:S(2)}, u32[]{:S(2)}) collective-permute-start(bf16[128,512]{1,0:T(8,128)(2,1)} %refs_5_.1), channel_id=1, source_target_pairs={{0,1},{1,2},{2,3},{3,4},{4,5},{5,6},{6,7},{7,0},{8,9},{9,10},{10,1... | collective-permute-start | bytes 393224 | tf_op jit(solution)/shard_map/ppermute | solution.py:102
  2.6 7.8 %collective-permute-start.1 = (bf16[128,512]{1,0:T(8,128)(2,1)}, bf16[128,512]{1,0:T(8,128)(2,1)}, u32[]{:S(2)}, u32[]{:S(2)}) collective-permute-start(bf16[128,512]{1,0:T(8,128)(2,1)} %refs_5_.1), channel_id=1, source_target_pairs={{0,7},{1,0},{2,1},{3,2},{4,3},{5,4},{6,5},{7,6},{8,15},{9,8},{10,9... | collective-permute-start | bytes 393224 | tf_op jit(solution)/shard_map/ppermute | solution.py:102
  10.4 6.4 %collective-permute-start.2 = (bf16[128,512]{1,0:T(8,128)(2,1)}, bf16[128,512]{1,0:T(8,128)(2,1)S(1)}, u32[]{:S(2)}, u32[]{:S(2)}) collective-permute-start(bf16[128,512]{1,0:T(8,128)(2,1)} %collective-permute-done.refs_1_.refs_9_), channel_id=1, source_target_pairs={{0,1},{1,2},{2,3},{3,4},{4,5},{5,6},{6,7},{7,0},{8,9},{9,10},{10,1... | collective-permute-start | bytes 393224 | tf_op jit(solution)/shard_map/ppermute | solution.py:102
  10.4 7.0 %collective-permute-start.5 = (bf16[128,512]{1,0:T(8,128)(2,1)}, bf16[128,512]{1,0:T(8,128)(2,1)S(1)}, u32[]{:S(2)}, u32[]{:S(2)}) collective-permute-start(bf16[128,512]{1,0:T(8,128)(2,1)} %collective-permute-done.1.refs_2_.refs_10_), channel_id=1, source_target_pairs={{0,7},{1,0},{2,1},{3,2},{4,3},{5,4},{6,5},{7,6},{8,15},{9,8},{10,9... | collective-permute-start | bytes 393224 | tf_op jit(solution)/shard_map/ppermute | solution.py:102
  17.4 6.3 %collective-permute-start.3 = (bf16[128,512]{1,0:T(8,128)(2,1)S(1)}, bf16[128,512]{1,0:T(8,128)(2,1)}, u32[]{:S(2)}, u32[]{:S(2)}) collective-permute-start(bf16[128,512]{1,0:T(8,128)(2,1)S(1)} %collective-permute-done.2.refs_3_.refs_11_), channel_id=1, source_target_pairs={{0,1},{1,2},{2,3},{3,4},{4,5},{5,6},{6,7},{7,0},{8,9},{9,10},{10,1... | collective-permute-start | bytes 393224 | tf_op jit(solution)/shard_map/ppermute | solution.py:102
  17.4 6.3 %collective-permute-start.6 = (bf16[128,512]{1,0:T(8,128)(2,1)S(1)}, bf16[128,512]{1,0:T(8,128)(2,1)S(1)}, u32[]{:S(2)}, u32[]{:S(2)}) collective-permute-start(bf16[128,512]{1,0:T(8,128)(2,1)S(1)} %collective-permute-done.5.refs_4_.refs_12_), channel_id=1, source_target_pairs={{0,7},{1,0},{2,1},{3,2},{4,3},{5,4},{6,5},{7,6},{8,15},{9,8},{10,9... | collective-permute-start | bytes 393224 | tf_op jit(solution)/shard_map/ppermute | solution.py:102
  23.7 6.5 %collective-permute-start.4 = (bf16[128,512]{1,0:T(8,128)(2,1)}, bf16[128,512]{1,0:T(8,128)(2,1)}, u32[]{:S(2)}, u32[]{:S(2)}) collective-permute-start(bf16[128,512]{1,0:T(8,128)(2,1)} %collective-permute-done.3.refs_5_.refs_13_), channel_id=1, source_target_pairs={{0,1},{1,2},{2,3},{3,4},{4,5},{5,6},{6,7},{7,0},{8,9},{9,10},{10,1... | collective-permute-start | bytes 393224 | tf_op jit(solution)/shard_map/ppermute | solution.py:102
  33.5 7.9 %copy-start.3 = (bf16[128,512]{1,0:T(8,128)(2,1)S(1)}, bf16[128,512]{1,0:T(8,128)(2,1)}, u32[]{:S(2)}) copy-start(bf16[128,512]{1,0:T(8,128)(2,1)} %refs_6_.1) | copy-start | bytes 393220
  33.5 27.2 %copy-start = (bf16[192,512]{1,0:T(8,128)(2,1)S(1)}, bf16[192,512]{1,0:T(8,128)(2,1)}, u32[]{:S(2)}) copy-start(bf16[192,512]{1,0:T(8,128)(2,1)} %weight_in.2) | copy-start | bytes 589828
  33.5 27.2 %copy-start.2 = (bf16[64,512]{1,0:T(8,128)(2,1)S(1)}, bf16[64,512]{1,0:T(8,128)(2,1)}, u32[]{:S(2)}) copy-start(bf16[64,512]{1,0:T(8,128)(2,1)} %weight_in.3) | copy-start | bytes 196612
  33.5 35.9 %all-to-all-start = ((bf16[64,128,128]{2,1,0:T(8,128)(2,1)}), bf16[64,128,128]{2,1,0:T(8,128)(2,1)}, u32[]{:S(2)}, u32[]{:S(2)}) async-start(bf16[64,128,128]{2,1,0:T(8,128)(2,1)} %get-tuple-element.62), calls=%async_computation | async-start | bytes 4194304 | tf_op jit(solution)/shard_map/all_to_all | solution.py:636
  41.3 6.8 %collective-permute-start.7 = (bf16[128,512]{1,0:T(8,128)(2,1)S(1)}, bf16[128,512]{1,0:T(8,128)(2,1)S(1)}, u32[]{:S(2)}, u32[]{:S(2)}) collective-permute-start(bf16[128,512]{1,0:T(8,128)(2,1)S(1)} %copy-done.3), channel_id=1, source_target_pairs={{0,1},{1,2},{2,3},{3,4},{4,5},{5,6},{6,7},{7,0},{8,9},{9,10},{10,1... | collective-permute-start | bytes 393224 | tf_op jit(solution)/shard_map/ppermute | solution.py:102
  41.9 6.3 %collective-permute-start.11 = (bf16[128,512]{1,0:T(8,128)(2,1)S(1)}, bf16[128,512]{1,0:T(8,128)(2,1)S(1)}, u32[]{:S(2)}, u32[]{:S(2)}) collective-permute-start(bf16[128,512]{1,0:T(8,128)(2,1)S(1)} %copy-done.3), channel_id=1, source_target_pairs={{0,7},{1,0},{2,1},{3,2},{4,3},{5,4},{6,5},{7,6},{8,15},{9,8},{10,9... | collective-permute-start | bytes 393224 | tf_op jit(solution)/shard_map/ppermute | solution.py:102
  48.2 6.2 %collective-permute-start.8 = (bf16[128,512]{1,0:T(8,128)(2,1)S(1)}, bf16[128,512]{1,0:T(8,128)(2,1)S(1)}, u32[]{:S(2)}, u32[]{:S(2)}) collective-permute-start(bf16[128,512]{1,0:T(8,128)(2,1)S(1)} %collective-permute-done.7.refs_1_), channel_id=1, source_target_pairs={{0,1},{1,2},{2,3},{3,4},{4,5},{5,6},{6,7},{7,0},{8,9},{9,10},{10,1... | collective-permute-start | bytes 393224 | tf_op jit(solution)/shard_map/ppermute | solution.py:102
  48.8 5.5 %collective-permute-start.12 = (bf16[128,512]{1,0:T(8,128)(2,1)S(1)}, bf16[128,512]{1,0:T(8,128)(2,1)}, u32[]{:S(2)}, u32[]{:S(2)}) collective-permute-start(bf16[128,512]{1,0:T(8,128)(2,1)S(1)} %collective-permute-done.11.refs_2_), channel_id=1, source_target_pairs={{0,7},{1,0},{2,1},{3,2},{4,3},{5,4},{6,5},{7,6},{8,15},{9,8},{10,9... | collective-permute-start | bytes 393224 | tf_op jit(solution)/shard_map/ppermute | solution.py:102
  54.4 6.3 %collective-permute-start.9 = (bf16[128,512]{1,0:T(8,128)(2,1)S(1)}, bf16[128,512]{1,0:T(8,128)(2,1)}, u32[]{:S(2)}, u32[]{:S(2)}) collective-permute-start(bf16[128,512]{1,0:T(8,128)(2,1)S(1)} %collective-permute-done.8.refs_3_), channel_id=1, source_target_pairs={{0,1},{1,2},{2,3},{3,4},{4,5},{5,6},{6,7},{7,0},{8,9},{9,10},{10,1... | collective-permute-start | bytes 393224 | tf_op jit(solution)/shard_map/ppermute | solution.py:102
  55.0 10.0 %collective-permute-start.13 = (bf16[128,512]{1,0:T(8,128)(2,1)}, bf16[128,512]{1,0:T(8,128)(2,1)}, u32[]{:S(2)}, u32[]{:S(2)}) collective-permute-start(bf16[128,512]{1,0:T(8,128)(2,1)} %collective-permute-done.12.refs_4_), channel_id=1, source_target_pairs={{0,7},{1,0},{2,1},{3,2},{4,3},{5,4},{6,5},{7,6},{8,15},{9,8},{10,9... | collective-permute-start | bytes 393224 | tf_op jit(solution)/shard_map/ppermute | solution.py:102
  60.7 7.0 %collective-permute-start.10 = (bf16[128,512]{1,0:T(8,128)(2,1)}, bf16[128,512]{1,0:T(8,128)(2,1)}, u32[]{:S(2)}, u32[]{:S(2)}) collective-permute-start(bf16[128,512]{1,0:T(8,128)(2,1)} %collective-permute-done.9.refs_5_), channel_id=1, source_target_pairs={{0,1},{1,2},{2,3},{3,4},{4,5},{5,6},{6,7},{7,0},{8,9},{9,10},{10,1... | collective-permute-start | bytes 393224 | tf_op jit(solution)/shard_map/ppermute | solution.py:102
  77.0 36.9 %all-to-all-start.1 = ((bf16[64,128,128]{2,1,0:T(8,128)(2,1)}), bf16[64,128,128]{2,1,0:T(8,128)(2,1)}, u32[]{:S(2)}, u32[]{:S(2)}) async-start(bf16[64,128,128]{2,1,0:T(8,128)(2,1)} %get-tuple-element.67), calls=%async_computation.1 | async-start | bytes 4194304 | tf_op jit(solution)/shard_map/all_to_all | solution.py:696
  84.6 10.0 %collective-permute-start.14 = (bf16[256,512]{1,0:T(8,128)(2,1)S(1)}, bf16[256,512]{1,0:T(8,128)(2,1)}, u32[]{:S(2)}, u32[]{:S(2)}) collective-permute-start(bf16[256,512]{1,0:T(8,128)(2,1)S(1)} %copy-done.1), channel_id=1, source_target_pairs={{0,1},{1,2},{2,3},{3,4},{4,5},{5,6},{6,7},{7,0},{8,9},{9,10},{10,1... | collective-permute-start | bytes 786440 | tf_op jit(solution)/shard_map/ppermute | solution.py:102
  84.7 9.9 %collective-permute-start.16 = (bf16[256,512]{1,0:T(8,128)(2,1)S(1)}, bf16[256,512]{1,0:T(8,128)(2,1)}, u32[]{:S(2)}, u32[]{:S(2)}) collective-permute-start(bf16[256,512]{1,0:T(8,128)(2,1)S(1)} %copy-done.1), channel_id=1, source_target_pairs={{0,7},{1,0},{2,1},{3,2},{4,3},{5,4},{6,5},{7,6},{8,15},{9,8},{10,9... | collective-permute-start | bytes 786440 | tf_op jit(solution)/shard_map/ppermute | solution.py:102
  94.6 10.5 %collective-permute-start.15 = (bf16[256,512]{1,0:T(8,128)(2,1)}, bf16[256,512]{1,0:T(8,128)(2,1)}, u32[]{:S(2)}, u32[]{:S(2)}) collective-permute-start(bf16[256,512]{1,0:T(8,128)(2,1)} %collective-permute-done.14.refs_0_), channel_id=1, source_target_pairs={{0,1},{1,2},{2,3},{3,4},{4,5},{5,6},{6,7},{7,0},{8,9},{9,10},{10,1... | collective-permute-start | bytes 786440 | tf_op jit(solution)/shard_map/ppermute | solution.py:102
  94.6 10.5 %collective-permute-start.17 = (bf16[256,512]{1,0:T(8,128)(2,1)}, bf16[256,512]{1,0:T(8,128)(2,1)}, u32[]{:S(2)}, u32[]{:S(2)}) collective-permute-start(bf16[256,512]{1,0:T(8,128)(2,1)} %collective-permute-done.16.refs_3_), channel_id=1, source_target_pairs={{0,7},{1,0},{2,1},{3,2},{4,3},{5,4},{6,5},{7,6},{8,15},{9,8},{10,9... | collective-permute-start | bytes 786440 | tf_op jit(solution)/shard_map/ppermute | solution.py:102
  105.1 8.9 %collective-permute-start.18 = (bf16[256,512]{1,0:T(8,128)(2,1)}, bf16[256,512]{1,0:T(8,128)(2,1)}, u32[]{:S(2)}, u32[]{:S(2)}) collective-permute-start(bf16[256,512]{1,0:T(8,128)(2,1)} %collective-permute-done.15.refs_4_), channel_id=1, source_target_pairs={{0,1},{1,2},{2,3},{3,4},{4,5},{5,6},{6,7},{7,0},{8,9},{9,10},{10,1... | collective-permute-start | bytes 786440 | tf_op jit(solution)/shard_map/ppermute | solution.py:102
  105.2 8.8 %collective-permute-start.19 = (bf16[256,512]{1,0:T(8,128)(2,1)}, bf16[256,512]{1,0:T(8,128)(2,1)}, u32[]{:S(2)}, u32[]{:S(2)}) collective-permute-start(bf16[256,512]{1,0:T(8,128)(2,1)} %collective-permute-done.17.refs_5_), channel_id=1, source_target_pairs={{0,7},{1,0},{2,1},{3,2},{4,3},{5,4},{6,5},{7,6},{8,15},{9,8},{10,9... | collective-permute-start | bytes 786440 | tf_op jit(solution)/shard_map/ppermute | solution.py:102
  113.9 12.3 %collective-permute-start.20 = (bf16[256,512]{1,0:T(8,128)(2,1)}, bf16[256,512]{1,0:T(8,128)(2,1)}, u32[]{:S(2)}, u32[]{:S(2)}) collective-permute-start(bf16[256,512]{1,0:T(8,128)(2,1)} %collective-permute-done.18.refs_1_), channel_id=1, source_target_pairs={{0,1},{1,2},{2,3},{3,4},{4,5},{5,6},{6,7},{7,0},{8,9},{9,10},{10,1... | collective-permute-start | bytes 786440 | tf_op jit(solution)/shard_map/ppermute | solution.py:102
  118.8 15.6 %all-to-all-start.2 = ((bf16[32,8,512]{2,1,0:T(8,128)(2,1)}), bf16[32,8,512]{2,1,0:T(8,128)(2,1)S(1)}, u32[]{:S(2)}, u32[]{:S(2)}) async-start(bf16[32,8,512]{2,1,0:T(8,128)(2,1)} %bitcast.7), calls=%async_computation.2 | async-start | bytes 524288 | tf_op jit(solution)/shard_map/all_to_all | solution.py:737
  126.2 16.4 %collective-permute-start.21 = (bf16[2,256,128]{2,1,0:T(8,128)(2,1)}, bf16[2,256,128]{2,1,0:T(8,128)(2,1)}, u32[]{:S(2)}, u32[]{:S(2)}) collective-permute-start(bf16[2,256,128]{2,1,0:T(8,128)(2,1)} %get-tuple-element.86), channel_id=1, source_target_pairs={{0,2},{1,3},{2,4},{3,5},{4,6},{5,7},{6,0},{7,1},{8,10},{9,11},{10,... | collective-permute-start | bytes 393224 | tf_op jit(solution)/shard_map/ppermute | solution.py:102
  130.8 12.5 %collective-permute-start.22 = (bf16[2,256,128]{2,1,0:T(8,128)(2,1)}, bf16[2,256,128]{2,1,0:T(8,128)(2,1)}, u32[]{:S(2)}, u32[]{:S(2)}) collective-permute-start(bf16[2,256,128]{2,1,0:T(8,128)(2,1)} %get-tuple-element.87), channel_id=1, source_target_pairs={{0,6},{1,7},{2,0},{3,1},{4,2},{5,3},{6,4},{7,5},{8,14},{9,15},{10,... | collective-permute-start | bytes 393224 | tf_op jit(solution)/shard_map/ppermute | solution.py:102
  130.8 13.8 %collective-permute-start.23 = (bf16[2,256,128]{2,1,0:T(8,128)(2,1)}, bf16[2,256,128]{2,1,0:T(8,128)(2,1)}, u32[]{:S(2)}, u32[]{:S(2)}) collective-permute-start(bf16[2,256,128]{2,1,0:T(8,128)(2,1)} %get-tuple-element.88), channel_id=1, source_target_pairs={{0,4},{1,5},{2,6},{3,7},{4,0},{5,1},{6,2},{7,3},{8,12},{9,13},{10,... | collective-permute-start | bytes 393224 | tf_op jit(solution)/shard_map/ppermute | solution.py:102
  135.2 16.2 %all-to-all-start.3 = ((bf16[32,8,512]{2,1,0:T(8,128)(2,1)}), bf16[32,8,512]{2,1,0:T(8,128)(2,1)}, u32[]{:S(2)}, u32[]{:S(2)}) async-start(bf16[32,8,512]{2,1,0:T(8,128)(2,1)} %sum_shares.1.refs_4_), calls=%async_computation.3 | async-start | bytes 524288 | tf_op jit(solution)/shard_map/all_to_all | solution.py:748
  146.2 8.8 %collective-permute-start.24 = (bf16[4,256,128]{2,1,0:T(8,128)(2,1)}, bf16[4,256,128]{2,1,0:T(8,128)(2,1)}, u32[]{:S(2)}, u32[]{:S(2)}) collective-permute-start(bf16[4,256,128]{2,1,0:T(8,128)(2,1)} %pack.1), channel_id=1, source_target_pairs={{0,1},{1,0},{2,3},{3,2},{4,5},{5,4},{6,7},{7,6},{8,9},{9,8},{10,11... | collective-permute-start | bytes 786440 | tf_op jit(solution)/shard_map/ppermute | solution.py:110
  (7 other events, 22.0 us)

commit v6 on v5

--- a/solution.py
+++ b/solution.py
@@ -154,11 +154,6 @@
     x = x_low.astype(F32)
     inv = lax.rsqrt(jnp.mean(x * x, axis=1, keepdims=True) + EPS)
     return (x * inv * gain).astype(BF16)
-
-
-def project(x_low, gain, wide):
-    proj = dot_nt(normed(x_low, gain), wide).astype(BF16)
-    return proj[:, :BLK] * jnp.asarray(SCALE, BF16), proj[:, BLK:]
 
 
 def wide_weight(weight):
@@ -214,7 +209,8 @@
     loads = copies([chunk_in, gain_in, weight_in], [chunk_ref, gain_ref, weight_ref], in_sems)
     start_all(loads)
     wait_all(loads)
-    query_ref[...], kv_ref[...] = project(chunk_ref[...], gain_ref[...], wide_weight(weight_ref[...]))
+    hidden = normed(chunk_ref[...], gain_ref[...])
+    kv_ref[...] = dot_nt(hidden, weight_ref[HD:, :]).astype(BF16)
 
     def over_slots(act):
         for slot in range(sent_sems.shape[0]):
@@ -224,6 +220,8 @@
                 act(pltpu.make_async_copy(kv_ref, sent_out.at[slot], sent_sems.at[slot]))
 
     over_slots(lambda job: job.start())
+    query = dot_nt(hidden, wide_weight(weight_ref[...])[:BLK]).astype(BF16)
+    query_ref[...] = query * jnp.asarray(SCALE, BF16)
     stores = copies([query_ref, kv_ref], [query_out.at[NB - 1], kv_out.at[NB - 1]], out_sems)
     start_all(stores)
     over_slots(lambda job: job.wait())
@@ -319,8 +317,8 @@
         scaled_ref[i] = scaled
         den_ref[i] = inv
         extra_ref[i] = jnp.sum(grad * attn, axis=1, keepdims=True) * inv
-        attn_ref[:, rows_at(i)] = attn.T[HD:].astype(BF16)
-        both_ref[i] = (query_ref[i] + scaled).astype(F32).T.astype(BF16)
+        attn_ref[:, rows_at(i)] = attn.astype(BF16).T[HD:]
+        both_ref[i] = (query_ref[i] + scaled).T
     start_all(stores)
     jobs = []
     for i in range(NB):
@@ -493,8 +491,9 @@
 
 
 def head_terms(piece, weight):
-    terms = piece.astype(F32).T.astype(BF16)
-    return dot(terms[:, 3 * HD :], weight[3 * HD :, :]), dot(terms[:, : 3 * HD], weight[: 3 * HD, :])
+    out = lax.dot_general(piece[3 * HD :, :], weight[3 * HD :, :], TN, preferred_element_type=F32)
+    back = lax.dot_general(piece[: 3 * HD, :], weight[: 3 * HD, :], TN, preferred_element_type=F32)
+    return out, back
 
 
 def first_heads_body(*refs):

time: 159 us -> 159 us (level)
  no operation moved by 1% of the time
where the time goes in v6:
time: 159 us; the launch traced here: 158 us
  starting transfers between devices  72.6 us (46%)
  Pallas kernels  45.7 us (29%)
  waiting for transfers between devices  34.5 us (22%)
  local copies, waits for them, and re-layouts  2.62 us (2%)
    ppermute x24, starting transfers between devices, shifted(): return lax.ppermute(x, 'col', [(i, (i + k) % NB) for i in range(NB)])  40 us
    ppermute x24, waiting for transfers between devices, shifted(): return lax.ppermute(x, 'col', [(i, (i + k) % NB) for i in range(NB)])  32.4 us
    all_to_all x1, starting transfers between devices, shards(): fetched = lax.all_to_all(outgoing, 'dom', 0, 0, tiled=True)  7.82 us
    all_to_all x1, starting transfers between devices, shards(): returned = lax.all_to_all(outgoing_back, 'dom', 0, 0, tiled=True)  7.56 us
    all_to_all x1, starting transfers between devices, shards(): total = lax.all_to_all(totals, 'dom', 0, 0, tiled=True).reshape(4 * HD, D)  7.43 us
    all_to_all x1, starting transfers between devices, shards(): lax.all_to_all(part.reshape(doms, share_rows, D), 'dom', 0, 0, tiled=True)  7.39 us
    pallas_call x1, Pallas kernels, shards(): call(near_backward_body, (across, blocks_float, shaped(2 * HD, D), states...  7.22 us
    pallas_call x1, Pallas kernels, shards(): call(far_body, (across, blocks, blocks_float, exchanged), [scalars()] * 2...  7.17 us
  transfers between devices with their start and end apart: 29, of which 12 were waited for; matrix products, arithmetic and copies ran while one was open for 1% of the time, Pallas kernels for 20%

profile of v6, /device:TPU:2, one launch (start us, length us, event | category | flops | bytes accessed | tf_op | source)
XLA Modules:
  0.0 157.9 jit_solution(16016823328625304363)
XLA Ops:
  2.6 4.0 %collective-permute-start.1 = (bf16[128,512]{1,0:T(8,128)(2,1)}, bf16[128,512]{1,0:T(8,128)(2,1)}, u32[]{:S(2)}, u32[]{:S(2)}) collective-permute-start(bf16[128,512]{1,0:T(8,128)(2,1)} %refs_5_.1), channel_id=1, source_target_pairs={{0,7},{1,0},{2,1},{3,2},{4,3},{5,4},{6,5},{7,6},{8,15},{9,8},{10,9... | collective-permute-start | bytes 393224 | tf_op jit(solution)/shard_map/ppermute | solution.py:102
  10.4 3.2 %collective-permute-start.5 = (bf16[128,512]{1,0:T(8,128)(2,1)}, bf16[128,512]{1,0:T(8,128)(2,1)S(1)}, u32[]{:S(2)}, u32[]{:S(2)}) collective-permute-start(bf16[128,512]{1,0:T(8,128)(2,1)} %collective-permute-done.1.refs_2_.refs_10_), channel_id=1, source_target_pairs={{0,7},{1,0},{2,1},{3,2},{4,3},{5,4},{6,5},{7,6},{8,15},{9,8},{10,9... | collective-permute-start | bytes 393224 | tf_op jit(solution)/shard_map/ppermute | solution.py:102
  13.6 3.2 %collective-permute-done.2.refs_3_.refs_11_ = bf16[128,512]{1,0:T(8,128)(2,1)S(1)} collective-permute-done((bf16[128,512]{1,0:T(8,128)(2,1)}, bf16[128,512]{1,0:T(8,128)(2,1)S(1)}, u32[]{:S(2)}, u32[]{:S(2)}) %collective-permute-start.2) | collective-permute-done | bytes 131104 | tf_op jit(solution)/shard_map/ppermute | solution.py:102
  17.4 3.2 %collective-permute-start.6 = (bf16[128,512]{1,0:T(8,128)(2,1)S(1)}, bf16[128,512]{1,0:T(8,128)(2,1)S(1)}, u32[]{:S(2)}, u32[]{:S(2)}) collective-permute-start(bf16[128,512]{1,0:T(8,128)(2,1)S(1)} %collective-permute-done.5.refs_4_.refs_12_), channel_id=1, source_target_pairs={{0,7},{1,0},{2,1},{3,2},{4,3},{5,4},{6,5},{7,6},{8,15},{9,8},{10,9... | collective-permute-start | bytes 393224 | tf_op jit(solution)/shard_map/ppermute | solution.py:102
  20.7 3.0 %collective-permute-done.3.refs_5_.refs_13_ = bf16[128,512]{1,0:T(8,128)(2,1)} collective-permute-done((bf16[128,512]{1,0:T(8,128)(2,1)S(1)}, bf16[128,512]{1,0:T(8,128)(2,1)}, u32[]{:S(2)}, u32[]{:S(2)}) %collective-permute-start.3) | collective-permute-done | bytes 131104 | tf_op jit(solution)/shard_map/ppermute | solution.py:102
  24.4 4.5 %project_most.1 = (bf16[8,128,128]{2,1,0:T(8,128)(2,1)}, bf16[8,128,128]{2,1,0:T(8,128)(2,1)}, bf16[64,128,128]{2,1,0:T(8,128)(2,1)}) custom-call(s32[2,256]{1,0:T(2,128)} %get-tuple-element.53.send_ref.home_ref, bf16[128,512]{1,0:T(8,128)(2,1)} %refs_5_.1, bf16[128,512]{1,0:T(8,128)(2,1)} %collective-permute-done.refs_1_.refs_9_, ...), custom_call_target="tpu_custom_call" | custom-call | flops 268435456 | bytes 1048576 | tf_op jit(solution)/shard_map/project_most/pallas_call | solution.py:606
  30.2 3.3 %project_last.1 = (bf16[8,128,128]{2,1,0:T(8,128)(2,1)}, bf16[8,128,128]{2,1,0:T(8,128)(2,1)}, bf16[64,128,128]{2,1,0:T(8,128)(2,1)}) custom-call(s32[2,256]{1,0:T(2,128)} %get-tuple-element.53.send_ref.home_ref, bf16[128,512]{1,0:T(8,128)(2,1)} %collective-permute-done.4.chunk_in.refs_15_, ...), custom_call_target="tpu_custom_call", output_to_operand_aliasing={{0}: (4, {}), {1}: (5, {}), {2}: (6, {})} | custom-call | flops 33554432 | bytes 1048576 | tf_op jit(solution)/shard_map/project_last/pallas_call | solution.py:619
  33.5 7.8 %all-to-all-start = ((bf16[64,128,128]{2,1,0:T(8,128)(2,1)}), bf16[64,128,128]{2,1,0:T(8,128)(2,1)}, u32[]{:S(2)}, u32[]{:S(2)}) async-start(bf16[64,128,128]{2,1,0:T(8,128)(2,1)} %get-tuple-element.62), calls=%async_computation | async-start | bytes 4194304 | tf_op jit(solution)/shard_map/all_to_all | solution.py:635
  41.9 2.8 %collective-permute-start.11 = (bf16[128,512]{1,0:T(8,128)(2,1)S(1)}, bf16[128,512]{1,0:T(8,128)(2,1)S(1)}, u32[]{:S(2)}, u32[]{:S(2)}) collective-permute-start(bf16[128,512]{1,0:T(8,128)(2,1)S(1)} %copy-done.3), channel_id=1, source_target_pairs={{0,7},{1,0},{2,1},{3,2},{4,3},{5,4},{6,5},{7,6},{8,15},{9,8},{10,9... | collective-permute-start | bytes 393224 | tf_op jit(solution)/shard_map/ppermute | solution.py:102
  44.7 3.5 %collective-permute-done.7.refs_1_ = bf16[128,512]{1,0:T(8,128)(2,1)S(1)} collective-permute-done((bf16[128,512]{1,0:T(8,128)(2,1)S(1)}, bf16[128,512]{1,0:T(8,128)(2,1)S(1)}, u32[]{:S(2)}, u32[]{:S(2)}) %collective-permute-start.7) | collective-permute-done | bytes 131104 | tf_op jit(solution)/shard_map/ppermute | solution.py:102
  48.9 2.7 %collective-permute-start.12 = (bf16[128,512]{1,0:T(8,128)(2,1)S(1)}, bf16[128,512]{1,0:T(8,128)(2,1)}, u32[]{:S(2)}, u32[]{:S(2)}) collective-permute-start(bf16[128,512]{1,0:T(8,128)(2,1)S(1)} %collective-permute-done.11.refs_2_), channel_id=1, source_target_pairs={{0,7},{1,0},{2,1},{3,2},{4,3},{5,4},{6,5},{7,6},{8,15},{9,8},{10,9... | collective-permute-start | bytes 393224 | tf_op jit(solution)/shard_map/ppermute | solution.py:102
  51.5 2.9 %collective-permute-done.8.refs_3_ = bf16[128,512]{1,0:T(8,128)(2,1)S(1)} collective-permute-done((bf16[128,512]{1,0:T(8,128)(2,1)S(1)}, bf16[128,512]{1,0:T(8,128)(2,1)S(1)}, u32[]{:S(2)}, u32[]{:S(2)}) %collective-permute-start.8) | collective-permute-done | bytes 131104 | tf_op jit(solution)/shard_map/ppermute | solution.py:102
  55.1 2.8 %collective-permute-start.13 = (bf16[128,512]{1,0:T(8,128)(2,1)}, bf16[128,512]{1,0:T(8,128)(2,1)}, u32[]{:S(2)}, u32[]{:S(2)}) collective-permute-start(bf16[128,512]{1,0:T(8,128)(2,1)} %collective-permute-done.12.refs_4_), channel_id=1, source_target_pairs={{0,7},{1,0},{2,1},{3,2},{4,3},{5,4},{6,5},{7,6},{8,15},{9,8},{10,9... | collective-permute-start | bytes 393224 | tf_op jit(solution)/shard_map/ppermute | solution.py:102
  57.8 2.9 %collective-permute-done.9.refs_5_ = bf16[128,512]{1,0:T(8,128)(2,1)} collective-permute-done((bf16[128,512]{1,0:T(8,128)(2,1)S(1)}, bf16[128,512]{1,0:T(8,128)(2,1)}, u32[]{:S(2)}, u32[]{:S(2)}) %collective-permute-start.9) | collective-permute-done | bytes 131104 | tf_op jit(solution)/shard_map/ppermute | solution.py:102
  61.4 3.7 %near_forward.1.num_in = f32[8,128,128]{2,1,0:T(8,128)} custom-call(s32[1]{0:T(128)} %bitcast.col_ref, bf16[8,128,128]{2,1,0:T(8,128)(2,1)} %get-tuple-element.60.query_in.refs_17_, bf16[8,128,128]{2,1,0:T(8,128)(2,1)} %get-tuple-element.63.kv_in.refs_18_, f32[8,1024]{1,0:T(8,128)} %get-tuple-element.64.count_in.refs_19_), custom_call_target="tpu_custom_call" | custom-call | flops 536870912 | bytes 1048576 | tf_op jit(solution)/shard_map/near_forward/pallas_call | solution.py:655
  65.1 2.6 %attn_grad.1.ag_in = f32[8,128,128]{2,1,0:T(8,128)} custom-call(bf16[128,512]{1,0:T(8,128)(2,1)} %refs_6_.1, bf16[128,512]{1,0:T(8,128)(2,1)} %copy-done.7, bf16[128,512]{1,0:T(8,128)(2,1)} %copy-done.8, bf16[128,512]{1,0:T(8,128)(2,1)} %copy-done.9, bf16[128,512]{1,0:T(8,128)(2,1)} %collective-permute-done.12.refs_4_, ...), custom_call_target="tpu_custom_call" | custom-call | flops 134217728 | bytes 1048576 | tf_op jit(solution)/shard_map/attn_grad/pallas_call | solution.py:642
  69.5 7.2 %far_both.1 = (bf16[64,1024]{1,0:T(8,128)(2,1)}, bf16[8,128,128]{2,1,0:T(8,128)(2,1)}, f32[8,128,128]{2,1,0:T(8,128)}, bf16[64,128,128]{2,1,0:T(8,128)(2,1)}) custom-call(s32[2]{0:T(128)} %pad_add_fusion.where_ref, s32[4,256]{1,0:T(4,128)} %get-tuple-element.54.place_ref, bf16[8,128,128]{2,1,0:T(8,128)(2,1)} %get-tuple-element.60.query_in.refs_17_, ...), custom_call_target="tpu_custom_call" | custom-call | flops 536870912 | bytes 1048576 | tf_op jit(solution)/shard_map/far_both/pallas_call | solution.py:674
  76.7 7.6 %all-to-all-start.1 = ((bf16[64,128,128]{2,1,0:T(8,128)(2,1)}), bf16[64,128,128]{2,1,0:T(8,128)(2,1)}, u32[]{:S(2)}, u32[]{:S(2)}) async-start(bf16[64,128,128]{2,1,0:T(8,128)(2,1)} %get-tuple-element.67), calls=%async_computation.1 | async-start | bytes 4194304 | tf_op jit(solution)/shard_map/all_to_all | solution.py:695
  84.3 3.3 %collective-permute-start.16 = (bf16[256,512]{1,0:T(8,128)(2,1)S(1)}, bf16[256,512]{1,0:T(8,128)(2,1)}, u32[]{:S(2)}, u32[]{:S(2)}) collective-permute-start(bf16[256,512]{1,0:T(8,128)(2,1)S(1)} %copy-done.1), channel_id=1, source_target_pairs={{0,7},{1,0},{2,1},{3,2},{4,3},{5,4},{6,5},{7,6},{8,15},{9,8},{10,9... | collective-permute-start | bytes 786440 | tf_op jit(solution)/shard_map/ppermute | solution.py:102
  87.6 6.6 %collective-permute-done.14.refs_0_ = bf16[256,512]{1,0:T(8,128)(2,1)} collective-permute-done((bf16[256,512]{1,0:T(8,128)(2,1)S(1)}, bf16[256,512]{1,0:T(8,128)(2,1)}, u32[]{:S(2)}, u32[]{:S(2)}) %collective-permute-start.14) | collective-permute-done | bytes 262176 | tf_op jit(solution)/shard_map/ppermute | solution.py:102
  94.3 3.2 %collective-permute-start.17 = (bf16[256,512]{1,0:T(8,128)(2,1)}, bf16[256,512]{1,0:T(8,128)(2,1)}, u32[]{:S(2)}, u32[]{:S(2)}) collective-permute-start(bf16[256,512]{1,0:T(8,128)(2,1)} %collective-permute-done.16.refs_3_), channel_id=1, source_target_pairs={{0,7},{1,0},{2,1},{3,2},{4,3},{5,4},{6,5},{7,6},{8,15},{9,8},{10,9... | collective-permute-start | bytes 786440 | tf_op jit(solution)/shard_map/ppermute | solution.py:102
  97.5 7.2 %near_backward.1 = (bf16[64,1024]{1,0:T(8,128)(2,1)}, f32[8,128,128]{2,1,0:T(8,128)}, bf16[128,512]{1,0:T(8,128)(2,1)}, bf16[8,128,512]{2,1,0:T(8,128)(2,1)}) custom-call(s32[1]{0:T(128)} %bitcast.col_ref, bf16[128,512]{1,0:T(8,128)(2,1)} %refs_6_.1, bf16[128,512]{1,0:T(8,128)(2,1)} %copy-done.7, bf16[128,512]{1,0:T(8,128)(2,1)} %copy-done.8, ...), custom_call_target="tpu_custom_call" | custom-call | flops 1342177280 | bytes 1048576 | tf_op jit(solution)/shard_map/near_backward/pallas_call | solution.py:699
  104.8 3.2 %collective-permute-start.19 = (bf16[256,512]{1,0:T(8,128)(2,1)}, bf16[256,512]{1,0:T(8,128)(2,1)}, u32[]{:S(2)}, u32[]{:S(2)}) collective-permute-start(bf16[256,512]{1,0:T(8,128)(2,1)} %collective-permute-done.17.refs_5_), channel_id=1, source_target_pairs={{0,7},{1,0},{2,1},{3,2},{4,3},{5,4},{6,5},{7,6},{8,15},{9,8},{10,9... | collective-permute-start | bytes 786440 | tf_op jit(solution)/shard_map/ppermute | solution.py:102
  108.1 5.6 %collective-permute-done.18.refs_1_ = bf16[256,512]{1,0:T(8,128)(2,1)} collective-permute-done((bf16[256,512]{1,0:T(8,128)(2,1)}, bf16[256,512]{1,0:T(8,128)(2,1)}, u32[]{:S(2)}, u32[]{:S(2)}) %collective-permute-start.18) | collective-permute-done | bytes 262176 | tf_op jit(solution)/shard_map/ppermute | solution.py:102
  114.3 4.1 %gather_grads.1 = (bf16[2,256,128]{2,1,0:T(8,128)(2,1)}, bf16[2,256,128]{2,1,0:T(8,128)(2,1)}, bf16[2,256,128]{2,1,0:T(8,128)(2,1)}, bf16[2,256,128]{2,1,0:T(8,128)(2,1)}, bf16[256,512]{1,0:T(8,128)(2,1)}) custom-call(s32[1]{0:T(128)} %bitcast.col_ref, s32[2,256]{1,0:T(2,128)} %get-tuple-element.53.send_ref.home_ref, ...), custom_call_target="tpu_custom_call" | custom-call | flops 134217728 | bytes 1048576 | tf_op jit(solution)/shard_map/gather_grads/pallas_call | solution.py:720
  118.4 7.4 %all-to-all-start.2 = ((bf16[32,8,512]{2,1,0:T(8,128)(2,1)}), bf16[32,8,512]{2,1,0:T(8,128)(2,1)S(1)}, u32[]{:S(2)}, u32[]{:S(2)}) async-start(bf16[32,8,512]{2,1,0:T(8,128)(2,1)} %bitcast.7), calls=%async_computation.2 | async-start | bytes 524288 | tf_op jit(solution)/shard_map/all_to_all | solution.py:736
  125.8 4.6 %collective-permute-start.21 = (bf16[2,256,128]{2,1,0:T(8,128)(2,1)}, bf16[2,256,128]{2,1,0:T(8,128)(2,1)}, u32[]{:S(2)}, u32[]{:S(2)}) collective-permute-start(bf16[2,256,128]{2,1,0:T(8,128)(2,1)} %get-tuple-element.86), channel_id=1, source_target_pairs={{0,2},{1,3},{2,4},{3,5},{4,6},{5,7},{6,0},{7,1},{8,10},{9,11},{10,... | collective-permute-start | bytes 393224 | tf_op jit(solution)/shard_map/ppermute | solution.py:102
  130.4 3.7 %collective-permute-start.23 = (bf16[2,256,128]{2,1,0:T(8,128)(2,1)}, bf16[2,256,128]{2,1,0:T(8,128)(2,1)}, u32[]{:S(2)}, u32[]{:S(2)}) collective-permute-start(bf16[2,256,128]{2,1,0:T(8,128)(2,1)} %get-tuple-element.88), channel_id=1, source_target_pairs={{0,4},{1,5},{2,6},{3,7},{4,0},{5,1},{6,2},{7,3},{8,12},{9,13},{10,... | collective-permute-start | bytes 393224 | tf_op jit(solution)/shard_map/ppermute | solution.py:102
  134.8 7.4 %all-to-all-start.3 = ((bf16[32,8,512]{2,1,0:T(8,128)(2,1)}), bf16[32,8,512]{2,1,0:T(8,128)(2,1)}, u32[]{:S(2)}, u32[]{:S(2)}) async-start(bf16[32,8,512]{2,1,0:T(8,128)(2,1)} %sum_shares.1.refs_4_), calls=%async_computation.3 | async-start | bytes 524288 | tf_op jit(solution)/shard_map/all_to_all | solution.py:747
  145.9 2.4 %collective-permute-start.24 = (bf16[4,256,128]{2,1,0:T(8,128)(2,1)}, bf16[4,256,128]{2,1,0:T(8,128)(2,1)}, u32[]{:S(2)}, u32[]{:S(2)}) collective-permute-start(bf16[4,256,128]{2,1,0:T(8,128)(2,1)} %pack.1), channel_id=1, source_target_pairs={{0,1},{1,0},{2,3},{3,2},{4,5},{5,4},{6,7},{7,6},{8,9},{9,8},{10,11... | collective-permute-start | bytes 786440 | tf_op jit(solution)/shard_map/ppermute | solution.py:110
  148.3 2.4 %first_heads.1.sum_in = f32[2,128,512]{2,1,0:T(8,128)} custom-call(bf16[2,256,128]{2,1,0:T(8,128)(2,1)} %get-tuple-element.85.refs_0_, bf16[2,256,128]{2,1,0:T(8,128)(2,1)} %collective-permute-done.21.refs_1_, bf16[2,256,128]{2,1,0:T(8,128)(2,1)} %collective-permute-done.22.refs_2_.refs_3_, bf16[256,512]{1,0:T(8,128)(2,1)} %pad_maximum_fusion.refs_3_, ...), custom_call_target="tpu_custom_call" | custom-call | flops 2684354 | bytes 1048576 | tf_op jit(solution)/shard_map/first_heads/pallas_call | solution.py:758
  154.6 3.1 %finish.1 = (bf16[128,512]{1,0:T(8,128)(2,1)}, bf16[128,512]{1,0:T(8,128)(2,1)}) custom-call(s32[1]{0:T(128)} %bitcast.col_ref, f32[2,128,512]{2,1,0:T(8,128)} %first_heads.1.sum_in, bf16[2,256,128]{2,1,0:T(8,128)(2,1)} %collective-permute-done.23.refs_2_.pair_in, bf16[4,256,128]{2,1,0:T(8,128)(2,1)} %collective-permute-done.24.beside_in, ...), custom_call_target="tpu_custom_call" | custom-call | flops 2684354 | bytes 1048576 | tf_op jit(solution)/shard_map/finish/pallas_call | solution.py:771
  (62 shorter events, 21.9 us)
Async XLA Ops:
  0.6 9.7 %collective-permute-start = (bf16[128,512]{1,0:T(8,128)(2,1)}, bf16[128,512]{1,0:T(8,128)(2,1)}, u32[]{:S(2)}, u32[]{:S(2)}) collective-permute-start(bf16[128,512]{1,0:T(8,128)(2,1)} %refs_5_.1), channel_id=1, source_target_pairs={{0,1},{1,2},{2,3},{3,4},{4,5},{5,6},{6,7},{7,0},{8,9},{9,10},{10,1... | collective-permute-start | bytes 393224 | tf_op jit(solution)/shard_map/ppermute | solution.py:102
  2.6 7.8 %collective-permute-start.1 = (bf16[128,512]{1,0:T(8,128)(2,1)}, bf16[128,512]{1,0:T(8,128)(2,1)}, u32[]{:S(2)}, u32[]{:S(2)}) collective-permute-start(bf16[128,512]{1,0:T(8,128)(2,1)} %refs_5_.1), channel_id=1, source_target_pairs={{0,7},{1,0},{2,1},{3,2},{4,3},{5,4},{6,5},{7,6},{8,15},{9,8},{10,9... | collective-permute-start | bytes 393224 | tf_op jit(solution)/shard_map/ppermute | solution.py:102
  10.4 6.4 %collective-permute-start.2 = (bf16[128,512]{1,0:T(8,128)(2,1)}, bf16[128,512]{1,0:T(8,128)(2,1)S(1)}, u32[]{:S(2)}, u32[]{:S(2)}) collective-permute-start(bf16[128,512]{1,0:T(8,128)(2,1)} %collective-permute-done.refs_1_.refs_9_), channel_id=1, source_target_pairs={{0,1},{1,2},{2,3},{3,4},{4,5},{5,6},{6,7},{7,0},{8,9},{9,10},{10,1... | collective-permute-start | bytes 393224 | tf_op jit(solution)/shard_map/ppermute | solution.py:102
  10.4 7.0 %collective-permute-start.5 = (bf16[128,512]{1,0:T(8,128)(2,1)}, bf16[128,512]{1,0:T(8,128)(2,1)S(1)}, u32[]{:S(2)}, u32[]{:S(2)}) collective-permute-start(bf16[128,512]{1,0:T(8,128)(2,1)} %collective-permute-done.1.refs_2_.refs_10_), channel_id=1, source_target_pairs={{0,7},{1,0},{2,1},{3,2},{4,3},{5,4},{6,5},{7,6},{8,15},{9,8},{10,9... | collective-permute-start | bytes 393224 | tf_op jit(solution)/shard_map/ppermute | solution.py:102
  17.4 6.3 %collective-permute-start.3 = (bf16[128,512]{1,0:T(8,128)(2,1)S(1)}, bf16[128,512]{1,0:T(8,128)(2,1)}, u32[]{:S(2)}, u32[]{:S(2)}) collective-permute-start(bf16[128,512]{1,0:T(8,128)(2,1)S(1)} %collective-permute-done.2.refs_3_.refs_11_), channel_id=1, source_target_pairs={{0,1},{1,2},{2,3},{3,4},{4,5},{5,6},{6,7},{7,0},{8,9},{9,10},{10,1... | collective-permute-start | bytes 393224 | tf_op jit(solution)/shard_map/ppermute | solution.py:102
  17.4 6.3 %collective-permute-start.6 = (bf16[128,512]{1,0:T(8,128)(2,1)S(1)}, bf16[128,512]{1,0:T(8,128)(2,1)S(1)}, u32[]{:S(2)}, u32[]{:S(2)}) collective-permute-start(bf16[128,512]{1,0:T(8,128)(2,1)S(1)} %collective-permute-done.5.refs_4_.refs_12_), channel_id=1, source_target_pairs={{0,7},{1,0},{2,1},{3,2},{4,3},{5,4},{6,5},{7,6},{8,15},{9,8},{10,9... | collective-permute-start | bytes 393224 | tf_op jit(solution)/shard_map/ppermute | solution.py:102
  23.7 6.5 %collective-permute-start.4 = (bf16[128,512]{1,0:T(8,128)(2,1)}, bf16[128,512]{1,0:T(8,128)(2,1)}, u32[]{:S(2)}, u32[]{:S(2)}) collective-permute-start(bf16[128,512]{1,0:T(8,128)(2,1)} %collective-permute-done.3.refs_5_.refs_13_), channel_id=1, source_target_pairs={{0,1},{1,2},{2,3},{3,4},{4,5},{5,6},{6,7},{7,0},{8,9},{9,10},{10,1... | collective-permute-start | bytes 393224 | tf_op jit(solution)/shard_map/ppermute | solution.py:102
  33.5 7.9 %copy-start.3 = (bf16[128,512]{1,0:T(8,128)(2,1)S(1)}, bf16[128,512]{1,0:T(8,128)(2,1)}, u32[]{:S(2)}) copy-start(bf16[128,512]{1,0:T(8,128)(2,1)} %refs_6_.1) | copy-start | bytes 393220
  33.5 27.2 %copy-start = (bf16[192,512]{1,0:T(8,128)(2,1)S(1)}, bf16[192,512]{1,0:T(8,128)(2,1)}, u32[]{:S(2)}) copy-start(bf16[192,512]{1,0:T(8,128)(2,1)} %weight_in.2) | copy-start | bytes 589828
  33.5 27.2 %copy-start.2 = (bf16[64,512]{1,0:T(8,128)(2,1)S(1)}, bf16[64,512]{1,0:T(8,128)(2,1)}, u32[]{:S(2)}) copy-start(bf16[64,512]{1,0:T(8,128)(2,1)} %weight_in.3) | copy-start | bytes 196612
  33.5 35.9 %all-to-all-start = ((bf16[64,128,128]{2,1,0:T(8,128)(2,1)}), bf16[64,128,128]{2,1,0:T(8,128)(2,1)}, u32[]{:S(2)}, u32[]{:S(2)}) async-start(bf16[64,128,128]{2,1,0:T(8,128)(2,1)} %get-tuple-element.62), calls=%async_computation | async-start | bytes 4194304 | tf_op jit(solution)/shard_map/all_to_all | solution.py:635
  41.4 6.8 %collective-permute-start.7 = (bf16[128,512]{1,0:T(8,128)(2,1)S(1)}, bf16[128,512]{1,0:T(8,128)(2,1)S(1)}, u32[]{:S(2)}, u32[]{:S(2)}) collective-permute-start(bf16[128,512]{1,0:T(8,128)(2,1)S(1)} %copy-done.3), channel_id=1, source_target_pairs={{0,1},{1,2},{2,3},{3,4},{4,5},{5,6},{6,7},{7,0},{8,9},{9,10},{10,1... | collective-permute-start | bytes 393224 | tf_op jit(solution)/shard_map/ppermute | solution.py:102
  41.9 6.3 %collective-permute-start.11 = (bf16[128,512]{1,0:T(8,128)(2,1)S(1)}, bf16[128,512]{1,0:T(8,128)(2,1)S(1)}, u32[]{:S(2)}, u32[]{:S(2)}) collective-permute-start(bf16[128,512]{1,0:T(8,128)(2,1)S(1)} %copy-done.3), channel_id=1, source_target_pairs={{0,7},{1,0},{2,1},{3,2},{4,3},{5,4},{6,5},{7,6},{8,15},{9,8},{10,9... | collective-permute-start | bytes 393224 | tf_op jit(solution)/shard_map/ppermute | solution.py:102
  48.2 6.2 %collective-permute-start.8 = (bf16[128,512]{1,0:T(8,128)(2,1)S(1)}, bf16[128,512]{1,0:T(8,128)(2,1)S(1)}, u32[]{:S(2)}, u32[]{:S(2)}) collective-permute-start(bf16[128,512]{1,0:T(8,128)(2,1)S(1)} %collective-permute-done.7.refs_1_), channel_id=1, source_target_pairs={{0,1},{1,2},{2,3},{3,4},{4,5},{5,6},{6,7},{7,0},{8,9},{9,10},{10,1... | collective-permute-start | bytes 393224 | tf_op jit(solution)/shard_map/ppermute | solution.py:102
  48.9 5.5 %collective-permute-start.12 = (bf16[128,512]{1,0:T(8,128)(2,1)S(1)}, bf16[128,512]{1,0:T(8,128)(2,1)}, u32[]{:S(2)}, u32[]{:S(2)}) collective-permute-start(bf16[128,512]{1,0:T(8,128)(2,1)S(1)} %collective-permute-done.11.refs_2_), channel_id=1, source_target_pairs={{0,7},{1,0},{2,1},{3,2},{4,3},{5,4},{6,5},{7,6},{8,15},{9,8},{10,9... | collective-permute-start | bytes 393224 | tf_op jit(solution)/shard_map/ppermute | solution.py:102
  54.4 6.3 %collective-permute-start.9 = (bf16[128,512]{1,0:T(8,128)(2,1)S(1)}, bf16[128,512]{1,0:T(8,128)(2,1)}, u32[]{:S(2)}, u32[]{:S(2)}) collective-permute-start(bf16[128,512]{1,0:T(8,128)(2,1)S(1)} %collective-permute-done.8.refs_3_), channel_id=1, source_target_pairs={{0,1},{1,2},{2,3},{3,4},{4,5},{5,6},{6,7},{7,0},{8,9},{9,10},{10,1... | collective-permute-start | bytes 393224 | tf_op jit(solution)/shard_map/ppermute | solution.py:102
  55.1 10.0 %collective-permute-start.13 = (bf16[128,512]{1,0:T(8,128)(2,1)}, bf16[128,512]{1,0:T(8,128)(2,1)}, u32[]{:S(2)}, u32[]{:S(2)}) collective-permute-start(bf16[128,512]{1,0:T(8,128)(2,1)} %collective-permute-done.12.refs_4_), channel_id=1, source_target_pairs={{0,7},{1,0},{2,1},{3,2},{4,3},{5,4},{6,5},{7,6},{8,15},{9,8},{10,9... | collective-permute-start | bytes 393224 | tf_op jit(solution)/shard_map/ppermute | solution.py:102
  60.7 7.0 %collective-permute-start.10 = (bf16[128,512]{1,0:T(8,128)(2,1)}, bf16[128,512]{1,0:T(8,128)(2,1)}, u32[]{:S(2)}, u32[]{:S(2)}) collective-permute-start(bf16[128,512]{1,0:T(8,128)(2,1)} %collective-permute-done.9.refs_5_), channel_id=1, source_target_pairs={{0,1},{1,2},{2,3},{3,4},{4,5},{5,6},{6,7},{7,0},{8,9},{9,10},{10,1... | collective-permute-start | bytes 393224 | tf_op jit(solution)/shard_map/ppermute | solution.py:102
  76.7 37.0 %all-to-all-start.1 = ((bf16[64,128,128]{2,1,0:T(8,128)(2,1)}), bf16[64,128,128]{2,1,0:T(8,128)(2,1)}, u32[]{:S(2)}, u32[]{:S(2)}) async-start(bf16[64,128,128]{2,1,0:T(8,128)(2,1)} %get-tuple-element.67), calls=%async_computation.1 | async-start | bytes 4194304 | tf_op jit(solution)/shard_map/all_to_all | solution.py:695
  84.2 10.0 %collective-permute-start.14 = (bf16[256,512]{1,0:T(8,128)(2,1)S(1)}, bf16[256,512]{1,0:T(8,128)(2,1)}, u32[]{:S(2)}, u32[]{:S(2)}) collective-permute-start(bf16[256,512]{1,0:T(8,128)(2,1)S(1)} %copy-done.1), channel_id=1, source_target_pairs={{0,1},{1,2},{2,3},{3,4},{4,5},{5,6},{6,7},{7,0},{8,9},{9,10},{10,1... | collective-permute-start | bytes 786440 | tf_op jit(solution)/shard_map/ppermute | solution.py:102
  84.3 9.9 %collective-permute-start.16 = (bf16[256,512]{1,0:T(8,128)(2,1)S(1)}, bf16[256,512]{1,0:T(8,128)(2,1)}, u32[]{:S(2)}, u32[]{:S(2)}) collective-permute-start(bf16[256,512]{1,0:T(8,128)(2,1)S(1)} %copy-done.1), channel_id=1, source_target_pairs={{0,7},{1,0},{2,1},{3,2},{4,3},{5,4},{6,5},{7,6},{8,15},{9,8},{10,9... | collective-permute-start | bytes 786440 | tf_op jit(solution)/shard_map/ppermute | solution.py:102
  94.3 10.5 %collective-permute-start.15 = (bf16[256,512]{1,0:T(8,128)(2,1)}, bf16[256,512]{1,0:T(8,128)(2,1)}, u32[]{:S(2)}, u32[]{:S(2)}) collective-permute-start(bf16[256,512]{1,0:T(8,128)(2,1)} %collective-permute-done.14.refs_0_), channel_id=1, source_target_pairs={{0,1},{1,2},{2,3},{3,4},{4,5},{5,6},{6,7},{7,0},{8,9},{9,10},{10,1... | collective-permute-start | bytes 786440 | tf_op jit(solution)/shard_map/ppermute | solution.py:102
  94.3 10.5 %collective-permute-start.17 = (bf16[256,512]{1,0:T(8,128)(2,1)}, bf16[256,512]{1,0:T(8,128)(2,1)}, u32[]{:S(2)}, u32[]{:S(2)}) collective-permute-start(bf16[256,512]{1,0:T(8,128)(2,1)} %collective-permute-done.16.refs_3_), channel_id=1, source_target_pairs={{0,7},{1,0},{2,1},{3,2},{4,3},{5,4},{6,5},{7,6},{8,15},{9,8},{10,9... | collective-permute-start | bytes 786440 | tf_op jit(solution)/shard_map/ppermute | solution.py:102
  104.7 8.9 %collective-permute-start.18 = (bf16[256,512]{1,0:T(8,128)(2,1)}, bf16[256,512]{1,0:T(8,128)(2,1)}, u32[]{:S(2)}, u32[]{:S(2)}) collective-permute-start(bf16[256,512]{1,0:T(8,128)(2,1)} %collective-permute-done.15.refs_4_), channel_id=1, source_target_pairs={{0,1},{1,2},{2,3},{3,4},{4,5},{5,6},{6,7},{7,0},{8,9},{9,10},{10,1... | collective-permute-start | bytes 786440 | tf_op jit(solution)/shard_map/ppermute | solution.py:102
  104.8 8.8 %collective-permute-start.19 = (bf16[256,512]{1,0:T(8,128)(2,1)}, bf16[256,512]{1,0:T(8,128)(2,1)}, u32[]{:S(2)}, u32[]{:S(2)}) collective-permute-start(bf16[256,512]{1,0:T(8,128)(2,1)} %collective-permute-done.17.refs_5_), channel_id=1, source_target_pairs={{0,7},{1,0},{2,1},{3,2},{4,3},{5,4},{6,5},{7,6},{8,15},{9,8},{10,9... | collective-permute-start | bytes 786440 | tf_op jit(solution)/shard_map/ppermute | solution.py:102
  113.6 12.2 %collective-permute-start.20 = (bf16[256,512]{1,0:T(8,128)(2,1)}, bf16[256,512]{1,0:T(8,128)(2,1)}, u32[]{:S(2)}, u32[]{:S(2)}) collective-permute-start(bf16[256,512]{1,0:T(8,128)(2,1)} %collective-permute-done.18.refs_1_), channel_id=1, source_target_pairs={{0,1},{1,2},{2,3},{3,4},{4,5},{5,6},{6,7},{7,0},{8,9},{9,10},{10,1... | collective-permute-start | bytes 786440 | tf_op jit(solution)/shard_map/ppermute | solution.py:102
  118.4 15.6 %all-to-all-start.2 = ((bf16[32,8,512]{2,1,0:T(8,128)(2,1)}), bf16[32,8,512]{2,1,0:T(8,128)(2,1)S(1)}, u32[]{:S(2)}, u32[]{:S(2)}) async-start(bf16[32,8,512]{2,1,0:T(8,128)(2,1)} %bitcast.7), calls=%async_computation.2 | async-start | bytes 524288 | tf_op jit(solution)/shard_map/all_to_all | solution.py:736
  125.8 16.4 %collective-permute-start.21 = (bf16[2,256,128]{2,1,0:T(8,128)(2,1)}, bf16[2,256,128]{2,1,0:T(8,128)(2,1)}, u32[]{:S(2)}, u32[]{:S(2)}) collective-permute-start(bf16[2,256,128]{2,1,0:T(8,128)(2,1)} %get-tuple-element.86), channel_id=1, source_target_pairs={{0,2},{1,3},{2,4},{3,5},{4,6},{5,7},{6,0},{7,1},{8,10},{9,11},{10,... | collective-permute-start | bytes 393224 | tf_op jit(solution)/shard_map/ppermute | solution.py:102
  130.4 12.6 %collective-permute-start.22 = (bf16[2,256,128]{2,1,0:T(8,128)(2,1)}, bf16[2,256,128]{2,1,0:T(8,128)(2,1)}, u32[]{:S(2)}, u32[]{:S(2)}) collective-permute-start(bf16[2,256,128]{2,1,0:T(8,128)(2,1)} %get-tuple-element.87), channel_id=1, source_target_pairs={{0,6},{1,7},{2,0},{3,1},{4,2},{5,3},{6,4},{7,5},{8,14},{9,15},{10,... | collective-permute-start | bytes 393224 | tf_op jit(solution)/shard_map/ppermute | solution.py:102
  130.4 13.9 %collective-permute-start.23 = (bf16[2,256,128]{2,1,0:T(8,128)(2,1)}, bf16[2,256,128]{2,1,0:T(8,128)(2,1)}, u32[]{:S(2)}, u32[]{:S(2)}) collective-permute-start(bf16[2,256,128]{2,1,0:T(8,128)(2,1)} %get-tuple-element.88), channel_id=1, source_target_pairs={{0,4},{1,5},{2,6},{3,7},{4,0},{5,1},{6,2},{7,3},{8,12},{9,13},{10,... | collective-permute-start | bytes 393224 | tf_op jit(solution)/shard_map/ppermute | solution.py:102
  134.8 15.9 %all-to-all-start.3 = ((bf16[32,8,512]{2,1,0:T(8,128)(2,1)}), bf16[32,8,512]{2,1,0:T(8,128)(2,1)}, u32[]{:S(2)}, u32[]{:S(2)}) async-start(bf16[32,8,512]{2,1,0:T(8,128)(2,1)} %sum_shares.1.refs_4_), calls=%async_computation.3 | async-start | bytes 524288 | tf_op jit(solution)/shard_map/all_to_all | solution.py:747
  145.9 8.7 %collective-permute-start.24 = (bf16[4,256,128]{2,1,0:T(8,128)(2,1)}, bf16[4,256,128]{2,1,0:T(8,128)(2,1)}, u32[]{:S(2)}, u32[]{:S(2)}) collective-permute-start(bf16[4,256,128]{2,1,0:T(8,128)(2,1)} %pack.1), channel_id=1, source_target_pairs={{0,1},{1,0},{2,3},{3,2},{4,5},{5,4},{6,7},{7,6},{8,9},{9,8},{10,11... | collective-permute-start | bytes 786440 | tf_op jit(solution)/shard_map/ppermute | solution.py:110
  (7 other events, 22.0 us)

commit v7 on v6

--- a/solution.py
+++ b/solution.py
@@ -455,8 +455,16 @@
         at = jnp.where(odd_place == 1, last_at, next_at)
         far_pieces.append(proj_ref.at[:, pl.ds(pl.multiple_of(at * BLK, BLK), BLK)])
     stores = copies(
-        [part_ref, *far_pieces, *near_pieces],
-        [part_out, *(out.at[1] for out in pair_outs), *(out.at[0] for out in pair_outs)],
+        [
+            *(part_ref.at[pl.ds(at, rows)] for at, rows in ((HD, 2 * HD), (0, HD), (3 * HD, HD))),
+            *far_pieces,
+            *near_pieces,
+        ],
+        [
+            *(part_out.at[pl.ds(at, rows)] for at, rows in ((HD, 2 * HD), (0, HD), (3 * HD, HD))),
+            *(out.at[1] for out in pair_outs),
+            *(out.at[0] for out in pair_outs),
+        ],
         out_sems,
     )
     start_all(stores[1:])
@@ -726,7 +734,7 @@
             *held(shaped(NB + 1, BLK, BLK, kind=F32), shaped(4 * HD, ROWS), states, shaped(4 * HD, D)),
             dma_sems(4),
             dma_sems(6),
-            dma_sems(1 + NB),
+            dma_sems(3 + NB),
         ],
         flops=2 * ROWS * D * 128,
         name="gather_grads",

time: 159 us -> 159 us (level)
  no operation moved by 1% of the time
where the time goes in v7:
time: 159 us; the launch traced here: 158 us
  starting transfers between devices  72.6 us (46%)
  Pallas kernels  45.7 us (29%)
  waiting for transfers between devices  34.6 us (22%)
  local copies, waits for them, and re-layouts  2.62 us (2%)
    ppermute x24, starting transfers between devices, shifted(): return lax.ppermute(x, 'col', [(i, (i + k) % NB) for i in range(NB)])  40 us
    ppermute x24, waiting for transfers between devices, shifted(): return lax.ppermute(x, 'col', [(i, (i + k) % NB) for i in range(NB)])  32.4 us
    all_to_all x1, starting transfers between devices, shards(): fetched = lax.all_to_all(outgoing, 'dom', 0, 0, tiled=True)  7.81 us
    all_to_all x1, starting transfers between devices, shards(): returned = lax.all_to_all(outgoing_back, 'dom', 0, 0, tiled=True)  7.56 us
    all_to_all x1, starting transfers between devices, shards(): total = lax.all_to_all(totals, 'dom', 0, 0, tiled=True).reshape(4 * HD, D)  7.43 us
    all_to_all x1, starting transfers between devices, shards(): lax.all_to_all(part.reshape(doms, share_rows, D), 'dom', 0, 0, tiled=True)  7.39 us
    pallas_call x1, Pallas kernels, shards(): call(near_backward_body, (across, blocks_float, shaped(2 * HD, D), states...  7.21 us
    pallas_call x1, Pallas kernels, shards(): call(far_body, (across, blocks, blocks_float, exchanged), [scalars()] * 2...  7.15 us
  transfers between devices with their start and end apart: 29, of which 12 were waited for; matrix products, arithmetic and copies ran while one was open for 1% of the time, Pallas kernels for 20%

profile of v7, /device:TPU:2, one launch (start us, length us, event | category | flops | bytes accessed | tf_op | source)
XLA Modules:
  0.0 157.9 jit_solution(14049960025112817476)
XLA Ops:
  2.6 4.0 %collective-permute-start.1 = (bf16[128,512]{1,0:T(8,128)(2,1)}, bf16[128,512]{1,0:T(8,128)(2,1)}, u32[]{:S(2)}, u32[]{:S(2)}) collective-permute-start(bf16[128,512]{1,0:T(8,128)(2,1)} %refs_5_.1), channel_id=1, source_target_pairs={{0,7},{1,0},{2,1},{3,2},{4,3},{5,4},{6,5},{7,6},{8,15},{9,8},{10,9... | collective-permute-start | bytes 393224 | tf_op jit(solution)/shard_map/ppermute | solution.py:102
  10.4 3.2 %collective-permute-start.5 = (bf16[128,512]{1,0:T(8,128)(2,1)}, bf16[128,512]{1,0:T(8,128)(2,1)S(1)}, u32[]{:S(2)}, u32[]{:S(2)}) collective-permute-start(bf16[128,512]{1,0:T(8,128)(2,1)} %collective-permute-done.1.refs_2_.refs_10_), channel_id=1, source_target_pairs={{0,7},{1,0},{2,1},{3,2},{4,3},{5,4},{6,5},{7,6},{8,15},{9,8},{10,9... | collective-permute-start | bytes 393224 | tf_op jit(solution)/shard_map/ppermute | solution.py:102
  13.6 3.2 %collective-permute-done.2.refs_3_.refs_11_ = bf16[128,512]{1,0:T(8,128)(2,1)S(1)} collective-permute-done((bf16[128,512]{1,0:T(8,128)(2,1)}, bf16[128,512]{1,0:T(8,128)(2,1)S(1)}, u32[]{:S(2)}, u32[]{:S(2)}) %collective-permute-start.2) | collective-permute-done | bytes 131104 | tf_op jit(solution)/shard_map/ppermute | solution.py:102
  17.4 3.2 %collective-permute-start.6 = (bf16[128,512]{1,0:T(8,128)(2,1)S(1)}, bf16[128,512]{1,0:T(8,128)(2,1)S(1)}, u32[]{:S(2)}, u32[]{:S(2)}) collective-permute-start(bf16[128,512]{1,0:T(8,128)(2,1)S(1)} %collective-permute-done.5.refs_4_.refs_12_), channel_id=1, source_target_pairs={{0,7},{1,0},{2,1},{3,2},{4,3},{5,4},{6,5},{7,6},{8,15},{9,8},{10,9... | collective-permute-start | bytes 393224 | tf_op jit(solution)/shard_map/ppermute | solution.py:102
  20.7 3.0 %collective-permute-done.3.refs_5_.refs_13_ = bf16[128,512]{1,0:T(8,128)(2,1)} collective-permute-done((bf16[128,512]{1,0:T(8,128)(2,1)S(1)}, bf16[128,512]{1,0:T(8,128)(2,1)}, u32[]{:S(2)}, u32[]{:S(2)}) %collective-permute-start.3) | collective-permute-done | bytes 131104 | tf_op jit(solution)/shard_map/ppermute | solution.py:102
  24.4 4.5 %project_most.1 = (bf16[8,128,128]{2,1,0:T(8,128)(2,1)}, bf16[8,128,128]{2,1,0:T(8,128)(2,1)}, bf16[64,128,128]{2,1,0:T(8,128)(2,1)}) custom-call(s32[2,256]{1,0:T(2,128)} %get-tuple-element.53.send_ref.home_ref, bf16[128,512]{1,0:T(8,128)(2,1)} %refs_5_.1, bf16[128,512]{1,0:T(8,128)(2,1)} %collective-permute-done.refs_1_.refs_9_, ...), custom_call_target="tpu_custom_call" | custom-call | flops 268435456 | bytes 1048576 | tf_op jit(solution)/shard_map/project_most/pallas_call | solution.py:614
  30.2 3.3 %project_last.1 = (bf16[8,128,128]{2,1,0:T(8,128)(2,1)}, bf16[8,128,128]{2,1,0:T(8,128)(2,1)}, bf16[64,128,128]{2,1,0:T(8,128)(2,1)}) custom-call(s32[2,256]{1,0:T(2,128)} %get-tuple-element.53.send_ref.home_ref, bf16[128,512]{1,0:T(8,128)(2,1)} %collective-permute-done.4.chunk_in.refs_15_, ...), custom_call_target="tpu_custom_call", output_to_operand_aliasing={{0}: (4, {}), {1}: (5, {}), {2}: (6, {})} | custom-call | flops 33554432 | bytes 1048576 | tf_op jit(solution)/shard_map/project_last/pallas_call | solution.py:627
  33.6 7.8 %all-to-all-start = ((bf16[64,128,128]{2,1,0:T(8,128)(2,1)}), bf16[64,128,128]{2,1,0:T(8,128)(2,1)}, u32[]{:S(2)}, u32[]{:S(2)}) async-start(bf16[64,128,128]{2,1,0:T(8,128)(2,1)} %get-tuple-element.62), calls=%async_computation | async-start | bytes 4194304 | tf_op jit(solution)/shard_map/all_to_all | solution.py:643
  41.9 2.8 %collective-permute-start.11 = (bf16[128,512]{1,0:T(8,128)(2,1)S(1)}, bf16[128,512]{1,0:T(8,128)(2,1)S(1)}, u32[]{:S(2)}, u32[]{:S(2)}) collective-permute-start(bf16[128,512]{1,0:T(8,128)(2,1)S(1)} %copy-done.3), channel_id=1, source_target_pairs={{0,7},{1,0},{2,1},{3,2},{4,3},{5,4},{6,5},{7,6},{8,15},{9,8},{10,9... | collective-permute-start | bytes 393224 | tf_op jit(solution)/shard_map/ppermute | solution.py:102
  44.7 3.5 %collective-permute-done.7.refs_1_ = bf16[128,512]{1,0:T(8,128)(2,1)S(1)} collective-permute-done((bf16[128,512]{1,0:T(8,128)(2,1)S(1)}, bf16[128,512]{1,0:T(8,128)(2,1)S(1)}, u32[]{:S(2)}, u32[]{:S(2)}) %collective-permute-start.7) | collective-permute-done | bytes 131104 | tf_op jit(solution)/shard_map/ppermute | solution.py:102
  48.9 2.7 %collective-permute-start.12 = (bf16[128,512]{1,0:T(8,128)(2,1)S(1)}, bf16[128,512]{1,0:T(8,128)(2,1)}, u32[]{:S(2)}, u32[]{:S(2)}) collective-permute-start(bf16[128,512]{1,0:T(8,128)(2,1)S(1)} %collective-permute-done.11.refs_2_), channel_id=1, source_target_pairs={{0,7},{1,0},{2,1},{3,2},{4,3},{5,4},{6,5},{7,6},{8,15},{9,8},{10,9... | collective-permute-start | bytes 393224 | tf_op jit(solution)/shard_map/ppermute | solution.py:102
  51.6 2.9 %collective-permute-done.8.refs_3_ = bf16[128,512]{1,0:T(8,128)(2,1)S(1)} collective-permute-done((bf16[128,512]{1,0:T(8,128)(2,1)S(1)}, bf16[128,512]{1,0:T(8,128)(2,1)S(1)}, u32[]{:S(2)}, u32[]{:S(2)}) %collective-permute-start.8) | collective-permute-done | bytes 131104 | tf_op jit(solution)/shard_map/ppermute | solution.py:102
  55.1 2.8 %collective-permute-start.13 = (bf16[128,512]{1,0:T(8,128)(2,1)}, bf16[128,512]{1,0:T(8,128)(2,1)}, u32[]{:S(2)}, u32[]{:S(2)}) collective-permute-start(bf16[128,512]{1,0:T(8,128)(2,1)} %collective-permute-done.12.refs_4_), channel_id=1, source_target_pairs={{0,7},{1,0},{2,1},{3,2},{4,3},{5,4},{6,5},{7,6},{8,15},{9,8},{10,9... | collective-permute-start | bytes 393224 | tf_op jit(solution)/shard_map/ppermute | solution.py:102
  57.8 2.9 %collective-permute-done.9.refs_5_ = bf16[128,512]{1,0:T(8,128)(2,1)} collective-permute-done((bf16[128,512]{1,0:T(8,128)(2,1)S(1)}, bf16[128,512]{1,0:T(8,128)(2,1)}, u32[]{:S(2)}, u32[]{:S(2)}) %collective-permute-start.9) | collective-permute-done | bytes 131104 | tf_op jit(solution)/shard_map/ppermute | solution.py:102
  61.5 3.7 %near_forward.1.num_in = f32[8,128,128]{2,1,0:T(8,128)} custom-call(s32[1]{0:T(128)} %bitcast.col_ref, bf16[8,128,128]{2,1,0:T(8,128)(2,1)} %get-tuple-element.60.query_in.refs_17_, bf16[8,128,128]{2,1,0:T(8,128)(2,1)} %get-tuple-element.63.kv_in.refs_18_, f32[8,1024]{1,0:T(8,128)} %get-tuple-element.64.count_in.refs_19_), custom_call_target="tpu_custom_call" | custom-call | flops 536870912 | bytes 1048576 | tf_op jit(solution)/shard_map/near_forward/pallas_call | solution.py:663
  65.1 2.6 %attn_grad.1.ag_in = f32[8,128,128]{2,1,0:T(8,128)} custom-call(bf16[128,512]{1,0:T(8,128)(2,1)} %refs_6_.1, bf16[128,512]{1,0:T(8,128)(2,1)} %copy-done.7, bf16[128,512]{1,0:T(8,128)(2,1)} %copy-done.8, bf16[128,512]{1,0:T(8,128)(2,1)} %copy-done.9, bf16[128,512]{1,0:T(8,128)(2,1)} %collective-permute-done.12.refs_4_, ...), custom_call_target="tpu_custom_call" | custom-call | flops 134217728 | bytes 1048576 | tf_op jit(solution)/shard_map/attn_grad/pallas_call | solution.py:650
  69.5 7.2 %far_both.1 = (bf16[64,1024]{1,0:T(8,128)(2,1)}, bf16[8,128,128]{2,1,0:T(8,128)(2,1)}, f32[8,128,128]{2,1,0:T(8,128)}, bf16[64,128,128]{2,1,0:T(8,128)(2,1)}) custom-call(s32[2]{0:T(128)} %pad_add_fusion.where_ref, s32[4,256]{1,0:T(4,128)} %get-tuple-element.54.place_ref, bf16[8,128,128]{2,1,0:T(8,128)(2,1)} %get-tuple-element.60.query_in.refs_17_, ...), custom_call_target="tpu_custom_call" | custom-call | flops 536870912 | bytes 1048576 | tf_op jit(solution)/shard_map/far_both/pallas_call | solution.py:682
  76.7 7.6 %all-to-all-start.1 = ((bf16[64,128,128]{2,1,0:T(8,128)(2,1)}), bf16[64,128,128]{2,1,0:T(8,128)(2,1)}, u32[]{:S(2)}, u32[]{:S(2)}) async-start(bf16[64,128,128]{2,1,0:T(8,128)(2,1)} %get-tuple-element.67), calls=%async_computation.1 | async-start | bytes 4194304 | tf_op jit(solution)/shard_map/all_to_all | solution.py:703
  84.3 3.3 %collective-permute-start.16 = (bf16[256,512]{1,0:T(8,128)(2,1)S(1)}, bf16[256,512]{1,0:T(8,128)(2,1)}, u32[]{:S(2)}, u32[]{:S(2)}) collective-permute-start(bf16[256,512]{1,0:T(8,128)(2,1)S(1)} %copy-done.1), channel_id=1, source_target_pairs={{0,7},{1,0},{2,1},{3,2},{4,3},{5,4},{6,5},{7,6},{8,15},{9,8},{10,9... | collective-permute-start | bytes 786440 | tf_op jit(solution)/shard_map/ppermute | solution.py:102
  87.7 6.6 %collective-permute-done.14.refs_0_ = bf16[256,512]{1,0:T(8,128)(2,1)} collective-permute-done((bf16[256,512]{1,0:T(8,128)(2,1)S(1)}, bf16[256,512]{1,0:T(8,128)(2,1)}, u32[]{:S(2)}, u32[]{:S(2)}) %collective-permute-start.14) | collective-permute-done | bytes 262176 | tf_op jit(solution)/shard_map/ppermute | solution.py:102
  94.3 3.2 %collective-permute-start.17 = (bf16[256,512]{1,0:T(8,128)(2,1)}, bf16[256,512]{1,0:T(8,128)(2,1)}, u32[]{:S(2)}, u32[]{:S(2)}) collective-permute-start(bf16[256,512]{1,0:T(8,128)(2,1)} %collective-permute-done.16.refs_3_), channel_id=1, source_target_pairs={{0,7},{1,0},{2,1},{3,2},{4,3},{5,4},{6,5},{7,6},{8,15},{9,8},{10,9... | collective-permute-start | bytes 786440 | tf_op jit(solution)/shard_map/ppermute | solution.py:102
  97.5 7.2 %near_backward.1 = (bf16[64,1024]{1,0:T(8,128)(2,1)}, f32[8,128,128]{2,1,0:T(8,128)}, bf16[128,512]{1,0:T(8,128)(2,1)}, bf16[8,128,512]{2,1,0:T(8,128)(2,1)}) custom-call(s32[1]{0:T(128)} %bitcast.col_ref, bf16[128,512]{1,0:T(8,128)(2,1)} %refs_6_.1, bf16[128,512]{1,0:T(8,128)(2,1)} %copy-done.7, bf16[128,512]{1,0:T(8,128)(2,1)} %copy-done.8, ...), custom_call_target="tpu_custom_call" | custom-call | flops 1342177280 | bytes 1048576 | tf_op jit(solution)/shard_map/near_backward/pallas_call | solution.py:707
  104.9 3.2 %collective-permute-start.19 = (bf16[256,512]{1,0:T(8,128)(2,1)}, bf16[256,512]{1,0:T(8,128)(2,1)}, u32[]{:S(2)}, u32[]{:S(2)}) collective-permute-start(bf16[256,512]{1,0:T(8,128)(2,1)} %collective-permute-done.17.refs_5_), channel_id=1, source_target_pairs={{0,7},{1,0},{2,1},{3,2},{4,3},{5,4},{6,5},{7,6},{8,15},{9,8},{10,9... | collective-permute-start | bytes 786440 | tf_op jit(solution)/shard_map/ppermute | solution.py:102
  108.1 5.6 %collective-permute-done.18.refs_1_ = bf16[256,512]{1,0:T(8,128)(2,1)} collective-permute-done((bf16[256,512]{1,0:T(8,128)(2,1)}, bf16[256,512]{1,0:T(8,128)(2,1)}, u32[]{:S(2)}, u32[]{:S(2)}) %collective-permute-start.18) | collective-permute-done | bytes 262176 | tf_op jit(solution)/shard_map/ppermute | solution.py:102
  114.3 4.1 %gather_grads.1 = (bf16[2,256,128]{2,1,0:T(8,128)(2,1)}, bf16[2,256,128]{2,1,0:T(8,128)(2,1)}, bf16[2,256,128]{2,1,0:T(8,128)(2,1)}, bf16[2,256,128]{2,1,0:T(8,128)(2,1)}, bf16[256,512]{1,0:T(8,128)(2,1)}) custom-call(s32[1]{0:T(128)} %bitcast.col_ref, s32[2,256]{1,0:T(2,128)} %get-tuple-element.53.send_ref.home_ref, ...), custom_call_target="tpu_custom_call" | custom-call | flops 134217728 | bytes 1048576 | tf_op jit(solution)/shard_map/gather_grads/pallas_call | solution.py:728
  118.4 7.4 %all-to-all-start.2 = ((bf16[32,8,512]{2,1,0:T(8,128)(2,1)}), bf16[32,8,512]{2,1,0:T(8,128)(2,1)S(1)}, u32[]{:S(2)}, u32[]{:S(2)}) async-start(bf16[32,8,512]{2,1,0:T(8,128)(2,1)} %bitcast.7), calls=%async_computation.2 | async-start | bytes 524288 | tf_op jit(solution)/shard_map/all_to_all | solution.py:744
  125.8 4.6 %collective-permute-start.21 = (bf16[2,256,128]{2,1,0:T(8,128)(2,1)}, bf16[2,256,128]{2,1,0:T(8,128)(2,1)}, u32[]{:S(2)}, u32[]{:S(2)}) collective-permute-start(bf16[2,256,128]{2,1,0:T(8,128)(2,1)} %get-tuple-element.86), channel_id=1, source_target_pairs={{0,2},{1,3},{2,4},{3,5},{4,6},{5,7},{6,0},{7,1},{8,10},{9,11},{10,... | collective-permute-start | bytes 393224 | tf_op jit(solution)/shard_map/ppermute | solution.py:102
  130.4 3.7 %collective-permute-start.23 = (bf16[2,256,128]{2,1,0:T(8,128)(2,1)}, bf16[2,256,128]{2,1,0:T(8,128)(2,1)}, u32[]{:S(2)}, u32[]{:S(2)}) collective-permute-start(bf16[2,256,128]{2,1,0:T(8,128)(2,1)} %get-tuple-element.88), channel_id=1, source_target_pairs={{0,4},{1,5},{2,6},{3,7},{4,0},{5,1},{6,2},{7,3},{8,12},{9,13},{10,... | collective-permute-start | bytes 393224 | tf_op jit(solution)/shard_map/ppermute | solution.py:102
  134.8 7.4 %all-to-all-start.3 = ((bf16[32,8,512]{2,1,0:T(8,128)(2,1)}), bf16[32,8,512]{2,1,0:T(8,128)(2,1)}, u32[]{:S(2)}, u32[]{:S(2)}) async-start(bf16[32,8,512]{2,1,0:T(8,128)(2,1)} %sum_shares.1.refs_4_), calls=%async_computation.3 | async-start | bytes 524288 | tf_op jit(solution)/shard_map/all_to_all | solution.py:755
  146.0 2.3 %collective-permute-start.24 = (bf16[4,256,128]{2,1,0:T(8,128)(2,1)}, bf16[4,256,128]{2,1,0:T(8,128)(2,1)}, u32[]{:S(2)}, u32[]{:S(2)}) collective-permute-start(bf16[4,256,128]{2,1,0:T(8,128)(2,1)} %pack.1), channel_id=1, source_target_pairs={{0,1},{1,0},{2,3},{3,2},{4,5},{5,4},{6,7},{7,6},{8,9},{9,8},{10,11... | collective-permute-start | bytes 786440 | tf_op jit(solution)/shard_map/ppermute | solution.py:110
  148.3 2.4 %first_heads.1.sum_in = f32[2,128,512]{2,1,0:T(8,128)} custom-call(bf16[2,256,128]{2,1,0:T(8,128)(2,1)} %get-tuple-element.85.refs_0_, bf16[2,256,128]{2,1,0:T(8,128)(2,1)} %collective-permute-done.21.refs_1_, bf16[2,256,128]{2,1,0:T(8,128)(2,1)} %collective-permute-done.22.refs_2_.refs_3_, bf16[256,512]{1,0:T(8,128)(2,1)} %pad_maximum_fusion.refs_3_, ...), custom_call_target="tpu_custom_call" | custom-call | flops 2684354 | bytes 1048576 | tf_op jit(solution)/shard_map/first_heads/pallas_call | solution.py:766
  154.6 3.1 %finish.1 = (bf16[128,512]{1,0:T(8,128)(2,1)}, bf16[128,512]{1,0:T(8,128)(2,1)}) custom-call(s32[1]{0:T(128)} %bitcast.col_ref, f32[2,128,512]{2,1,0:T(8,128)} %first_heads.1.sum_in, bf16[2,256,128]{2,1,0:T(8,128)(2,1)} %collective-permute-done.23.refs_2_.pair_in, bf16[4,256,128]{2,1,0:T(8,128)(2,1)} %collective-permute-done.24.beside_in, ...), custom_call_target="tpu_custom_call" | custom-call | flops 2684354 | bytes 1048576 | tf_op jit(solution)/shard_map/finish/pallas_call | solution.py:779
  (62 shorter events, 21.8 us)
Async XLA Ops:
  0.6 9.7 %collective-permute-start = (bf16[128,512]{1,0:T(8,128)(2,1)}, bf16[128,512]{1,0:T(8,128)(2,1)}, u32[]{:S(2)}, u32[]{:S(2)}) collective-permute-start(bf16[128,512]{1,0:T(8,128)(2,1)} %refs_5_.1), channel_id=1, source_target_pairs={{0,1},{1,2},{2,3},{3,4},{4,5},{5,6},{6,7},{7,0},{8,9},{9,10},{10,1... | collective-permute-start | bytes 393224 | tf_op jit(solution)/shard_map/ppermute | solution.py:102
  2.6 7.8 %collective-permute-start.1 = (bf16[128,512]{1,0:T(8,128)(2,1)}, bf16[128,512]{1,0:T(8,128)(2,1)}, u32[]{:S(2)}, u32[]{:S(2)}) collective-permute-start(bf16[128,512]{1,0:T(8,128)(2,1)} %refs_5_.1), channel_id=1, source_target_pairs={{0,7},{1,0},{2,1},{3,2},{4,3},{5,4},{6,5},{7,6},{8,15},{9,8},{10,9... | collective-permute-start | bytes 393224 | tf_op jit(solution)/shard_map/ppermute | solution.py:102
  10.4 6.4 %collective-permute-start.2 = (bf16[128,512]{1,0:T(8,128)(2,1)}, bf16[128,512]{1,0:T(8,128)(2,1)S(1)}, u32[]{:S(2)}, u32[]{:S(2)}) collective-permute-start(bf16[128,512]{1,0:T(8,128)(2,1)} %collective-permute-done.refs_1_.refs_9_), channel_id=1, source_target_pairs={{0,1},{1,2},{2,3},{3,4},{4,5},{5,6},{6,7},{7,0},{8,9},{9,10},{10,1... | collective-permute-start | bytes 393224 | tf_op jit(solution)/shard_map/ppermute | solution.py:102
  10.4 7.0 %collective-permute-start.5 = (bf16[128,512]{1,0:T(8,128)(2,1)}, bf16[128,512]{1,0:T(8,128)(2,1)S(1)}, u32[]{:S(2)}, u32[]{:S(2)}) collective-permute-start(bf16[128,512]{1,0:T(8,128)(2,1)} %collective-permute-done.1.refs_2_.refs_10_), channel_id=1, source_target_pairs={{0,7},{1,0},{2,1},{3,2},{4,3},{5,4},{6,5},{7,6},{8,15},{9,8},{10,9... | collective-permute-start | bytes 393224 | tf_op jit(solution)/shard_map/ppermute | solution.py:102
  17.4 6.3 %collective-permute-start.3 = (bf16[128,512]{1,0:T(8,128)(2,1)S(1)}, bf16[128,512]{1,0:T(8,128)(2,1)}, u32[]{:S(2)}, u32[]{:S(2)}) collective-permute-start(bf16[128,512]{1,0:T(8,128)(2,1)S(1)} %collective-permute-done.2.refs_3_.refs_11_), channel_id=1, source_target_pairs={{0,1},{1,2},{2,3},{3,4},{4,5},{5,6},{6,7},{7,0},{8,9},{9,10},{10,1... | collective-permute-start | bytes 393224 | tf_op jit(solution)/shard_map/ppermute | solution.py:102
  17.4 6.3 %collective-permute-start.6 = (bf16[128,512]{1,0:T(8,128)(2,1)S(1)}, bf16[128,512]{1,0:T(8,128)(2,1)S(1)}, u32[]{:S(2)}, u32[]{:S(2)}) collective-permute-start(bf16[128,512]{1,0:T(8,128)(2,1)S(1)} %collective-permute-done.5.refs_4_.refs_12_), channel_id=1, source_target_pairs={{0,7},{1,0},{2,1},{3,2},{4,3},{5,4},{6,5},{7,6},{8,15},{9,8},{10,9... | collective-permute-start | bytes 393224 | tf_op jit(solution)/shard_map/ppermute | solution.py:102
  23.7 6.5 %collective-permute-start.4 = (bf16[128,512]{1,0:T(8,128)(2,1)}, bf16[128,512]{1,0:T(8,128)(2,1)}, u32[]{:S(2)}, u32[]{:S(2)}) collective-permute-start(bf16[128,512]{1,0:T(8,128)(2,1)} %collective-permute-done.3.refs_5_.refs_13_), channel_id=1, source_target_pairs={{0,1},{1,2},{2,3},{3,4},{4,5},{5,6},{6,7},{7,0},{8,9},{9,10},{10,1... | collective-permute-start | bytes 393224 | tf_op jit(solution)/shard_map/ppermute | solution.py:102
  33.5 7.9 %copy-start.3 = (bf16[128,512]{1,0:T(8,128)(2,1)S(1)}, bf16[128,512]{1,0:T(8,128)(2,1)}, u32[]{:S(2)}) copy-start(bf16[128,512]{1,0:T(8,128)(2,1)} %refs_6_.1) | copy-start | bytes 393220
  33.6 27.2 %copy-start = (bf16[192,512]{1,0:T(8,128)(2,1)S(1)}, bf16[192,512]{1,0:T(8,128)(2,1)}, u32[]{:S(2)}) copy-start(bf16[192,512]{1,0:T(8,128)(2,1)} %weight_in.2) | copy-start | bytes 589828
  33.6 27.2 %copy-start.2 = (bf16[64,512]{1,0:T(8,128)(2,1)S(1)}, bf16[64,512]{1,0:T(8,128)(2,1)}, u32[]{:S(2)}) copy-start(bf16[64,512]{1,0:T(8,128)(2,1)} %weight_in.3) | copy-start | bytes 196612
  33.6 35.9 %all-to-all-start = ((bf16[64,128,128]{2,1,0:T(8,128)(2,1)}), bf16[64,128,128]{2,1,0:T(8,128)(2,1)}, u32[]{:S(2)}, u32[]{:S(2)}) async-start(bf16[64,128,128]{2,1,0:T(8,128)(2,1)} %get-tuple-element.62), calls=%async_computation | async-start | bytes 4194304 | tf_op jit(solution)/shard_map/all_to_all | solution.py:643
  41.4 6.8 %collective-permute-start.7 = (bf16[128,512]{1,0:T(8,128)(2,1)S(1)}, bf16[128,512]{1,0:T(8,128)(2,1)S(1)}, u32[]{:S(2)}, u32[]{:S(2)}) collective-permute-start(bf16[128,512]{1,0:T(8,128)(2,1)S(1)} %copy-done.3), channel_id=1, source_target_pairs={{0,1},{1,2},{2,3},{3,4},{4,5},{5,6},{6,7},{7,0},{8,9},{9,10},{10,1... | collective-permute-start | bytes 393224 | tf_op jit(solution)/shard_map/ppermute | solution.py:102
  41.9 6.3 %collective-permute-start.11 = (bf16[128,512]{1,0:T(8,128)(2,1)S(1)}, bf16[128,512]{1,0:T(8,128)(2,1)S(1)}, u32[]{:S(2)}, u32[]{:S(2)}) collective-permute-start(bf16[128,512]{1,0:T(8,128)(2,1)S(1)} %copy-done.3), channel_id=1, source_target_pairs={{0,7},{1,0},{2,1},{3,2},{4,3},{5,4},{6,5},{7,6},{8,15},{9,8},{10,9... | collective-permute-start | bytes 393224 | tf_op jit(solution)/shard_map/ppermute | solution.py:102
  48.2 6.2 %collective-permute-start.8 = (bf16[128,512]{1,0:T(8,128)(2,1)S(1)}, bf16[128,512]{1,0:T(8,128)(2,1)S(1)}, u32[]{:S(2)}, u32[]{:S(2)}) collective-permute-start(bf16[128,512]{1,0:T(8,128)(2,1)S(1)} %collective-permute-done.7.refs_1_), channel_id=1, source_target_pairs={{0,1},{1,2},{2,3},{3,4},{4,5},{5,6},{6,7},{7,0},{8,9},{9,10},{10,1... | collective-permute-start | bytes 393224 | tf_op jit(solution)/shard_map/ppermute | solution.py:102
  48.9 5.5 %collective-permute-start.12 = (bf16[128,512]{1,0:T(8,128)(2,1)S(1)}, bf16[128,512]{1,0:T(8,128)(2,1)}, u32[]{:S(2)}, u32[]{:S(2)}) collective-permute-start(bf16[128,512]{1,0:T(8,128)(2,1)S(1)} %collective-permute-done.11.refs_2_), channel_id=1, source_target_pairs={{0,7},{1,0},{2,1},{3,2},{4,3},{5,4},{6,5},{7,6},{8,15},{9,8},{10,9... | collective-permute-start | bytes 393224 | tf_op jit(solution)/shard_map/ppermute | solution.py:102
  54.4 6.3 %collective-permute-start.9 = (bf16[128,512]{1,0:T(8,128)(2,1)S(1)}, bf16[128,512]{1,0:T(8,128)(2,1)}, u32[]{:S(2)}, u32[]{:S(2)}) collective-permute-start(bf16[128,512]{1,0:T(8,128)(2,1)S(1)} %collective-permute-done.8.refs_3_), channel_id=1, source_target_pairs={{0,1},{1,2},{2,3},{3,4},{4,5},{5,6},{6,7},{7,0},{8,9},{9,10},{10,1... | collective-permute-start | bytes 393224 | tf_op jit(solution)/shard_map/ppermute | solution.py:102
  55.1 10.1 %collective-permute-start.13 = (bf16[128,512]{1,0:T(8,128)(2,1)}, bf16[128,512]{1,0:T(8,128)(2,1)}, u32[]{:S(2)}, u32[]{:S(2)}) collective-permute-start(bf16[128,512]{1,0:T(8,128)(2,1)} %collective-permute-done.12.refs_4_), channel_id=1, source_target_pairs={{0,7},{1,0},{2,1},{3,2},{4,3},{5,4},{6,5},{7,6},{8,15},{9,8},{10,9... | collective-permute-start | bytes 393224 | tf_op jit(solution)/shard_map/ppermute | solution.py:102
  60.7 7.0 %collective-permute-start.10 = (bf16[128,512]{1,0:T(8,128)(2,1)}, bf16[128,512]{1,0:T(8,128)(2,1)}, u32[]{:S(2)}, u32[]{:S(2)}) collective-permute-start(bf16[128,512]{1,0:T(8,128)(2,1)} %collective-permute-done.9.refs_5_), channel_id=1, source_target_pairs={{0,1},{1,2},{2,3},{3,4},{4,5},{5,6},{6,7},{7,0},{8,9},{9,10},{10,1... | collective-permute-start | bytes 393224 | tf_op jit(solution)/shard_map/ppermute | solution.py:102
  76.7 37.0 %all-to-all-start.1 = ((bf16[64,128,128]{2,1,0:T(8,128)(2,1)}), bf16[64,128,128]{2,1,0:T(8,128)(2,1)}, u32[]{:S(2)}, u32[]{:S(2)}) async-start(bf16[64,128,128]{2,1,0:T(8,128)(2,1)} %get-tuple-element.67), calls=%async_computation.1 | async-start | bytes 4194304 | tf_op jit(solution)/shard_map/all_to_all | solution.py:703
  84.2 10.1 %collective-permute-start.14 = (bf16[256,512]{1,0:T(8,128)(2,1)S(1)}, bf16[256,512]{1,0:T(8,128)(2,1)}, u32[]{:S(2)}, u32[]{:S(2)}) collective-permute-start(bf16[256,512]{1,0:T(8,128)(2,1)S(1)} %copy-done.1), channel_id=1, source_target_pairs={{0,1},{1,2},{2,3},{3,4},{4,5},{5,6},{6,7},{7,0},{8,9},{9,10},{10,1... | collective-permute-start | bytes 786440 | tf_op jit(solution)/shard_map/ppermute | solution.py:102
  84.3 10.0 %collective-permute-start.16 = (bf16[256,512]{1,0:T(8,128)(2,1)S(1)}, bf16[256,512]{1,0:T(8,128)(2,1)}, u32[]{:S(2)}, u32[]{:S(2)}) collective-permute-start(bf16[256,512]{1,0:T(8,128)(2,1)S(1)} %copy-done.1), channel_id=1, source_target_pairs={{0,7},{1,0},{2,1},{3,2},{4,3},{5,4},{6,5},{7,6},{8,15},{9,8},{10,9... | collective-permute-start | bytes 786440 | tf_op jit(solution)/shard_map/ppermute | solution.py:102
  94.3 10.5 %collective-permute-start.15 = (bf16[256,512]{1,0:T(8,128)(2,1)}, bf16[256,512]{1,0:T(8,128)(2,1)}, u32[]{:S(2)}, u32[]{:S(2)}) collective-permute-start(bf16[256,512]{1,0:T(8,128)(2,1)} %collective-permute-done.14.refs_0_), channel_id=1, source_target_pairs={{0,1},{1,2},{2,3},{3,4},{4,5},{5,6},{6,7},{7,0},{8,9},{9,10},{10,1... | collective-permute-start | bytes 786440 | tf_op jit(solution)/shard_map/ppermute | solution.py:102
  94.3 10.5 %collective-permute-start.17 = (bf16[256,512]{1,0:T(8,128)(2,1)}, bf16[256,512]{1,0:T(8,128)(2,1)}, u32[]{:S(2)}, u32[]{:S(2)}) collective-permute-start(bf16[256,512]{1,0:T(8,128)(2,1)} %collective-permute-done.16.refs_3_), channel_id=1, source_target_pairs={{0,7},{1,0},{2,1},{3,2},{4,3},{5,4},{6,5},{7,6},{8,15},{9,8},{10,9... | collective-permute-start | bytes 786440 | tf_op jit(solution)/shard_map/ppermute | solution.py:102
  104.8 8.9 %collective-permute-start.18 = (bf16[256,512]{1,0:T(8,128)(2,1)}, bf16[256,512]{1,0:T(8,128)(2,1)}, u32[]{:S(2)}, u32[]{:S(2)}) collective-permute-start(bf16[256,512]{1,0:T(8,128)(2,1)} %collective-permute-done.15.refs_4_), channel_id=1, source_target_pairs={{0,1},{1,2},{2,3},{3,4},{4,5},{5,6},{6,7},{7,0},{8,9},{9,10},{10,1... | collective-permute-start | bytes 786440 | tf_op jit(solution)/shard_map/ppermute | solution.py:102
  104.9 8.8 %collective-permute-start.19 = (bf16[256,512]{1,0:T(8,128)(2,1)}, bf16[256,512]{1,0:T(8,128)(2,1)}, u32[]{:S(2)}, u32[]{:S(2)}) collective-permute-start(bf16[256,512]{1,0:T(8,128)(2,1)} %collective-permute-done.17.refs_5_), channel_id=1, source_target_pairs={{0,7},{1,0},{2,1},{3,2},{4,3},{5,4},{6,5},{7,6},{8,15},{9,8},{10,9... | collective-permute-start | bytes 786440 | tf_op jit(solution)/shard_map/ppermute | solution.py:102
  113.7 12.1 %collective-permute-start.20 = (bf16[256,512]{1,0:T(8,128)(2,1)}, bf16[256,512]{1,0:T(8,128)(2,1)}, u32[]{:S(2)}, u32[]{:S(2)}) collective-permute-start(bf16[256,512]{1,0:T(8,128)(2,1)} %collective-permute-done.18.refs_1_), channel_id=1, source_target_pairs={{0,1},{1,2},{2,3},{3,4},{4,5},{5,6},{6,7},{7,0},{8,9},{9,10},{10,1... | collective-permute-start | bytes 786440 | tf_op jit(solution)/shard_map/ppermute | solution.py:102
  118.4 15.7 %all-to-all-start.2 = ((bf16[32,8,512]{2,1,0:T(8,128)(2,1)}), bf16[32,8,512]{2,1,0:T(8,128)(2,1)S(1)}, u32[]{:S(2)}, u32[]{:S(2)}) async-start(bf16[32,8,512]{2,1,0:T(8,128)(2,1)} %bitcast.7), calls=%async_computation.2 | async-start | bytes 524288 | tf_op jit(solution)/shard_map/all_to_all | solution.py:744
  125.8 16.4 %collective-permute-start.21 = (bf16[2,256,128]{2,1,0:T(8,128)(2,1)}, bf16[2,256,128]{2,1,0:T(8,128)(2,1)}, u32[]{:S(2)}, u32[]{:S(2)}) collective-permute-start(bf16[2,256,128]{2,1,0:T(8,128)(2,1)} %get-tuple-element.86), channel_id=1, source_target_pairs={{0,2},{1,3},{2,4},{3,5},{4,6},{5,7},{6,0},{7,1},{8,10},{9,11},{10,... | collective-permute-start | bytes 393224 | tf_op jit(solution)/shard_map/ppermute | solution.py:102
  130.4 12.6 %collective-permute-start.22 = (bf16[2,256,128]{2,1,0:T(8,128)(2,1)}, bf16[2,256,128]{2,1,0:T(8,128)(2,1)}, u32[]{:S(2)}, u32[]{:S(2)}) collective-permute-start(bf16[2,256,128]{2,1,0:T(8,128)(2,1)} %get-tuple-element.87), channel_id=1, source_target_pairs={{0,6},{1,7},{2,0},{3,1},{4,2},{5,3},{6,4},{7,5},{8,14},{9,15},{10,... | collective-permute-start | bytes 393224 | tf_op jit(solution)/shard_map/ppermute | solution.py:102
  130.4 14.0 %collective-permute-start.23 = (bf16[2,256,128]{2,1,0:T(8,128)(2,1)}, bf16[2,256,128]{2,1,0:T(8,128)(2,1)}, u32[]{:S(2)}, u32[]{:S(2)}) collective-permute-start(bf16[2,256,128]{2,1,0:T(8,128)(2,1)} %get-tuple-element.88), channel_id=1, source_target_pairs={{0,4},{1,5},{2,6},{3,7},{4,0},{5,1},{6,2},{7,3},{8,12},{9,13},{10,... | collective-permute-start | bytes 393224 | tf_op jit(solution)/shard_map/ppermute | solution.py:102
  134.8 16.0 %all-to-all-start.3 = ((bf16[32,8,512]{2,1,0:T(8,128)(2,1)}), bf16[32,8,512]{2,1,0:T(8,128)(2,1)}, u32[]{:S(2)}, u32[]{:S(2)}) async-start(bf16[32,8,512]{2,1,0:T(8,128)(2,1)} %sum_shares.1.refs_4_), calls=%async_computation.3 | async-start | bytes 524288 | tf_op jit(solution)/shard_map/all_to_all | solution.py:755
  146.0 8.7 %collective-permute-start.24 = (bf16[4,256,128]{2,1,0:T(8,128)(2,1)}, bf16[4,256,128]{2,1,0:T(8,128)(2,1)}, u32[]{:S(2)}, u32[]{:S(2)}) collective-permute-start(bf16[4,256,128]{2,1,0:T(8,128)(2,1)} %pack.1), channel_id=1, source_target_pairs={{0,1},{1,0},{2,3},{3,2},{4,5},{5,4},{6,7},{7,6},{8,9},{9,8},{10,11... | collective-permute-start | bytes 786440 | tf_op jit(solution)/shard_map/ppermute | solution.py:110
  (7 other events, 22.0 us)
